TPU v7x, 32 devices: a whole 2x2x4 slice. The times are simulated.
32 devices in a mesh: band: 4 (over y, x), set: 8 (over z, core).
Axes of the slice: x: 2, y: 2, z: 4, core: 2. Of those that a mesh axis runs over, the one named last changes fastest.
Arguments:
- grid: float32 [8, 5152, 128], P('band', 'set'), may hold values from -6 to 6
- row_points: int32 [8], P('band'), may hold values from 20 to 5136, as said below
- legendre: bfloat16 [640, 8, 1408], P('set'), may hold values from -1.5 to 1.5
Outputs:
- spectra: float32 [640, 1408, 128], P('set', 'band')
Inputs may be any that keep to these rules, and one draw needn't show every extreme that they name: row_points[r] is 4 j + 20 for some row j of the model grid with r * (160) <= j < (r + 1) * 160; the last row has 5136 points.
All inputs are finite; a program needn't handle non-finite values.
Results may differ from a plain program's by a relative error of at most 0.0029.
Values may be sent and summed in bfloat16 or wider, within the bound.
No kernel may reach another device: no remote copies, remote signals or barrier semaphores. Data moves between devices by JAX's collectives and lax.ppermute only.
A program may use at most 64 MiB of HBM per device.

v0:
```python
import math

import jax
import jax.numpy as jnp
from jax import lax
from jax.sharding import PartitionSpec as P

TRUNC = 1279


def selection(pair_ids, slot_ids):
    is_first = slot_ids[None, :] <= TRUNC - pair_ids[:, None]
    parity = jnp.where(
        is_first, slot_ids[None, :] % 2, (slot_ids[None, :] - 1 - TRUNC + pair_ids[:, None]) % 2
    )
    selector = jnp.where(is_first, 0, 2) + parity
    class_ids = jnp.arange(4, dtype=jnp.int32)
    return (selector[:, :, None] == class_ids[None, None, :]).astype(jnp.float32)


def wave_numbers(position, pair_count):
    within = position % (2 * pair_count)
    owned_pair = position // (2 * pair_count) * pair_count + within % pair_count
    return jnp.where(within < pair_count, owned_pair, TRUNC - owned_pair)


def shards(grid, row_points, legendre):
    set_index = lax.axis_index("set")
    band_index = lax.axis_index("band")
    band_size = lax.axis_size("band")
    row_count, point_count, flat_width = grid.shape
    columns = flat_width // 2
    pair_count = legendre.shape[0]
    slot_count = legendre.shape[2] // band_size
    length_float = row_points.astype(jnp.float32)
    row_scale = lax.rsqrt(length_float)
    point_ids = set_index * point_count + jnp.arange(point_count, dtype=jnp.int32)
    in_row = point_ids[None, :] < row_points[:, None]
    grid_split = grid.reshape(row_count, point_count, 2, columns)
    position = jnp.arange(2 * pair_count * lax.axis_size("set"), dtype=jnp.int32)
    wave_ids = wave_numbers(position, pair_count)
    residue = point_ids[None, :, None] * wave_ids[None, None, :] % row_points[:, None, None]
    phases = residue.astype(jnp.float32) * (2.0 * math.pi / length_float)[:, None, None]
    usable = in_row[:, :, None] & (wave_ids[None, None, :] <= (row_points[:, None, None] - 1) // 2)
    cosine_part = jnp.where(usable, jnp.cos(phases) * row_scale[:, None, None], 0.0)
    sine_part = jnp.where(usable, -jnp.sin(phases) * row_scale[:, None, None], 0.0)
    table = jnp.stack([cosine_part, sine_part], axis=2)
    fourier = jnp.einsum("rqhc,rqem->mhrec", grid_split, table, precision=lax.Precision.HIGHEST)
    halves = jnp.stack([fourier[:, 0] + fourier[:, 1], fourier[:, 0] - fourier[:, 1]], axis=1)
    sums = lax.psum_scatter(
        halves.reshape(2 * pair_count * lax.axis_size("set"), 2, row_count, 2 * columns),
        "set",
        scatter_dimension=0,
        tiled=True,
    )
    rounded = sums.astype(jnp.bfloat16)
    sources = rounded.reshape(2, pair_count, 2, row_count, 2 * columns).transpose(1, 0, 2, 3, 4)
    sources = sources.reshape(pair_count, 4, row_count, 2 * columns)
    pair_ids = set_index * pair_count + jnp.arange(pair_count, dtype=jnp.int32)
    slot_ids = band_index * slot_count + jnp.arange(slot_count, dtype=jnp.int32)
    weights = selection(pair_ids, slot_ids)
    legend_mine = lax.dynamic_slice_in_dim(legendre, band_index * slot_count, slot_count, 2)
    products = jnp.einsum(
        "prk,pjrc->pkjc",
        legend_mine,
        lax.all_gather(sources, "band", axis=2, tiled=True),
        preferred_element_type=jnp.float32,
    )
    return jnp.sum(products * weights[:, :, :, None], axis=2)


def solution(mesh):
    return jax.shard_map(
        shards,
        mesh=mesh,
        in_specs=(P("band", "set", None), P("band"), P("set", None, None)),
        out_specs=P("set", "band", None),
        check_vma=False,
    )
```

profile of v0, /device:TPU:0, one launch (start us, length us, event | category | flops | bytes accessed | tf_op | source)
XLA Modules:
  0.0 219.4 jit_solution(4880194958099761582)
XLA Ops:
  6.5 0.0 copy-start
  6.5 0.0 reduce-scatter.2.cloned.1.call-start
  6.6 0.8 and_select_fusion.2
  7.4 0.7 convert_divide_fusion
  8.0 0.7 broadcast_compare_fusion.2
  8.7 0.7 broadcast_compare_fusion.1
  9.4 2.0 broadcast_multiply_fusion
  11.4 0.1 broadcast_compare_fusion
  11.5 1.4 copy.14
  12.9 90.0 %and_select_fusion.1 = (f32[2,644,1,1280]{3,1,2,0:T(8,128)S(1)}, f32[2,644,1,1280]{3,1,2,0:T(8,128)S(1)}) fusion(f32[2]{0:T(128)S(1)} %get-tuple-element.12, f32[2]{0:T(128)S(1)} %get-tuple-element.11, s32[2]{0:T(128)S(1)} %get-tuple-element.10, s32[644,1280]{1,0:T(8,128)} %broadcast_multiply_fusion, pred[2]{0:T(512)(128)(4,1)S(1)} %broadcast_compare_fusion.2, ...), kind=kLoop, calls=%fused_computation.10 | loop fusion | flops 24729600 | bytes 16490274 | tf_op jit(solution)/shard_map/jit(_where)/select_n | solution.py:45
  102.9 9.4 %fusion.12 = f32[1280,2,2,2,64]{0,4,1,3,2:T(8,128)S(1)} fusion(f32[2,644,2,64,1]{1,3,2,4,0:T(8,128)S(1)} %bitcast.30, f32[2,644,1,1280]{3,1,2,0:T(8,128)S(1)} %get-tuple-element.6, f32[2,644,1,1280]{3,1,2,0:T(8,128)S(1)} %get-tuple-element.5), kind=kOutput, calls=%fused_computation.20 | convolution fusion | flops 5067919360 | bytes 16470016 | tf_op jit(solution)/shard_map/rqhc,rqem->mhrec/dot_general | solution.py:48
  112.4 1.3 slice_add_fusion
  113.7 2.8 %copy.15 = f32[1280,1,2,128]{3,0,2,1:T(8,128)} copy(f32[1280,1,2,128]{0,3,2,1:T(8,128)} %bitcast.29) | data formatting | bytes 2621440 | tf_op jit(solution)/shard_map/stack | solution.py:49
  116.4 1.5 copy.16
  117.9 3.4 %pad_maximum_fusion = f32[1280,2,2,128]{3,0,2,1:T(8,128)} fusion(f32[1280,1,2,128]{3,0,2,1:T(8,128)} %copy.16, f32[1280,1,2,128]{3,0,2,1:T(8,128)} %copy.15), kind=kLoop, calls=%fused_computation.21 | loop fusion | flops 655360 | bytes 5242880 | tf_op jit(solution)/shard_map/stack | solution.py:49
  121.3 0.0 reduce-scatter.2.cloned.1.call-update
  121.3 0.1 fusion.17
  121.5 0.1 fusion.16
  121.6 39.9 %reduce-scatter.2.cloned.1.call-done = f32[160,2,2,128]{3,0,2,1:T(8,128)} async-done(((f32[1280,2,2,128]{3,0,2,1:T(8,128)}), f32[160,2,2,128]{3,0,2,1:T(8,128)}) %reduce-scatter.2.cloned.1.call-update) | async-done | bytes 327696 | tf_op jit(solution)/shard_map/reduce_scatter | solution.py:50
  161.5 1.0 convert_element_type.29
  162.5 11.6 %all_gather.3 = bf16[80,4,8,128]{3,0,1,2:T(8,128)(2,1)S(1)} all-gather(bf16[80,4,2,128]{3,0,1,2:T(8,128)(2,1)S(1)} %copy.18), channel_id=1, replica_groups=mesh['band'=4,'set'=8] {'band'}, dimensions={2}, use_global_device_ids=true | all-gather | bytes 819200 | tf_op jit(solution)/shard_map/all_gather | solution.py:66
  174.1 0.0 copy-done
  174.1 38.4 %multiply_reduce_fusion = f32[80,352,128]{2,1,0:T(8,128)} fusion(f32[80,352,4]{1,2,0:T(4,128)S(1)} %fusion.16, bf16[80,4,8,128]{3,0,1,2:T(8,128)(2,1)S(1)} %all_gather.3, bf16[80,8,1408]{2,1,0:T(8,128)(2,1)S(1)} %copy-done, s32[]{:T(128)S(6)} %select_n.130), kind=kOutput, calls=%fused_computation | convolution fusion | flops 255918080 | bytes 16056324 | tf_op jit(solution)/shard_map/prk,pjrc->pkjc/dot_general | solution.py:63
  (7 shorter events, 0.1 us)
Async XLA Ops:
  6.5 167.6 %copy-start = (bf16[80,8,1408]{2,1,0:T(8,128)(2,1)S(1)}, bf16[80,8,1408]{2,1,0:T(8,128)(2,1)}, u32[]{:S(2)}) copy-start(bf16[80,8,1408]{2,1,0:T(8,128)(2,1)} %param.5) | copy-start | bytes 5406724
  6.5 154.9 %reduce-scatter.2.cloned.1.call-start = ((), (), s32[]{:S(2)}) async-start(), calls=%async_computation.1 | async-start | bytes 2949120 | tf_op jit(solution)/shard_map/reduce_scatter | solution.py:50
Sparse Core Ops, SparseCore 0:
  121.4 39.9 reduce-scatter.1
where the time goes:
time: 220 us; the launch traced here: 219 us
  other arithmetic  101 us (46%)
  matrix products  47.9 us (22%)
  waiting for transfers between devices  39.9 us (18%)
  between operations  13.5 us (6%)
  blocking collectives  11.6 us (5%)
  local copies, waits for them, and re-layouts  5.64 us (3%)
    select_n x1, other arithmetic, shards(): jnp.where(usable, jnp.cos(phases) * row_scale[:, None, None], 0.0)  90 us
    reduce_scatter x1, waiting for transfers between devices, shards(): lax.psum_scatter(halves.reshape(2 * pair_count * lax.axis_size('set'), 2,...  39.9 us
    dot_general x1, matrix products, shards(): jnp.einsum('prk,pjrc->pkjc', legend_mine, lax.all_gather(sources, 'band',...  38.4 us
    all_gather x1, blocking collectives, shards(): lax.all_gather(sources, 'band', axis=2, tiled=True)  11.6 us
    dot_general x1, matrix products, shards(): jnp.einsum('rqhc,rqem->mhrec', grid_split, table, precision=lax.Precision...  9.44 us
  transfers between devices with their start and end apart: 1, of which 1 were waited for; matrix products, arithmetic and copies ran while one was open for 0% of the time, Pallas kernels for 0%

commit v1 on v0

v1 whole, which is shorter than its diff:
```python
import functools
import math

import jax
import jax.numpy as jnp
from jax import lax
from jax.experimental import pallas as pl
from jax.experimental.pallas import tpu as pltpu
from jax.sharding import PartitionSpec as P

TRUNC = 1279
GROUP = 8
F32 = jnp.float32
BF16 = jnp.bfloat16
WIRE = jnp.float16


def round_up(value, step):
    return -(-value // step) * step


def unit_circle(multiplier, point, length, inverse):
    product = (multiplier * point).astype(F32)
    residue = product - jnp.floor(product * inverse + 0.5) * length
    quarters = 4.0 * residue * inverse
    turn = jnp.floor(quarters + 0.5)
    angle = (quarters - turn) * (0.5 * math.pi)
    square = angle * angle
    sine = angle * (1.0 + square * (-1 / 6 + square * (1 / 120 + square * (-1 / 5040 + square / 362880))))
    cosine = 1.0 + square * (-0.5 + square * (1 / 24 + square * (-1 / 720 + square / 40320)))
    quadrant = turn.astype(jnp.int32) & 3
    odd = (quadrant & 1) == 1
    real = jnp.where(odd, sine, cosine)
    imag = jnp.where(odd, cosine, sine)
    real = jnp.where((quadrant == 1) | (quadrant == 2), -real, real)
    imag = jnp.where(quadrant >= 2, imag, -imag)
    return real, imag


def rotate(a, b):
    return a[0] * b[0] - a[1] * b[1], a[0] * b[1] + a[1] * b[0]


def split(values):
    high = values.astype(BF16)
    return high, (values - high.astype(F32)).astype(BF16)


def fourier_kernel(groups, first_group, peers, seg, points, info, mine, theirs, *refs):
    outs = refs[:peers]
    values, factor, table, sums = refs[peers:]
    rows = mine.shape[0]
    width = mine.shape[2]
    depth = values.shape[0]
    lane = lax.broadcasted_iota(jnp.int32, (1, width), 1)
    north = lane < width // 2
    slot = lax.broadcasted_iota(jnp.int32, (1, depth), 1)
    point = jnp.where(slot < seg, info[0] + slot, info[1] + slot - seg)
    sub = lax.broadcasted_iota(jnp.int32, (GROUP, 1), 0)
    tiles = peers * groups * 2
    for r in range(rows):
        length_int = info[2 + r]
        length = length_int.astype(F32)
        inverse = 1.0 / length
        scale = lax.rsqrt(jnp.full((1, width), length, F32))
        values[...] = jnp.zeros(values.shape, BF16)
        for half, block in enumerate((mine, theirs)):
            raw = block[r]
            where = info[half] + lax.broadcasted_iota(jnp.int32, (points, 1), 0)
            folded = pltpu.roll(raw, width // 2, 1) + jnp.where(north, raw, -raw)
            folded = jnp.where(where < length_int, folded * scale, 0.0)
            high, low = split(folded)
            values[half * seg:half * seg + points, :width] = high
            values[half * seg:half * seg + points, width:] = low
        near = unit_circle(sub, point, length, inverse)
        last = unit_circle(TRUNC, point, length, inverse)
        for peer in range(peers):
            for g in range(groups):
                base = info[2 + rows + peer] + (first_group + g) * GROUP
                index = peer * groups + g
                real, imag = unit_circle(base, point, length, inverse)
                factor[0, index:index + 1, :] = real
                factor[1, index:index + 1, :] = imag

        def fill(index, carry):
            base = factor[0, pl.ds(index, 1), :], factor[1, pl.ds(index, 1), :]
            first = rotate(base, near)
            second = rotate(last, (first[0], -first[1]))
            block = jnp.concatenate([*first, *second], axis=0)
            high, low = split(block)
            start = pl.multiple_of(index * 4 * GROUP, 4 * GROUP)
            table[0, pl.ds(start, 4 * GROUP), :] = high
            table[1, pl.ds(start, 4 * GROUP), :] = low
            return carry

        lax.fori_loop(0, peers * groups, fill, 0)
        wide = jnp.dot(table[0], values[...], preferred_element_type=F32)
        narrow = jnp.dot(table[1], values[:, :width], preferred_element_type=F32)
        sums[r] = wide[:, :width] + wide[:, width:] + narrow
    for peer in range(peers):
        for g in range(groups):
            base = info[2 + rows + peer] + (first_group + g) * GROUP
            for side in range(2):
                wave = base + sub
                wave = TRUNC - wave if side else wave
                at = ((peer * groups + g) * 2 + side) * 2 * GROUP
                for r in range(rows):
                    real = sums[r, at:at + GROUP, :]
                    imag = sums[r, at + GROUP:at + 2 * GROUP, :]
                    usable = wave <= (info[2 + r] - 1) // 2
                    even = jnp.where(north, real, pltpu.roll(imag, width // 2, 1))
                    odd = jnp.where(north, pltpu.roll(real, width // 2, 1), imag)
                    for parity, block in enumerate((even, odd)):
                        to = (((g * 2 + side) * 2 + parity) * rows + r) * GROUP
                        outs[peer][to:to + GROUP, :] = jnp.where(usable, block, 0.0)


def fourier_sums(info, mine, theirs, groups, first_group, peers):
    rows, points, width = mine.shape
    seg = round_up(points, 16)
    depth = round_up(2 * seg, 128)
    out_rows = groups * 4 * rows * GROUP
    tall = peers * groups * 4 * GROUP
    vmem = pl.BlockSpec(memory_space=pltpu.VMEM)
    return pl.pallas_call(
        functools.partial(fourier_kernel, groups, first_group, peers, seg, points),
        out_shape=[jax.ShapeDtypeStruct((out_rows, width), F32)] * peers,
        in_specs=[pl.BlockSpec(memory_space=pltpu.SMEM), vmem, vmem],
        out_specs=[vmem] * peers,
        scratch_shapes=[
            pltpu.VMEM((depth, 2 * width), BF16),
            pltpu.VMEM((2, round_up(peers * groups, 8), depth), F32),
            pltpu.VMEM((2, tall, depth), BF16),
            pltpu.VMEM((rows, tall, width), F32),
        ],
        compiler_params=pltpu.CompilerParams(vmem_limit_bytes=48 * 2**20),
        name="fourier_sums",
    )(info, mine, theirs)


def weights_kernel(pair_count, rows, bands, info, legend, out):
    group = pl.program_id(0)
    total = rows * bands
    slots = legend.shape[2]
    wide = out.shape[2]
    held = legend[...].astype(F32)
    pair = group * GROUP + lax.broadcasted_iota(jnp.int32, (GROUP, 1, 1), 0)
    held = jnp.where(pair < pair_count, held, 0.0).reshape(GROUP * total, slots).astype(BF16)
    source = lax.broadcasted_iota(jnp.int32, (GROUP * total, 1), 0)
    lane = lax.broadcasted_iota(jnp.int32, (1, wide), 1)
    member = lane % GROUP
    row = lane // GROUP % rows
    parity = lane // (GROUP * rows) % 2
    side = lane // (GROUP * rows * 2) % 2
    band = (lane // (GROUP * rows * 4)) ^ info[0]
    spread = (source == member * total + band * rows + row).astype(F32).astype(BF16)
    moved = lax.dot_general(held, spread, (((0,), (0,)), ((), ())), preferred_element_type=F32)
    slot = info[1] + lax.broadcasted_iota(jnp.int32, (slots, 1), 0)
    first = TRUNC - (info[2] + group * GROUP + member)
    is_first = slot <= first
    count = jnp.where(is_first, slot, slot - 1 - first)
    match = ((count & 1) == parity) & (is_first == (side == 0))
    out[0] = jnp.where(match, moved, 0.0).astype(BF16)


def spread_weights(info, legend, rows, bands):
    pair_count, total, slots = legend.shape
    groups = pl.cdiv(pair_count, GROUP)
    wide = bands * 4 * rows * GROUP
    return pl.pallas_call(
        functools.partial(weights_kernel, pair_count, rows, bands),
        grid=(groups,),
        out_shape=jax.ShapeDtypeStruct((groups, slots, wide), BF16),
        in_specs=[
            pl.BlockSpec(memory_space=pltpu.SMEM),
            pl.BlockSpec((GROUP, total, slots), lambda g: (g, 0, 0)),
        ],
        out_specs=pl.BlockSpec((1, slots, wide), lambda g: (g, 0, 0)),
        compiler_params=pltpu.CompilerParams(vmem_limit_bytes=48 * 2**20),
        name="spread_weights",
    )(info, legend)


def spectra_kernel(bands, weights, *refs):
    held = refs[:bands]
    out = refs[-1]
    width = held[0].shape[1]
    stacked = jnp.concatenate([ref[...] for ref in held], axis=0)
    member = lax.broadcasted_iota(jnp.int32, stacked.shape, 0) % GROUP
    for at in range(0, GROUP, 2):
        pairs = [stacked * (member == at + i).astype(F32).astype(BF16) for i in range(2)]
        product = jnp.dot(weights[0], jnp.concatenate(pairs, axis=1), preferred_element_type=F32)
        out[at] = product[:, :width]
        out[at + 1] = product[:, width:]


def spectra_part(weights, held, out, pair_count, first_group):
    bands = len(held)
    width = held[0].shape[1]
    slots, wide = weights.shape[1:]
    block = wide // bands
    groups = held[0].shape[0] // block
    previous = [] if out is None else [out]
    return pl.pallas_call(
        functools.partial(spectra_kernel, bands),
        grid=(groups,),
        out_shape=jax.ShapeDtypeStruct((pair_count, slots, width), F32),
        in_specs=[pl.BlockSpec((1, slots, wide), lambda g: (first_group + g, 0, 0))]
        + [pl.BlockSpec((block, width), lambda g: (g, 0))] * bands
        + [pl.BlockSpec(memory_space=pl.ANY)] * len(previous),
        out_specs=pl.BlockSpec((GROUP, slots, width), lambda g: (first_group + g, 0, 0)),
        input_output_aliases={1 + bands: 0} if previous else {},
        compiler_params=pltpu.CompilerParams(vmem_limit_bytes=48 * 2**20),
        name="spectra_part",
    )(weights, *held, *previous)


def swap(axis, size, step):
    return [(i, i ^ step) for i in range(size)]


def shards(grid, row_points, legendre):
    set_index = lax.axis_index("set")
    set_size = lax.axis_size("set")
    band_index = lax.axis_index("band")
    band_size = lax.axis_size("band")
    rows, points, width = grid.shape
    pair_count = legendre.shape[0]
    slots = legendre.shape[2] // band_size
    peers = set_size // 2
    theirs = lax.ppermute(grid, "set", swap("set", set_size, 1))
    steps = jnp.arange(peers, dtype=jnp.int32) * 2
    places = jnp.stack([set_index * points, (set_index ^ 1) * points])
    info = jnp.concatenate([places, row_points, (set_index ^ steps) * pair_count]).astype(jnp.int32)
    legend = lax.dynamic_slice_in_dim(legendre, band_index * slots, slots, 2)
    place = jnp.stack([band_index, band_index * slots, set_index * pair_count]).astype(jnp.int32)
    weights = spread_weights(place, legend, rows, band_size)
    all_groups = pl.cdiv(pair_count, GROUP)
    cut = (all_groups + 1) // 2
    out = None
    for first_group, groups in ((0, cut), (cut, all_groups - cut)):
        parts = fourier_sums(info, grid, theirs, groups, first_group, peers)
        total = parts[0]
        for k in range(1, peers):
            arrived = lax.ppermute(parts[k].astype(WIRE), "set", swap("set", set_size, 2 * k))
            total = total + arrived.astype(F32)
        rounded = total.astype(BF16)
        held = [rounded]
        for k in range(1, band_size):
            held.append(lax.ppermute(rounded, "band", swap("band", band_size, k)))
        out = spectra_part(weights, held, out, pair_count, first_group)
    return out


def solution(mesh):
    return jax.shard_map(
        shards,
        mesh=mesh,
        in_specs=(P("band", "set", None), P("band"), P("set", None, None)),
        out_specs=P("set", "band", None),
        check_vma=False,
    )
```

time: 220 us -> 55.6 us (0.25)
  other arithmetic: 101 us -> 1 us
  matrix products: 47.9 us -> 0 us
  waiting for transfers between devices: 39.9 us -> 3.04 us
  Pallas kernels: 0 us -> 30 us
  starting transfers between devices: 0.01 us -> 19.8 us
  between operations: 13.5 us -> 0.14 us
  blocking collectives: 11.6 us -> 0 us
  local copies, waits for them, and re-layouts: 5.64 us -> 1.5 us
    select_n x4 -> x0, other arithmetic: 90.9 us -> none  [the longest x1 90 us: shards(): jnp.where(usable, jnp.cos(phases) * row_scale[:, None, None], 0.0)]
    dot_general x2 -> x0, matrix products: 47.9 us -> none  [the longest x1 38.4 us: shards(): jnp.einsum('prk,pjrc->pkjc', legend_mine, lax.all_gather(sources, 'band',...]
    reduce_scatter x1 -> x0, waiting for transfers between devices: 39.9 us -> none  [shards(): lax.psum_scatter(halves.reshape(2 * pair_count * lax.axis_size('set'), 2,...]
    pallas_call x0 -> x5, Pallas kernels: none -> 30 us  [the longest x2 17.3 us: fourier_sums(): pl.pallas_call(functools.partial(fourier_kernel, groups, first_group, pee...]
    ppermute x0 -> x13, starting transfers between devices: none -> 19.8 us  [the longest x6 10.1 us: shards(): lax.ppermute(parts[k].astype(WIRE), 'set', swap('set', set_size, 2 * k))]
    all_gather x1 -> x0, blocking collectives: 11.6 us -> none  [shards(): lax.all_gather(sources, 'band', axis=2, tiled=True)]
    another operation x2 -> x0, local copies, waits for them, and re-layouts: 4.25 us -> none  [shards(): jnp.stack([fourier[:, 0] + fourier[:, 1], fourier[:, 0] - fourier[:, 1]],...]
    another operation x1, other arithmetic: 3.37 us -> 0.08 us  [shards(): jnp.stack([band_index, band_index * slots, set_index * pair_count])]
  transfers between devices with their start and end apart: 1 -> 13, of which waited for: 1 -> 1; matrix products, arithmetic and copies ran while one was open for 0% -> 4% of each run, Pallas kernels for 0% -> 30%
where the time goes in v1:
time: 55.6 us; the launch traced here: 55.4 us
  Pallas kernels  30 us (54%)
  starting transfers between devices  19.8 us (36%)
  waiting for transfers between devices  3.04 us (5%)
  local copies, waits for them, and re-layouts  1.5 us (3%)
  other arithmetic  1 us (2%)
    pallas_call x2, Pallas kernels, fourier_sums(): pl.pallas_call(functools.partial(fourier_kernel, groups, first_group, pee...  17.3 us
    ppermute x6, starting transfers between devices, shards(): lax.ppermute(parts[k].astype(WIRE), 'set', swap('set', set_size, 2 * k))  10.1 us
    ppermute x6, starting transfers between devices, shards(): held.append(lax.ppermute(rounded, 'band', swap('band', band_size, k)))  9.22 us
    pallas_call x2, Pallas kernels, spectra_part(): pl.pallas_call(functools.partial(spectra_kernel, bands), grid=(groups,),...  8.97 us
    pallas_call x1, Pallas kernels, spread_weights(): pl.pallas_call(functools.partial(weights_kernel, pair_count, rows, bands)...  3.72 us
    ppermute x6, waiting for transfers between devices, shards(): lax.ppermute(parts[k].astype(WIRE), 'set', swap('set', set_size, 2 * k))  3.02 us
    unnamed x3, local copies, waits for them, and re-layouts  1.22 us
  transfers between devices with their start and end apart: 13, of which 1 were waited for; matrix products, arithmetic and copies ran while one was open for 4% of the time, Pallas kernels for 30%

profile of v1, /device:TPU:0, one launch (start us, length us, event | category | flops | bytes accessed | tf_op | source)
XLA Modules:
  0.0 55.4 jit_solution(4866742708753270651)
XLA Ops:
  0.0 0.5 collective-permute-start
  0.5 1.2 %copy.8.mine = f32[2,644,128]{2,1,0:T(8,128)S(1)} copy(f32[2,644,128]{2,0,1:T(2,128)} %param.3) | data formatting | bytes 1318912 | tf_op args[0]
  1.7 0.7 %pad_add_fusion.1.info = s32[8]{0:T(128)S(1)} fusion(s32[4]{0:T(128)S(1)} %xor_multiply_fusion, s32[2]{0:T(128)} %param.4, s32[1]{0:T(128)} %bitcast.4, s32[1]{0:T(128)} %bitcast.3), kind=kLoop, calls=%fused_computation.3 | loop fusion | flops 24 | bytes 64 | tf_op jit(solution)/shard_map/concatenate | solution.py:234
  2.4 0.0 collective-permute-done
  2.5 8.7 %fourier_sums.3 = (f32[320,128]{1,0:T(8,128)S(1)}, f32[320,128]{1,0:T(8,128)S(1)}, f32[320,128]{1,0:T(8,128)S(1)}, f32[320,128]{1,0:T(8,128)S(1)}) custom-call(s32[8]{0:T(128)S(1)} %pad_add_fusion.1.info, f32[2,644,128]{2,1,0:T(8,128)S(1)} %copy.8.mine, f32[2,644,128]{2,1,0:T(8,128)S(1)} %copy.9.theirs), custom_call_target="tpu_custom_call" | custom-call | tf_op jit(solution)/shard_map/fourier_sums/pallas_call | solution.py:125
  11.3 5.0 %collective-permute-start.9 = (f16[320,128]{1,0:T(8,128)(2,1)S(1)}, f16[320,128]{1,0:T(8,128)(2,1)S(1)}, u32[]{:S(2)}, u32[]{:S(2)}) collective-permute-start(f16[320,128]{1,0:T(8,128)(2,1)S(1)} %convert_element_type.53), channel_id=1, source_target_pairs={{0,6},{1,7},{2,4},{3,5},{4,2},{5,3},{6,0},{7,1},{8,14},{9,15},{10,... | collective-permute-start | bytes 245768 | tf_op jit(solution)/shard_map/ppermute | solution.py:245
  16.3 0.0 collective-permute-start.8
  16.3 0.6 %collective-permute-start.7 = (f16[320,128]{1,0:T(8,128)(2,1)S(1)}, f16[320,128]{1,0:T(8,128)(2,1)S(1)}, u32[]{:S(2)}, u32[]{:S(2)}) collective-permute-start(f16[320,128]{1,0:T(8,128)(2,1)S(1)} %convert_element_type.49), channel_id=1, source_target_pairs={{0,2},{1,3},{2,0},{3,1},{4,6},{5,7},{6,4},{7,5},{8,10},{9,11},{10,... | collective-permute-start | bytes 245768 | tf_op jit(solution)/shard_map/ppermute | solution.py:245
  16.9 0.2 constant_dynamic-slice_fusion.legend
  17.2 8.6 %fourier_sums.2 = (f32[320,128]{1,0:T(8,128)S(1)}, f32[320,128]{1,0:T(8,128)S(1)}, f32[320,128]{1,0:T(8,128)S(1)}, f32[320,128]{1,0:T(8,128)S(1)}) custom-call(s32[8]{0:T(128)S(1)} %pad_add_fusion.1.info, f32[2,644,128]{2,1,0:T(8,128)S(1)} %copy.8.mine, f32[2,644,128]{2,1,0:T(8,128)S(1)} %copy.9.theirs), custom_call_target="tpu_custom_call" | custom-call | tf_op jit(solution)/shard_map/fourier_sums/pallas_call | solution.py:125
  25.8 3.8 %collective-permute-start.3 = (f16[320,128]{1,0:T(8,128)(2,1)S(1)}, f16[320,128]{1,0:T(8,128)(2,1)S(1)}, u32[]{:S(2)}, u32[]{:S(2)}) collective-permute-start(f16[320,128]{1,0:T(8,128)(2,1)S(1)} %convert_element_type.46), channel_id=1, source_target_pairs={{0,6},{1,7},{2,4},{3,5},{4,2},{5,3},{6,0},{7,1},{8,14},{9,15},{10,... | collective-permute-start | bytes 245768 | tf_op jit(solution)/shard_map/ppermute | solution.py:245
  29.6 0.0 collective-permute-start.2
  29.6 0.0 collective-permute-done.9
  29.6 0.6 %collective-permute-start.1 = (f16[320,128]{1,0:T(8,128)(2,1)S(1)}, f16[320,128]{1,0:T(8,128)(2,1)S(1)}, u32[]{:S(2)}, u32[]{:S(2)}) collective-permute-start(f16[320,128]{1,0:T(8,128)(2,1)S(1)} %convert_element_type.42), channel_id=1, source_target_pairs={{0,2},{1,3},{2,0},{3,1},{4,6},{5,7},{6,4},{7,5},{8,10},{9,11},{10,... | collective-permute-start | bytes 245768 | tf_op jit(solution)/shard_map/ppermute | solution.py:245
  30.3 0.0 collective-permute-done.8
  30.3 0.0 collective-permute-done.7
  30.3 2.7 %collective-permute-start.12 = (bf16[320,128]{1,0:T(8,128)(2,1)S(1)}, bf16[320,128]{1,0:T(8,128)(2,1)S(1)}, u32[]{:S(2)}, u32[]{:S(2)}) collective-permute-start(bf16[320,128]{1,0:T(8,128)(2,1)S(1)} %add_convert_fusion.refs_0_), channel_id=1, source_target_pairs={{0,24},{8,16},{16,8},{24,0},{1,25},{9,17},{17,9},{25,1},{2,26},{10... | collective-permute-start | bytes 245768 | tf_op jit(solution)/shard_map/ppermute | solution.py:250
  33.0 0.0 collective-permute-done.3
  33.0 3.0 %collective-permute-done.2 = f16[320,128]{1,0:T(8,128)(2,1)S(1)} collective-permute-done((f16[320,128]{1,0:T(8,128)(2,1)S(1)}, f16[320,128]{1,0:T(8,128)(2,1)S(1)}, u32[]{:S(2)}, u32[]{:S(2)}) %collective-permute-start.2) | collective-permute-done | bytes 81952 | tf_op jit(solution)/shard_map/ppermute | solution.py:245
  36.0 0.0 collective-permute-done.1
  36.0 2.5 %collective-permute-start.6 = (bf16[320,128]{1,0:T(8,128)(2,1)S(1)}, bf16[320,128]{1,0:T(8,128)(2,1)S(1)}, u32[]{:S(2)}, u32[]{:S(2)}) collective-permute-start(bf16[320,128]{1,0:T(8,128)(2,1)S(1)} %add_convert_fusion.1.refs_0_), channel_id=1, source_target_pairs={{0,24},{8,16},{16,8},{24,0},{1,25},{9,17},{17,9},{25,1},{2,26},{10... | collective-permute-start | bytes 245768 | tf_op jit(solution)/shard_map/ppermute | solution.py:250
  38.6 0.5 collective-permute-start.5
  39.1 0.5 collective-permute-start.4
  39.6 1.6 %collective-permute-start.11 = (bf16[320,128]{1,0:T(8,128)(2,1)S(1)}, bf16[320,128]{1,0:T(8,128)(2,1)S(1)}, u32[]{:S(2)}, u32[]{:S(2)}) collective-permute-start(bf16[320,128]{1,0:T(8,128)(2,1)S(1)} %add_convert_fusion.refs_0_), channel_id=1, source_target_pairs={{0,16},{8,24},{16,0},{24,8},{1,17},{9,25},{17,1},{25,9},{2,18},{10... | collective-permute-start | bytes 245768 | tf_op jit(solution)/shard_map/ppermute | solution.py:250
  41.2 0.0 collective-permute-done.12.refs_3_
  41.2 1.5 %collective-permute-start.10 = (bf16[320,128]{1,0:T(8,128)(2,1)S(1)}, bf16[320,128]{1,0:T(8,128)(2,1)S(1)}, u32[]{:S(2)}, u32[]{:S(2)}) collective-permute-start(bf16[320,128]{1,0:T(8,128)(2,1)S(1)} %add_convert_fusion.refs_0_), channel_id=1, source_target_pairs={{0,8},{8,0},{16,24},{24,16},{1,9},{9,1},{17,25},{25,17},{2,10},{10... | collective-permute-start | bytes 245768 | tf_op jit(solution)/shard_map/ppermute | solution.py:250
  42.6 0.1 pad_add_fusion.info
  42.7 3.7 %spread_weights.1.weights = bf16[10,352,256]{2,1,0:T(8,128)(2,1)S(1)} custom-call(s32[3]{0:T(128)S(1)} %pad_add_fusion.info, bf16[80,8,352]{2,1,0:T(8,128)(2,1)S(1)} %constant_dynamic-slice_fusion.legend), custom_call_target="tpu_custom_call" | custom-call | tf_op jit(solution)/shard_map/spread_weights/pallas_call | solution.py:170
  46.4 0.0 collective-permute-done.11.refs_2_
  46.4 0.0 collective-permute-done.10.refs_1_
  46.4 4.5 %spectra_part.2.refs_4_ = f32[80,352,128]{2,1,0:T(8,128)} custom-call(bf16[10,352,256]{2,1,0:T(8,128)(2,1)S(1)} %spread_weights.1.weights, bf16[320,128]{1,0:T(8,128)(2,1)S(1)} %add_convert_fusion.refs_0_, bf16[320,128]{1,0:T(8,128)(2,1)S(1)} %collective-permute-done.10.refs_1_, bf16[320,128]{1,0:T(8,128)(2,1)S(1)} %collective-permute-done.11.refs_2_, ...), custom_call_target="tpu_custom_call" | custom-call | tf_op jit(solution)/shard_map/spectra_part/pallas_call | solution.py:204
  50.9 4.5 %spectra_part.3 = f32[80,352,128]{2,1,0:T(8,128)} custom-call(bf16[10,352,256]{2,1,0:T(8,128)(2,1)S(1)} %spread_weights.1.weights, bf16[320,128]{1,0:T(8,128)(2,1)S(1)} %add_convert_fusion.1.refs_0_, bf16[320,128]{1,0:T(8,128)(2,1)S(1)} %collective-permute-done.4.refs_1_, ...), custom_call_target="tpu_custom_call", output_to_operand_aliasing={{}: (5, {})} | custom-call | tf_op jit(solution)/shard_map/spectra_part/pallas_call | solution.py:204
  (15 shorter events, 0.2 us)
Async XLA Ops:
  0.0 16.9 %copy-start = (bf16[80,8,1408]{2,1,0:T(8,128)(2,1)S(1)}, bf16[80,8,1408]{2,1,0:T(8,128)(2,1)}, u32[]{:S(2)}) copy-start(bf16[80,8,1408]{2,1,0:T(8,128)(2,1)} %param.5) | copy-start | bytes 5406724
  0.0 2.4 %collective-permute-start = (f32[2,644,128]{2,0,1:T(2,128)}, f32[2,644,128]{2,0,1:T(2,128)S(1)}, u32[]{:S(2)}, u32[]{:S(2)}) collective-permute-start(f32[2,644,128]{2,0,1:T(2,128)} %param.3), channel_id=1, source_target_pairs={{0,1},{1,0},{2,3},{3,2},{4,5},{5,4},{6,7},{7,6},{8,9},{9,8},{10,11... | collective-permute-start | bytes 1978376 | tf_op jit(solution)/shard_map/ppermute | solution.py:231
  11.3 18.3 %collective-permute-start.9 = (f16[320,128]{1,0:T(8,128)(2,1)S(1)}, f16[320,128]{1,0:T(8,128)(2,1)S(1)}, u32[]{:S(2)}, u32[]{:S(2)}) collective-permute-start(f16[320,128]{1,0:T(8,128)(2,1)S(1)} %convert_element_type.53), channel_id=1, source_target_pairs={{0,6},{1,7},{2,4},{3,5},{4,2},{5,3},{6,0},{7,1},{8,14},{9,15},{10,... | collective-permute-start | bytes 245768 | tf_op jit(solution)/shard_map/ppermute | solution.py:245
  16.3 14.0 %collective-permute-start.8 = (f16[320,128]{1,0:T(8,128)(2,1)S(1)}, f16[320,128]{1,0:T(8,128)(2,1)S(1)}, u32[]{:S(2)}, u32[]{:S(2)}) collective-permute-start(f16[320,128]{1,0:T(8,128)(2,1)S(1)} %convert_element_type.51), channel_id=1, source_target_pairs={{0,4},{1,5},{2,6},{3,7},{4,0},{5,1},{6,2},{7,3},{8,12},{9,13},{10,... | collective-permute-start | bytes 245768 | tf_op jit(solution)/shard_map/ppermute | solution.py:245
  16.3 14.0 %collective-permute-start.7 = (f16[320,128]{1,0:T(8,128)(2,1)S(1)}, f16[320,128]{1,0:T(8,128)(2,1)S(1)}, u32[]{:S(2)}, u32[]{:S(2)}) collective-permute-start(f16[320,128]{1,0:T(8,128)(2,1)S(1)} %convert_element_type.49), channel_id=1, source_target_pairs={{0,2},{1,3},{2,0},{3,1},{4,6},{5,7},{6,4},{7,5},{8,10},{9,11},{10,... | collective-permute-start | bytes 245768 | tf_op jit(solution)/shard_map/ppermute | solution.py:245
  25.8 7.2 %collective-permute-start.3 = (f16[320,128]{1,0:T(8,128)(2,1)S(1)}, f16[320,128]{1,0:T(8,128)(2,1)S(1)}, u32[]{:S(2)}, u32[]{:S(2)}) collective-permute-start(f16[320,128]{1,0:T(8,128)(2,1)S(1)} %convert_element_type.46), channel_id=1, source_target_pairs={{0,6},{1,7},{2,4},{3,5},{4,2},{5,3},{6,0},{7,1},{8,14},{9,15},{10,... | collective-permute-start | bytes 245768 | tf_op jit(solution)/shard_map/ppermute | solution.py:245
  29.6 6.4 %collective-permute-start.2 = (f16[320,128]{1,0:T(8,128)(2,1)S(1)}, f16[320,128]{1,0:T(8,128)(2,1)S(1)}, u32[]{:S(2)}, u32[]{:S(2)}) collective-permute-start(f16[320,128]{1,0:T(8,128)(2,1)S(1)} %convert_element_type.44), channel_id=1, source_target_pairs={{0,4},{1,5},{2,6},{3,7},{4,0},{5,1},{6,2},{7,3},{8,12},{9,13},{10,... | collective-permute-start | bytes 245768 | tf_op jit(solution)/shard_map/ppermute | solution.py:245
  29.6 6.4 %collective-permute-start.1 = (f16[320,128]{1,0:T(8,128)(2,1)S(1)}, f16[320,128]{1,0:T(8,128)(2,1)S(1)}, u32[]{:S(2)}, u32[]{:S(2)}) collective-permute-start(f16[320,128]{1,0:T(8,128)(2,1)S(1)} %convert_element_type.42), channel_id=1, source_target_pairs={{0,2},{1,3},{2,0},{3,1},{4,6},{5,7},{6,4},{7,5},{8,10},{9,11},{10,... | collective-permute-start | bytes 245768 | tf_op jit(solution)/shard_map/ppermute | solution.py:245
  30.3 10.8 %collective-permute-start.12 = (bf16[320,128]{1,0:T(8,128)(2,1)S(1)}, bf16[320,128]{1,0:T(8,128)(2,1)S(1)}, u32[]{:S(2)}, u32[]{:S(2)}) collective-permute-start(bf16[320,128]{1,0:T(8,128)(2,1)S(1)} %add_convert_fusion.refs_0_), channel_id=1, source_target_pairs={{0,24},{8,16},{16,8},{24,0},{1,25},{9,17},{17,9},{25,1},{2,26},{10... | collective-permute-start | bytes 245768 | tf_op jit(solution)/shard_map/ppermute | solution.py:250
  36.0 14.9 %collective-permute-start.6 = (bf16[320,128]{1,0:T(8,128)(2,1)S(1)}, bf16[320,128]{1,0:T(8,128)(2,1)S(1)}, u32[]{:S(2)}, u32[]{:S(2)}) collective-permute-start(bf16[320,128]{1,0:T(8,128)(2,1)S(1)} %add_convert_fusion.1.refs_0_), channel_id=1, source_target_pairs={{0,24},{8,16},{16,8},{24,0},{1,25},{9,17},{17,9},{25,1},{2,26},{10... | collective-permute-start | bytes 245768 | tf_op jit(solution)/shard_map/ppermute | solution.py:250
  38.6 12.4 %collective-permute-start.5 = (bf16[320,128]{1,0:T(8,128)(2,1)S(1)}, bf16[320,128]{1,0:T(8,128)(2,1)S(1)}, u32[]{:S(2)}, u32[]{:S(2)}) collective-permute-start(bf16[320,128]{1,0:T(8,128)(2,1)S(1)} %add_convert_fusion.1.refs_0_), channel_id=1, source_target_pairs={{0,16},{8,24},{16,0},{24,8},{1,17},{9,25},{17,1},{25,9},{2,18},{10... | collective-permute-start | bytes 245768 | tf_op jit(solution)/shard_map/ppermute | solution.py:250
  39.1 11.9 %collective-permute-start.4 = (bf16[320,128]{1,0:T(8,128)(2,1)S(1)}, bf16[320,128]{1,0:T(8,128)(2,1)S(1)}, u32[]{:S(2)}, u32[]{:S(2)}) collective-permute-start(bf16[320,128]{1,0:T(8,128)(2,1)S(1)} %add_convert_fusion.1.refs_0_), channel_id=1, source_target_pairs={{0,8},{8,0},{16,24},{24,16},{1,9},{9,1},{17,25},{25,17},{2,10},{10... | collective-permute-start | bytes 245768 | tf_op jit(solution)/shard_map/ppermute | solution.py:250
  39.6 6.8 %collective-permute-start.11 = (bf16[320,128]{1,0:T(8,128)(2,1)S(1)}, bf16[320,128]{1,0:T(8,128)(2,1)S(1)}, u32[]{:S(2)}, u32[]{:S(2)}) collective-permute-start(bf16[320,128]{1,0:T(8,128)(2,1)S(1)} %add_convert_fusion.refs_0_), channel_id=1, source_target_pairs={{0,16},{8,24},{16,0},{24,8},{1,17},{9,25},{17,1},{25,9},{2,18},{10... | collective-permute-start | bytes 245768 | tf_op jit(solution)/shard_map/ppermute | solution.py:250
  41.2 5.3 %collective-permute-start.10 = (bf16[320,128]{1,0:T(8,128)(2,1)S(1)}, bf16[320,128]{1,0:T(8,128)(2,1)S(1)}, u32[]{:S(2)}, u32[]{:S(2)}) collective-permute-start(bf16[320,128]{1,0:T(8,128)(2,1)S(1)} %add_convert_fusion.refs_0_), channel_id=1, source_target_pairs={{0,8},{8,0},{16,24},{24,16},{1,9},{9,1},{17,25},{25,17},{2,10},{10... | collective-permute-start | bytes 245768 | tf_op jit(solution)/shard_map/ppermute | solution.py:250

commit v2 on v1

v2 whole, which is shorter than its diff:
```python
import functools
import math

import jax
import jax.numpy as jnp
from jax import lax
from jax.experimental import pallas as pl
from jax.experimental.pallas import tpu as pltpu
from jax.sharding import PartitionSpec as P

TRUNC = 1279
GROUP = 8
F32 = jnp.float32
BF16 = jnp.bfloat16
WIRE = jnp.float16


def round_up(value, step):
    return -(-value // step) * step


def unit_circle(multiplier, point, length, inverse):
    product = (multiplier * point).astype(F32)
    residue = product - jnp.floor(product * inverse + 0.5) * length
    quarters = 4.0 * residue * inverse
    turn = jnp.floor(quarters + 0.5)
    angle = (quarters - turn) * (0.5 * math.pi)
    square = angle * angle
    sine = angle * (1.0 + square * (-1 / 6 + square * (1 / 120 + square * (-1 / 5040 + square / 362880))))
    cosine = 1.0 + square * (-0.5 + square * (1 / 24 + square * (-1 / 720 + square / 40320)))
    quadrant = turn.astype(jnp.int32) & 3
    odd = (quadrant & 1) == 1
    real = jnp.where(odd, sine, cosine)
    imag = jnp.where(odd, cosine, sine)
    real = jnp.where((quadrant == 1) | (quadrant == 2), -real, real)
    imag = jnp.where(quadrant >= 2, imag, -imag)
    return real, imag


def rotate(a, b):
    return a[0] * b[0] - a[1] * b[1], a[0] * b[1] + a[1] * b[0]


def split(values):
    high = values.astype(BF16)
    return high, (values - high.astype(F32)).astype(BF16)


def prepare_values(raw, start, length, length_int):
    width = raw.shape[1]
    lane = lax.broadcasted_iota(jnp.int32, (1, width), 1)
    where = start + lax.broadcasted_iota(jnp.int32, (raw.shape[0], 1), 0)
    folded = pltpu.roll(raw, width // 2, 1) + jnp.where(lane < width // 2, raw, -raw)
    scale = lax.rsqrt(jnp.full((1, width), length, F32))
    return split(jnp.where(where < length_int, folded * scale, 0.0))


def store_values(out, r, raw, start, length_int):
    points, width = raw.shape
    out[r, :points, :width], out[r, :points, width:] = prepare_values(raw, start, length_int.astype(F32), length_int)
    out[r, points:, :] = jnp.zeros((out.shape[1] - points, 2 * width), BF16)


def row_of(block, r, rows):
    return block[pl.ds(r, block.shape[0] // rows, stride=rows), :]


def prepare_kernel(peers, pair_count, points, row_points, mine, values, factor):
    rows, _, tall, depth = factor.shape
    held = round_up(pl.cdiv(pair_count, GROUP), GROUP)
    set_index = lax.axis_index("set")
    start = set_index * points
    beside = (set_index ^ 1) * points - start
    slot = lax.broadcasted_iota(jnp.int32, (1, depth), 1)
    point = jnp.where(slot < values.shape[1], start + slot, beside)
    heads = round_up(peers + 1, GROUP)
    sub = lax.broadcasted_iota(jnp.int32, (GROUP + heads + held, 1), 0)
    order = sub - GROUP
    head = jnp.where(order < peers, (set_index ^ (2 * order)) * pair_count, TRUNC)
    multiplier = jnp.where(sub < GROUP, sub, jnp.where(order < heads, head, (order - heads) * GROUP))
    for r in range(rows):
        length = row_points[r].astype(F32)
        real, imag = unit_circle(multiplier, point, length, 1.0 / length)
        factor[r, 0, :GROUP, :] = real[:GROUP]
        factor[r, 1, :GROUP, :] = imag[:GROUP]
        last = GROUP + peers
        factor[r, 0, GROUP:2 * GROUP, :] = jnp.broadcast_to(real[last:last + 1], (GROUP, depth))
        factor[r, 1, GROUP:2 * GROUP, :] = jnp.broadcast_to(imag[last:last + 1], (GROUP, depth))
        tail = real[GROUP + heads:], imag[GROUP + heads:]
        for peer in range(peers):
            at = GROUP + peer
            base = rotate((real[at:at + 1], imag[at:at + 1]), tail)
            to = 2 * GROUP + peer * held
            factor[r, 0, to:to + held, :] = base[0]
            factor[r, 1, to:to + held, :] = base[1]
        store_values(values, r, row_of(mine, r, rows), start, row_points[r])


def prepare(row_points, mine, peers, pair_count):
    rows = row_points.shape[0]
    points, width = mine.shape[0] // rows, mine.shape[1]
    depth = round_up(points, 128)
    tall = 2 * GROUP + peers * round_up(pl.cdiv(pair_count, GROUP), GROUP)
    vmem = pl.BlockSpec(memory_space=pltpu.VMEM)
    return pl.pallas_call(
        functools.partial(prepare_kernel, peers, pair_count, points),
        out_shape=[
            jax.ShapeDtypeStruct((rows, depth, 2 * width), BF16),
            jax.ShapeDtypeStruct((rows, 2, tall, depth + 128), F32),
        ],
        in_specs=[pl.BlockSpec(memory_space=pltpu.SMEM), vmem],
        out_specs=[vmem, vmem],
        compiler_params=pltpu.CompilerParams(vmem_limit_bytes=48 * 2**20),
        name="prepare",
    )(row_points, mine)


def fourier_kernel(groups, first_group, peers, pair_count, fresh, row_points, mine, theirs, factor, *refs):
    outs = refs[:peers]
    table, sums, twist = refs[-3:]
    rows, depth, double = mine.shape
    width = double // 2
    held = round_up(pl.cdiv(pair_count, GROUP), GROUP)
    set_index = lax.axis_index("set")
    if fresh:
        values = refs[peers]
        points = theirs.shape[0] // rows
        for r in range(rows):
            store_values(values, r, row_of(theirs, r, rows), (set_index ^ 1) * points, row_points[r])
    else:
        values = theirs
    lane = lax.broadcasted_iota(jnp.int32, (1, width), 1)
    north = lane < width // 2
    sub = lax.broadcasted_iota(jnp.int32, (GROUP, 1), 0)
    for r in range(rows):

        def fill(index, carry):
            at = 2 * GROUP + index // groups * held + first_group + index % groups
            base = factor[r, 0, pl.ds(at, 1), :], factor[r, 1, pl.ds(at, 1), :]
            first = rotate(base, (factor[r, 0, :GROUP, :], factor[r, 1, :GROUP, :]))
            last = factor[r, 0, GROUP:2 * GROUP, :], factor[r, 1, GROUP:2 * GROUP, :]
            second = rotate(last, (first[0], -first[1]))
            block = jnp.concatenate([*first, *second], axis=0)
            high, low = split(block[:, :depth])
            start = pl.multiple_of(index * 4 * GROUP, 4 * GROUP)
            table[0, pl.ds(start, 4 * GROUP), :] = high
            table[1, pl.ds(start, 4 * GROUP), :] = low
            twist[r, pl.ds(start, 4 * GROUP), :] = block[:, depth:]
            return carry

        lax.fori_loop(0, peers * groups, fill, 0, unroll=2)
        own = jnp.dot(table[0], mine[r], preferred_element_type=F32)
        other = jnp.dot(table[0], values[r], preferred_element_type=F32)
        both = jnp.concatenate([mine[r, :, :width], values[r, :, :width]], axis=1)
        rest = jnp.dot(table[1], both, preferred_element_type=F32)
        sums[r, :, :width] = own[:, :width] + own[:, width:] + rest[:, :width]
        sums[r, :, width:] = other[:, :width] + other[:, width:] + rest[:, width:]
    for peer in range(peers):
        for g in range(groups):
            base = (set_index ^ (2 * peer)) * pair_count + (first_group + g) * GROUP
            for side in range(2):
                wave = base + sub
                wave = TRUNC - wave if side else wave
                at = ((peer * groups + g) * 2 + side) * 2 * GROUP
                for r in range(rows):
                    turn = twist[r, at:at + GROUP, :], twist[r, at + GROUP:at + 2 * GROUP, :]
                    far = sums[r, at:at + GROUP, width:], sums[r, at + GROUP:at + 2 * GROUP, width:]
                    far = rotate(turn, far)
                    real = sums[r, at:at + GROUP, :width] + far[0]
                    imag = sums[r, at + GROUP:at + 2 * GROUP, :width] + far[1]
                    usable = wave <= (row_points[r] - 1) // 2
                    even = jnp.where(north, real, pltpu.roll(imag, width // 2, 1))
                    odd = jnp.where(north, pltpu.roll(real, width // 2, 1), imag)
                    for parity, block in enumerate((even, odd)):
                        to = (((g * 2 + side) * 2 + parity) * rows + r) * GROUP
                        outs[peer][to:to + GROUP, :] = jnp.where(usable, block, 0.0)


def fourier_sums(row_points, mine, theirs, factor, groups, first_group, peers, pair_count):
    rows, depth, double = mine.shape
    width = double // 2
    fresh = theirs.ndim == 2
    out_rows = groups * 4 * rows * GROUP
    tall = peers * groups * 4 * GROUP
    vmem = pl.BlockSpec(memory_space=pltpu.VMEM)
    out_shape = [jax.ShapeDtypeStruct((out_rows, width), F32)] * peers
    out_shape += [jax.ShapeDtypeStruct(mine.shape, BF16)] if fresh else []
    return pl.pallas_call(
        functools.partial(fourier_kernel, groups, first_group, peers, pair_count, fresh),
        out_shape=out_shape,
        in_specs=[pl.BlockSpec(memory_space=pltpu.SMEM), vmem, vmem, vmem],
        out_specs=[vmem] * len(out_shape),
        scratch_shapes=[
            pltpu.VMEM((2, tall, depth), BF16),
            pltpu.VMEM((rows, tall, double), F32),
            pltpu.VMEM((rows, tall, 128), F32),
        ],
        compiler_params=pltpu.CompilerParams(vmem_limit_bytes=48 * 2**20),
        name="fourier_sums",
    )(row_points, mine, theirs, factor)


def weights_kernel(rows, bands, legend, out):
    pair_count, total, slots = legend.shape
    wide = out.shape[2]
    band_index = lax.axis_index("band")
    first_pair = lax.axis_index("set") * pair_count
    source = lax.broadcasted_iota(jnp.int32, (GROUP * total, 1), 0)
    lane = lax.broadcasted_iota(jnp.int32, (1, wide), 1)
    member = lane % GROUP
    row = lane // GROUP % rows
    parity = lane // (GROUP * rows) % 2
    side = lane // (GROUP * rows * 2) % 2
    band = (lane // (GROUP * rows * 4)) ^ band_index
    spread = (source == member * total + band * rows + row).astype(F32).astype(BF16)
    slot = band_index * slots + lax.broadcasted_iota(jnp.int32, (slots, 1), 0)
    for group in range(out.shape[0]):
        count = min(GROUP, pair_count - group * GROUP)
        held = legend[group * GROUP:group * GROUP + count].astype(F32).reshape(count * total, slots)
        if count < GROUP:
            held = jnp.concatenate([held, jnp.zeros(((GROUP - count) * total, slots), F32)], axis=0)
        moved = lax.dot_general(
            held.astype(BF16), spread, (((0,), (0,)), ((), ())), preferred_element_type=F32
        )
        first = TRUNC - (first_pair + group * GROUP + member)
        start = jnp.where(side == 0, 0, first + 1)
        sign = 1 - 2 * side
        match = (((slot - start) & 1) == parity) & (sign * slot <= sign * first - side)
        out[group] = jnp.where(match, moved, 0.0).astype(BF16)


def spread_weights(legend, rows, bands):
    pair_count, total, slots = legend.shape
    groups = pl.cdiv(pair_count, GROUP)
    vmem = pl.BlockSpec(memory_space=pltpu.VMEM)
    return pl.pallas_call(
        functools.partial(weights_kernel, rows, bands),
        out_shape=jax.ShapeDtypeStruct((groups, slots, bands * 4 * rows * GROUP), BF16),
        in_specs=[vmem],
        out_specs=vmem,
        compiler_params=pltpu.CompilerParams(vmem_limit_bytes=48 * 2**20),
        name="spread_weights",
    )(legend)


def spectra_kernel(bands, first_group, pairs, weights, *refs):
    held = refs[:bands]
    out, block, sems = refs[-3:]
    width = held[0].shape[1]
    tall = held[0].shape[0]
    groups = pl.cdiv(pairs, GROUP)
    part = tall // groups
    member = lax.broadcasted_iota(jnp.int32, (2 * GROUP, width), 0) % GROUP
    masks = [jnp.tile((member == i).astype(F32).astype(BF16), (bands * part // (2 * GROUP), 1)) for i in range(GROUP)]
    copies = []
    for g in range(groups):
        stacked = jnp.concatenate([ref[g * part:(g + 1) * part, :] for ref in held], axis=0)
        for at in range(0, min(GROUP, pairs - g * GROUP), 2):
            both = jnp.concatenate([stacked * masks[at], stacked * masks[at + 1]], axis=1)
            product = jnp.dot(weights[first_group + g], both, preferred_element_type=F32)
            pair = g * GROUP + at
            block[pair] = product[:, :width]
            block[pair + 1] = product[:, width:]
            copy = pltpu.make_async_copy(
                block.at[pl.ds(pair, 2)], out.at[pl.ds(first_group * GROUP + pair, 2)], sems.at[pair // 2]
            )
            copy.start()
            copies.append(copy)
    for copy in copies:
        copy.wait()


def spectra_part(weights, held, out, pair_count, first_group, groups):
    bands = len(held)
    width = held[0].shape[1]
    slots = weights.shape[1]
    pairs = min(groups * GROUP, pair_count - first_group * GROUP)
    previous = [] if out is None else [out]
    vmem = pl.BlockSpec(memory_space=pltpu.VMEM)
    anywhere = pl.BlockSpec(memory_space=pl.ANY)
    return pl.pallas_call(
        functools.partial(spectra_kernel, bands, first_group, pairs),
        out_shape=jax.ShapeDtypeStruct((pair_count, slots, width), F32),
        in_specs=[vmem] * (1 + bands) + [anywhere] * len(previous),
        out_specs=anywhere,
        input_output_aliases={1 + bands: 0} if previous else {},
        scratch_shapes=[pltpu.VMEM((pairs, slots, width), F32), pltpu.SemaphoreType.DMA((pairs // 2,))],
        compiler_params=pltpu.CompilerParams(vmem_limit_bytes=48 * 2**20),
        name="spectra_part",
    )(weights, *held, *previous)


def swap(axis, size, step):
    return [(i, i ^ step) for i in range(size)]


def exchange(array, axis, steps):
    return [lax.ppermute(part, axis, swap(axis, lax.axis_size(axis), step)) for part, step in zip(array, steps)]


def shards(grid, row_points, legendre):
    set_size = lax.axis_size("set")
    band_size = lax.axis_size("band")
    rows, points, width = grid.shape
    pair_count = legendre.shape[0]
    slots = legendre.shape[2] // band_size
    peers = set_size // 2
    flat = grid.transpose(1, 0, 2).reshape(points * rows, width)
    theirs = lax.ppermute(flat, "set", swap("set", set_size, 1))
    mine, factor = prepare(row_points, flat, peers, pair_count)
    legend = lax.dynamic_slice_in_dim(legendre, lax.axis_index("band") * slots, slots, 2)
    weights = spread_weights(legend, rows, band_size)
    all_groups = pl.cdiv(pair_count, GROUP)
    cut = (all_groups + 1) // 2
    out = None
    steps = list(range(1, peers, 2)) + list(range(2, peers, 2))[::-1]
    chunks = ((0, cut), (cut, all_groups - cut))
    gathered = []
    partial = []
    for first_group, groups in chunks:
        parts = list(fourier_sums(row_points, mine, theirs, factor, groups, first_group, peers, pair_count))
        if not partial:
            theirs = parts.pop()
        partial.append(parts)
    for parts in partial:
        arrived = exchange([parts[k].astype(WIRE) for k in steps], "set", [2 * k for k in steps])
        if gathered:
            arrived, weights, gathered[0] = lax.optimization_barrier((arrived, weights, gathered[0]))
        total = parts[0]
        for part in arrived:
            total = total + part.astype(F32)
        rounded = total.astype(BF16)
        turns = list(range(1, band_size))
        gathered.append([rounded] + exchange([rounded] * len(turns), "band", turns))
    for held, (first_group, groups) in zip(gathered, chunks):
        out = spectra_part(weights, held, out, pair_count, first_group, groups)
    return out


def solution(mesh):
    return jax.shard_map(
        shards,
        mesh=mesh,
        in_specs=(P("band", "set", None), P("band"), P("set", None, None)),
        out_specs=P("set", "band", None),
        check_vma=False,
    )
```

time: 55.6 us -> 48.2 us (0.87)
  Pallas kernels: 30 us -> 18.3 us
  local copies, waits for them, and re-layouts: 1.5 us -> 6.1 us
  starting transfers between devices: 19.8 us -> 18.4 us
  waiting for transfers between devices: 3.04 us -> 3.96 us
    pallas_call x2, Pallas kernels: 17.3 us -> 9.21 us  [fourier_sums(): pl.pallas_call(functools.partial(fourier_kernel, groups, first_group, pee...]
    unnamed x3 -> x16, local copies, waits for them, and re-layouts: 1.22 us -> 5.87 us
    pallas_call x3 -> x4, Pallas kernels: 12.7 us -> 9.08 us  [the longest x2 6.71 us: spectra_part(): pl.pallas_call(functools.partial(spectra_kernel, bands, first_group, pair...]
    ppermute x13, starting transfers between devices: 19.8 us -> 18.4 us  [the longest x12 17.9 us: exchange(): lax.ppermute(part, axis, swap(axis, lax.axis_size(axis), step))]
    ppermute x13, waiting for transfers between devices: 3.04 us -> 3.96 us  [the longest x12 3.96 us: exchange(): lax.ppermute(part, axis, swap(axis, lax.axis_size(axis), step))]
    convert_element_type x2, other arithmetic: 0.09 us -> 0.99 us  [shards(): rounded = total.astype(BF16)]
    concatenate x1 -> x0, other arithmetic: 0.74 us -> none  [shards(): jnp.concatenate([places, row_points, (set_index ^ steps) * pair_count])]
  transfers between devices with their start and end apart: 13 -> 13, of which waited for: 1 -> 3; matrix products, arithmetic and copies ran while one was open for 4% -> 3% of each run, Pallas kernels for 30% -> 21%
where the time goes in v2:
time: 48.2 us; the launch traced here: 48 us
  starting transfers between devices  18.4 us (38%)
  Pallas kernels  18.3 us (38%)
  local copies, waits for them, and re-layouts  6.1 us (13%)
  waiting for transfers between devices  3.96 us (8%)
  other arithmetic  1.08 us (2%)
    ppermute x12, starting transfers between devices, exchange(): lax.ppermute(part, axis, swap(axis, lax.axis_size(axis), step))  17.9 us
    pallas_call x2, Pallas kernels, fourier_sums(): pl.pallas_call(functools.partial(fourier_kernel, groups, first_group, pee...  9.21 us
    pallas_call x2, Pallas kernels, spectra_part(): pl.pallas_call(functools.partial(spectra_kernel, bands, first_group, pair...  6.71 us
    unnamed x16, local copies, waits for them, and re-layouts  5.87 us
    ppermute x12, waiting for transfers between devices, exchange(): lax.ppermute(part, axis, swap(axis, lax.axis_size(axis), step))  3.96 us
    pallas_call x1, Pallas kernels, prepare(): pl.pallas_call(functools.partial(prepare_kernel, peers, pair_count, point...  1.39 us
    convert_element_type x2, other arithmetic, shards(): rounded = total.astype(BF16)  0.99 us
    pallas_call x1, Pallas kernels, spread_weights(): pl.pallas_call(functools.partial(weights_kernel, rows, bands), out_shape=...  0.97 us
  transfers between devices with their start and end apart: 13, of which 3 were waited for; matrix products, arithmetic and copies ran while one was open for 3% of the time, Pallas kernels for 21%

profile of v2, /device:TPU:0, one launch (start us, length us, event | category | flops | bytes accessed | tf_op | source)
XLA Modules:
  0.0 48.0 jit_solution(13151203058138502991)
XLA Ops:
  0.0 0.5 collective-permute-start
  0.5 1.2 %copy-done.5 = f32[2,644,128]{2,0,1:T(2,128)S(1)} copy-done((f32[2,644,128]{2,0,1:T(2,128)S(1)}, f32[2,644,128]{2,0,1:T(2,128)}, u32[]{:S(2)}) %copy-start.5) | copy-done | bytes 659480
  1.6 0.7 %copy-done.6 = s32[2]{0:T(128)S(1)} copy-done((s32[2]{0:T(128)S(1)}, s32[2]{0:T(128)}, u32[]{:S(2)}) %copy-start.6) | copy-done | bytes 32
  2.3 1.4 %prepare.1 = (bf16[2,768,256]{2,1,0:T(8,128)(2,1)S(1)}, f32[2,2,80,896]{3,2,1,0:T(8,128)S(1)}) custom-call(s32[2]{0:T(128)S(1)} %copy-done.6, f32[1288,128]{1,0:T(8,128)S(1)} %bitcast.4), custom_call_target="tpu_custom_call" | custom-call | tf_op jit(solution)/shard_map/prepare/pallas_call | solution.py:105
  3.7 0.0 copy-start.7
  3.7 4.8 %fourier_sums.2 = (f32[320,128]{1,0:T(8,128)S(1)}, f32[320,128]{1,0:T(8,128)S(1)}, f32[320,128]{1,0:T(8,128)S(1)}, f32[320,128]{1,0:T(8,128)S(1)}, bf16[2,768,256]{2,1,0:T(8,128)(2,1)S(1)}) custom-call(s32[2]{0:T(128)S(1)} %copy-done.6, bf16[2,768,256]{2,1,0:T(8,128)(2,1)S(1)} %get-tuple-element.24.mine, f32[1288,128]{1,0:T(8,128)S(1)} %collective-permute-done.theirs, ...), custom_call_target="tpu_custom_call" | custom-call | tf_op jit(solution)/shard_map/fourier_sums/pallas_call | solution.py:188
  8.5 0.0 copy-start.1
  8.5 0.9 %copy-done.1 = bf16[2,768,256]{2,1,0:T(8,128)(2,1)} copy-done((bf16[2,768,256]{2,1,0:T(8,128)(2,1)}, bf16[2,768,256]{2,1,0:T(8,128)(2,1)S(1)}, u32[]{:S(2)}) %copy-start.1) | copy-done | bytes 786456
  9.4 0.9 %copy-done.3 = bf16[2,768,256]{2,1,0:T(8,128)(2,1)} copy-done((bf16[2,768,256]{2,1,0:T(8,128)(2,1)}, bf16[2,768,256]{2,1,0:T(8,128)(2,1)S(1)}, u32[]{:S(2)}) %copy-start.3) | copy-done | bytes 786456
  10.3 3.7 %collective-permute-start.6 = (f16[320,128]{1,0:T(8,128)(2,1)S(1)}, f16[320,128]{1,0:T(8,128)(2,1)S(1)}, u32[]{:S(2)}, u32[]{:S(2)}) collective-permute-start(f16[320,128]{1,0:T(8,128)(2,1)S(1)} %convert_element_type.49), channel_id=1, source_target_pairs={{0,4},{1,5},{2,6},{3,7},{4,0},{5,1},{6,2},{7,3},{8,12},{9,13},{10,... | collective-permute-start | bytes 245768 | tf_op jit(solution)/shard_map/ppermute | solution.py:298
  14.0 1.4 %collective-permute-start.5 = (f16[320,128]{1,0:T(8,128)(2,1)S(1)}, f16[320,128]{1,0:T(8,128)(2,1)S(1)}, u32[]{:S(2)}, u32[]{:S(2)}) collective-permute-start(f16[320,128]{1,0:T(8,128)(2,1)S(1)} %convert_element_type.47), channel_id=1, source_target_pairs={{0,6},{1,7},{2,4},{3,5},{4,2},{5,3},{6,0},{7,1},{8,14},{9,15},{10,... | collective-permute-start | bytes 245768 | tf_op jit(solution)/shard_map/ppermute | solution.py:298
  15.4 0.3 collective-permute-start.4
  15.7 1.1 %copy-done.2 = bf16[2,768,256]{2,1,0:T(8,128)(2,1)S(1)} copy-done((bf16[2,768,256]{2,1,0:T(8,128)(2,1)S(1)}, bf16[2,768,256]{2,1,0:T(8,128)(2,1)}, u32[]{:S(2)}) %copy-start.2) | copy-done | bytes 786456
  16.9 1.1 %copy-done.4 = bf16[2,768,256]{2,1,0:T(8,128)(2,1)S(1)} copy-done((bf16[2,768,256]{2,1,0:T(8,128)(2,1)S(1)}, bf16[2,768,256]{2,1,0:T(8,128)(2,1)}, u32[]{:S(2)}) %copy-start.4) | copy-done | bytes 786456
  18.0 4.4 %fourier_sums.3 = (f32[320,128]{1,0:T(8,128)S(1)}, f32[320,128]{1,0:T(8,128)S(1)}, f32[320,128]{1,0:T(8,128)S(1)}, f32[320,128]{1,0:T(8,128)S(1)}) custom-call(s32[2]{0:T(128)S(1)} %copy-done.7, bf16[2,768,256]{2,1,0:T(8,128)(2,1)S(1)} %copy-done.2, bf16[2,768,256]{2,1,0:T(8,128)(2,1)S(1)} %copy-done.4, f32[2,2,80,896]{3,2,1,0:T(8,128)S(1)} %get-tuple-element.25.factor), custom_call_target="tpu_custom_call" | custom-call | tf_op jit(solution)/shard_map/fourier_sums/pallas_call | solution.py:188
  22.5 2.8 %collective-permute-start.3 = (f16[320,128]{1,0:T(8,128)(2,1)S(1)}, f16[320,128]{1,0:T(8,128)(2,1)S(1)}, u32[]{:S(2)}, u32[]{:S(2)}) collective-permute-start(f16[320,128]{1,0:T(8,128)(2,1)S(1)} %convert_element_type.44), channel_id=1, source_target_pairs={{0,4},{1,5},{2,6},{3,7},{4,0},{5,1},{6,2},{7,3},{8,12},{9,13},{10,... | collective-permute-start | bytes 245768 | tf_op jit(solution)/shard_map/ppermute | solution.py:298
  25.3 1.3 %collective-permute-start.2 = (f16[320,128]{1,0:T(8,128)(2,1)S(1)}, f16[320,128]{1,0:T(8,128)(2,1)S(1)}, u32[]{:S(2)}, u32[]{:S(2)}) collective-permute-start(f16[320,128]{1,0:T(8,128)(2,1)S(1)} %convert_element_type.43), channel_id=1, source_target_pairs={{0,6},{1,7},{2,4},{3,5},{4,2},{5,3},{6,0},{7,1},{8,14},{9,15},{10,... | collective-permute-start | bytes 245768 | tf_op jit(solution)/shard_map/ppermute | solution.py:298
  26.7 0.9 %add_convert_fusion.1.refs_0_ = bf16[320,128]{1,0:T(8,128)(2,1)S(1)} fusion(f16[320,128]{1,0:T(8,128)(2,1)S(1)} %collective-permute-done.6, f16[320,128]{1,0:T(8,128)(2,1)S(1)} %collective-permute-done.5, f32[320,128]{1,0:T(8,128)S(1)} %get-tuple-element.30, f16[320,128]{1,0:T(8,128)(2,1)} %collective-permute-done.4), kind=kLoop, calls=%fused_computation.1 | loop fusion | flops 286720 | bytes 491520 | tf_op jit(solution)/shard_map/convert_element_type | solution.py:332
  27.6 2.5 %collective-permute-start.9 = (bf16[320,128]{1,0:T(8,128)(2,1)S(1)}, bf16[320,128]{1,0:T(8,128)(2,1)S(1)}, u32[]{:S(2)}, u32[]{:S(2)}) collective-permute-start(bf16[320,128]{1,0:T(8,128)(2,1)S(1)} %add_convert_fusion.1.refs_0_), channel_id=1, source_target_pairs={{0,24},{8,16},{16,8},{24,0},{1,25},{9,17},{17,9},{25,1},{2,26},{10... | collective-permute-start | bytes 245768 | tf_op jit(solution)/shard_map/ppermute | solution.py:298
  30.1 0.5 %collective-permute-start.8 = (bf16[320,128]{1,0:T(8,128)(2,1)S(1)}, bf16[320,128]{1,0:T(8,128)(2,1)S(1)}, u32[]{:S(2)}, u32[]{:S(2)}) collective-permute-start(bf16[320,128]{1,0:T(8,128)(2,1)S(1)} %add_convert_fusion.1.refs_0_), channel_id=1, source_target_pairs={{0,16},{8,24},{16,0},{24,8},{1,17},{9,25},{17,1},{25,9},{2,18},{10... | collective-permute-start | bytes 245768 | tf_op jit(solution)/shard_map/ppermute | solution.py:298
  30.7 1.4 %collective-permute-done.3 = f16[320,128]{1,0:T(8,128)(2,1)S(1)} collective-permute-done((f16[320,128]{1,0:T(8,128)(2,1)S(1)}, f16[320,128]{1,0:T(8,128)(2,1)S(1)}, u32[]{:S(2)}, u32[]{:S(2)}) %collective-permute-start.3) | collective-permute-done | bytes 81952 | tf_op jit(solution)/shard_map/ppermute | solution.py:298
  32.0 1.5 %collective-permute-start.7 = (bf16[320,128]{1,0:T(8,128)(2,1)S(1)}, bf16[320,128]{1,0:T(8,128)(2,1)S(1)}, u32[]{:S(2)}, u32[]{:S(2)}) collective-permute-start(bf16[320,128]{1,0:T(8,128)(2,1)S(1)} %add_convert_fusion.1.refs_0_), channel_id=1, source_target_pairs={{0,8},{8,0},{16,24},{24,16},{1,9},{9,1},{17,25},{25,17},{2,10},{10... | collective-permute-start | bytes 245768 | tf_op jit(solution)/shard_map/ppermute | solution.py:298
  33.5 0.2 constant_dynamic-slice_fusion.legend
  33.7 1.0 %spread_weights.1.weights = bf16[10,352,256]{2,1,0:T(8,128)(2,1)S(1)} custom-call(bf16[80,8,352]{2,1,0:T(8,128)(2,1)S(1)} %constant_dynamic-slice_fusion.legend), custom_call_target="tpu_custom_call" | custom-call | tf_op jit(solution)/shard_map/spread_weights/pallas_call | solution.py:236
  34.8 1.7 %collective-permute-done.7.refs_1_ = bf16[320,128]{1,0:T(8,128)(2,1)S(1)} collective-permute-done((bf16[320,128]{1,0:T(8,128)(2,1)S(1)}, bf16[320,128]{1,0:T(8,128)(2,1)S(1)}, u32[]{:S(2)}, u32[]{:S(2)}) %collective-permute-start.7) | collective-permute-done | bytes 81952 | tf_op jit(solution)/shard_map/ppermute | solution.py:298
  36.4 0.1 add_convert_fusion.refs_0_
  36.5 2.6 %collective-permute-start.12 = (bf16[320,128]{1,0:T(8,128)(2,1)S(1)}, bf16[320,128]{1,0:T(8,128)(2,1)S(1)}, u32[]{:S(2)}, u32[]{:S(2)}) collective-permute-start(bf16[320,128]{1,0:T(8,128)(2,1)S(1)} %add_convert_fusion.refs_0_), channel_id=1, source_target_pairs={{0,24},{8,16},{16,8},{24,0},{1,25},{9,17},{17,9},{25,1},{2,26},{10... | collective-permute-start | bytes 245768 | tf_op jit(solution)/shard_map/ppermute | solution.py:298
  39.1 1.1 %collective-permute-start.11 = (bf16[320,128]{1,0:T(8,128)(2,1)S(1)}, bf16[320,128]{1,0:T(8,128)(2,1)S(1)}, u32[]{:S(2)}, u32[]{:S(2)}) collective-permute-start(bf16[320,128]{1,0:T(8,128)(2,1)S(1)} %add_convert_fusion.refs_0_), channel_id=1, source_target_pairs={{0,16},{8,24},{16,0},{24,8},{1,17},{9,25},{17,1},{25,9},{2,18},{10... | collective-permute-start | bytes 245768 | tf_op jit(solution)/shard_map/ppermute | solution.py:298
  40.2 0.2 collective-permute-start.10
  40.3 3.4 %spectra_part.2.refs_4_ = f32[80,352,128]{2,1,0:T(8,128)} custom-call(bf16[10,352,256]{2,1,0:T(8,128)(2,1)S(1)} %spread_weights.1.weights, bf16[320,128]{1,0:T(8,128)(2,1)S(1)} %add_convert_fusion.1.refs_0_, bf16[320,128]{1,0:T(8,128)(2,1)S(1)} %collective-permute-done.7.refs_1_, bf16[320,128]{1,0:T(8,128)(2,1)S(1)} %collective-permute-done.8.refs_2_, ...), custom_call_target="tpu_custom_call" | custom-call | tf_op jit(solution)/shard_map/spectra_part/pallas_call | solution.py:281
  43.7 0.9 %collective-permute-done.10.refs_1_ = bf16[320,128]{1,0:T(8,128)(2,1)S(1)} collective-permute-done((bf16[320,128]{1,0:T(8,128)(2,1)S(1)}, bf16[320,128]{1,0:T(8,128)(2,1)S(1)}, u32[]{:S(2)}, u32[]{:S(2)}) %collective-permute-start.10) | collective-permute-done | bytes 81952 | tf_op jit(solution)/shard_map/ppermute | solution.py:298
  44.6 3.4 %spectra_part.3 = f32[80,352,128]{2,1,0:T(8,128)} custom-call(bf16[10,352,256]{2,1,0:T(8,128)(2,1)S(1)} %spread_weights.1.weights, bf16[320,128]{1,0:T(8,128)(2,1)S(1)} %add_convert_fusion.refs_0_, bf16[320,128]{1,0:T(8,128)(2,1)S(1)} %collective-permute-done.10.refs_1_, ...), custom_call_target="tpu_custom_call", output_to_operand_aliasing={{}: (5, {})} | custom-call | tf_op jit(solution)/shard_map/spectra_part/pallas_call | solution.py:281
  (25 shorter events, 0.1 us)
Async XLA Ops:
  0.0 33.5 %copy-start = (bf16[80,8,1408]{2,1,0:T(8,128)(2,1)S(1)}, bf16[80,8,1408]{2,1,0:T(8,128)(2,1)}, u32[]{:S(2)}) copy-start(bf16[80,8,1408]{2,1,0:T(8,128)(2,1)} %param.5) | copy-start | bytes 5406724
  0.0 3.7 %collective-permute-start = (f32[1288,128]{1,0:T(8,128)}, f32[1288,128]{1,0:T(8,128)S(1)}, u32[]{:S(2)}, u32[]{:S(2)}) collective-permute-start(f32[1288,128]{1,0:T(8,128)} %bitcast.3), channel_id=1, source_target_pairs={{0,1},{1,0},{2,3},{3,2},{4,5},{5,4},{6,7},{7,6},{8,9},{9,8},{10,11... | collective-permute-start | bytes 1978376 | tf_op jit(solution)/shard_map/ppermute | solution.py:309
  0.5 1.2 %copy-start.5 = (f32[2,644,128]{2,0,1:T(2,128)S(1)}, f32[2,644,128]{2,0,1:T(2,128)}, u32[]{:S(2)}) copy-start(f32[2,644,128]{2,0,1:T(2,128)} %param.3) | copy-start | bytes 1978372
  1.6 0.7 %copy-start.6 = (s32[2]{0:T(128)S(1)}, s32[2]{0:T(128)}, u32[]{:S(2)}) copy-start(s32[2]{0:T(128)} %row_points.5) | copy-start | bytes 28
  3.7 12.1 %copy-start.7 = (s32[2]{0:T(128)S(1)}, s32[2]{0:T(128)}, u32[]{:S(2)}) copy-start(s32[2]{0:T(128)} %row_points.5) | copy-start | bytes 28
  8.5 0.9 %copy-start.1 = (bf16[2,768,256]{2,1,0:T(8,128)(2,1)}, bf16[2,768,256]{2,1,0:T(8,128)(2,1)S(1)}, u32[]{:S(2)}) copy-start(bf16[2,768,256]{2,1,0:T(8,128)(2,1)S(1)} %get-tuple-element.24.mine) | copy-start | bytes 2359300
  9.4 0.9 %copy-start.3 = (bf16[2,768,256]{2,1,0:T(8,128)(2,1)}, bf16[2,768,256]{2,1,0:T(8,128)(2,1)S(1)}, u32[]{:S(2)}) copy-start(bf16[2,768,256]{2,1,0:T(8,128)(2,1)S(1)} %get-tuple-element.26.theirs) | copy-start | bytes 2359300
  10.3 16.4 %collective-permute-start.6 = (f16[320,128]{1,0:T(8,128)(2,1)S(1)}, f16[320,128]{1,0:T(8,128)(2,1)S(1)}, u32[]{:S(2)}, u32[]{:S(2)}) collective-permute-start(f16[320,128]{1,0:T(8,128)(2,1)S(1)} %convert_element_type.49), channel_id=1, source_target_pairs={{0,4},{1,5},{2,6},{3,7},{4,0},{5,1},{6,2},{7,3},{8,12},{9,13},{10,... | collective-permute-start | bytes 245768 | tf_op jit(solution)/shard_map/ppermute | solution.py:298
  14.0 12.7 %collective-permute-start.5 = (f16[320,128]{1,0:T(8,128)(2,1)S(1)}, f16[320,128]{1,0:T(8,128)(2,1)S(1)}, u32[]{:S(2)}, u32[]{:S(2)}) collective-permute-start(f16[320,128]{1,0:T(8,128)(2,1)S(1)} %convert_element_type.47), channel_id=1, source_target_pairs={{0,6},{1,7},{2,4},{3,5},{4,2},{5,3},{6,0},{7,1},{8,14},{9,15},{10,... | collective-permute-start | bytes 245768 | tf_op jit(solution)/shard_map/ppermute | solution.py:298
  15.4 11.2 %collective-permute-start.4 = (f16[320,128]{1,0:T(8,128)(2,1)S(1)}, f16[320,128]{1,0:T(8,128)(2,1)}, u32[]{:S(2)}, u32[]{:S(2)}) collective-permute-start(f16[320,128]{1,0:T(8,128)(2,1)S(1)} %convert_element_type.45), channel_id=1, source_target_pairs={{0,2},{1,3},{2,0},{3,1},{4,6},{5,7},{6,4},{7,5},{8,10},{9,11},{10,... | collective-permute-start | bytes 245768 | tf_op jit(solution)/shard_map/ppermute | solution.py:298
  15.7 1.1 %copy-start.2 = (bf16[2,768,256]{2,1,0:T(8,128)(2,1)S(1)}, bf16[2,768,256]{2,1,0:T(8,128)(2,1)}, u32[]{:S(2)}) copy-start(bf16[2,768,256]{2,1,0:T(8,128)(2,1)} %copy-done.1) | copy-start | bytes 2359300
  16.9 1.1 %copy-start.4 = (bf16[2,768,256]{2,1,0:T(8,128)(2,1)S(1)}, bf16[2,768,256]{2,1,0:T(8,128)(2,1)}, u32[]{:S(2)}) copy-start(bf16[2,768,256]{2,1,0:T(8,128)(2,1)} %copy-done.3) | copy-start | bytes 2359300
  22.5 9.5 %collective-permute-start.3 = (f16[320,128]{1,0:T(8,128)(2,1)S(1)}, f16[320,128]{1,0:T(8,128)(2,1)S(1)}, u32[]{:S(2)}, u32[]{:S(2)}) collective-permute-start(f16[320,128]{1,0:T(8,128)(2,1)S(1)} %convert_element_type.44), channel_id=1, source_target_pairs={{0,4},{1,5},{2,6},{3,7},{4,0},{5,1},{6,2},{7,3},{8,12},{9,13},{10,... | collective-permute-start | bytes 245768 | tf_op jit(solution)/shard_map/ppermute | solution.py:298
  25.3 9.4 %collective-permute-start.2 = (f16[320,128]{1,0:T(8,128)(2,1)S(1)}, f16[320,128]{1,0:T(8,128)(2,1)S(1)}, u32[]{:S(2)}, u32[]{:S(2)}) collective-permute-start(f16[320,128]{1,0:T(8,128)(2,1)S(1)} %convert_element_type.43), channel_id=1, source_target_pairs={{0,6},{1,7},{2,4},{3,5},{4,2},{5,3},{6,0},{7,1},{8,14},{9,15},{10,... | collective-permute-start | bytes 245768 | tf_op jit(solution)/shard_map/ppermute | solution.py:298
  26.7 8.1 %collective-permute-start.1 = (f16[320,128]{1,0:T(8,128)(2,1)S(1)}, f16[320,128]{1,0:T(8,128)(2,1)S(1)}, u32[]{:S(2)}, u32[]{:S(2)}) collective-permute-start(f16[320,128]{1,0:T(8,128)(2,1)S(1)} %convert_element_type.42), channel_id=1, source_target_pairs={{0,2},{1,3},{2,0},{3,1},{4,6},{5,7},{6,4},{7,5},{8,10},{9,11},{10,... | collective-permute-start | bytes 245768 | tf_op jit(solution)/shard_map/ppermute | solution.py:298
  27.6 7.1 %collective-permute-start.9 = (bf16[320,128]{1,0:T(8,128)(2,1)S(1)}, bf16[320,128]{1,0:T(8,128)(2,1)S(1)}, u32[]{:S(2)}, u32[]{:S(2)}) collective-permute-start(bf16[320,128]{1,0:T(8,128)(2,1)S(1)} %add_convert_fusion.1.refs_0_), channel_id=1, source_target_pairs={{0,24},{8,16},{16,8},{24,0},{1,25},{9,17},{17,9},{25,1},{2,26},{10... | collective-permute-start | bytes 245768 | tf_op jit(solution)/shard_map/ppermute | solution.py:298
  30.1 4.6 %collective-permute-start.8 = (bf16[320,128]{1,0:T(8,128)(2,1)S(1)}, bf16[320,128]{1,0:T(8,128)(2,1)S(1)}, u32[]{:S(2)}, u32[]{:S(2)}) collective-permute-start(bf16[320,128]{1,0:T(8,128)(2,1)S(1)} %add_convert_fusion.1.refs_0_), channel_id=1, source_target_pairs={{0,16},{8,24},{16,0},{24,8},{1,17},{9,25},{17,1},{25,9},{2,18},{10... | collective-permute-start | bytes 245768 | tf_op jit(solution)/shard_map/ppermute | solution.py:298
  32.0 4.4 %collective-permute-start.7 = (bf16[320,128]{1,0:T(8,128)(2,1)S(1)}, bf16[320,128]{1,0:T(8,128)(2,1)S(1)}, u32[]{:S(2)}, u32[]{:S(2)}) collective-permute-start(bf16[320,128]{1,0:T(8,128)(2,1)S(1)} %add_convert_fusion.1.refs_0_), channel_id=1, source_target_pairs={{0,8},{8,0},{16,24},{24,16},{1,9},{9,1},{17,25},{25,17},{2,10},{10... | collective-permute-start | bytes 245768 | tf_op jit(solution)/shard_map/ppermute | solution.py:298
  36.5 7.2 %collective-permute-start.12 = (bf16[320,128]{1,0:T(8,128)(2,1)S(1)}, bf16[320,128]{1,0:T(8,128)(2,1)S(1)}, u32[]{:S(2)}, u32[]{:S(2)}) collective-permute-start(bf16[320,128]{1,0:T(8,128)(2,1)S(1)} %add_convert_fusion.refs_0_), channel_id=1, source_target_pairs={{0,24},{8,16},{16,8},{24,0},{1,25},{9,17},{17,9},{25,1},{2,26},{10... | collective-permute-start | bytes 245768 | tf_op jit(solution)/shard_map/ppermute | solution.py:298
  39.1 4.7 %collective-permute-start.11 = (bf16[320,128]{1,0:T(8,128)(2,1)S(1)}, bf16[320,128]{1,0:T(8,128)(2,1)S(1)}, u32[]{:S(2)}, u32[]{:S(2)}) collective-permute-start(bf16[320,128]{1,0:T(8,128)(2,1)S(1)} %add_convert_fusion.refs_0_), channel_id=1, source_target_pairs={{0,16},{8,24},{16,0},{24,8},{1,17},{9,25},{17,1},{25,9},{2,18},{10... | collective-permute-start | bytes 245768 | tf_op jit(solution)/shard_map/ppermute | solution.py:298
  40.2 4.4 %collective-permute-start.10 = (bf16[320,128]{1,0:T(8,128)(2,1)S(1)}, bf16[320,128]{1,0:T(8,128)(2,1)S(1)}, u32[]{:S(2)}, u32[]{:S(2)}) collective-permute-start(bf16[320,128]{1,0:T(8,128)(2,1)S(1)} %add_convert_fusion.refs_0_), channel_id=1, source_target_pairs={{0,8},{8,0},{16,24},{24,16},{1,9},{9,1},{17,25},{25,17},{2,10},{10... | collective-permute-start | bytes 245768 | tf_op jit(solution)/shard_map/ppermute | solution.py:298

commit v3 on v2

--- a/solution.py
+++ b/solution.py
@@ -13,6 +13,7 @@
 F32 = jnp.float32
 BF16 = jnp.bfloat16
 WIRE = jnp.float16
+VMEM = 16 * 2**20
 
 
 def round_up(value, step):
@@ -55,24 +56,29 @@
     return split(jnp.where(where < length_int, folded * scale, 0.0))
 
 
-def store_values(out, r, raw, start, length_int):
+def store_values(out, r, side, raw, start, length_int):
     points, width = raw.shape
-    out[r, :points, :width], out[r, :points, width:] = prepare_values(raw, start, length_int.astype(F32), length_int)
-    out[r, points:, :] = jnp.zeros((out.shape[1] - points, 2 * width), BF16)
+    depth = out.shape[1] // 3
+    lanes = slice(side * width, (side + 1) * width)
+    high, low = prepare_values(raw, start, length_int.astype(F32), length_int)
+    for part, values in enumerate((high, low, high)):
+        out[r, part * depth:part * depth + points, lanes] = values
+        rest = jnp.zeros((depth - points, width), BF16)
+        out[r, part * depth + points:(part + 1) * depth, lanes] = rest
 
 
 def row_of(block, r, rows):
     return block[pl.ds(r, block.shape[0] // rows, stride=rows), :]
 
 
-def prepare_kernel(peers, pair_count, points, row_points, mine, values, factor):
+def prepare_kernel(peers, pair_count, points, row_points, factor):
     rows, _, tall, depth = factor.shape
     held = round_up(pl.cdiv(pair_count, GROUP), GROUP)
     set_index = lax.axis_index("set")
     start = set_index * points
     beside = (set_index ^ 1) * points - start
     slot = lax.broadcasted_iota(jnp.int32, (1, depth), 1)
-    point = jnp.where(slot < values.shape[1], start + slot, beside)
+    point = jnp.where(slot < round_up(points, 128), start + slot, beside)
     heads = round_up(peers + 1, GROUP)
     sub = lax.broadcasted_iota(jnp.int32, (GROUP + heads + held, 1), 0)
     order = sub - GROUP
@@ -93,68 +99,54 @@
             to = 2 * GROUP + peer * held
             factor[r, 0, to:to + held, :] = base[0]
             factor[r, 1, to:to + held, :] = base[1]
-        store_values(values, r, row_of(mine, r, rows), start, row_points[r])
-
-
-def prepare(row_points, mine, peers, pair_count):
+
+
+def prepare(row_points, points, peers, pair_count):
     rows = row_points.shape[0]
-    points, width = mine.shape[0] // rows, mine.shape[1]
-    depth = round_up(points, 128)
     tall = 2 * GROUP + peers * round_up(pl.cdiv(pair_count, GROUP), GROUP)
-    vmem = pl.BlockSpec(memory_space=pltpu.VMEM)
     return pl.pallas_call(
         functools.partial(prepare_kernel, peers, pair_count, points),
-        out_shape=[
-            jax.ShapeDtypeStruct((rows, depth, 2 * width), BF16),
-            jax.ShapeDtypeStruct((rows, 2, tall, depth + 128), F32),
-        ],
-        in_specs=[pl.BlockSpec(memory_space=pltpu.SMEM), vmem],
-        out_specs=[vmem, vmem],
-        compiler_params=pltpu.CompilerParams(vmem_limit_bytes=48 * 2**20),
+        out_shape=jax.ShapeDtypeStruct((rows, 2, tall, round_up(points, 128) + 128), F32),
+        in_specs=[pl.BlockSpec(memory_space=pltpu.SMEM)],
+        out_specs=pl.BlockSpec(memory_space=pltpu.VMEM),
+        compiler_params=pltpu.CompilerParams(vmem_limit_bytes=VMEM),
+        cost_estimate=pl.CostEstimate(flops=1 << 22, bytes_accessed=1 << 22, transcendentals=0),
         name="prepare",
-    )(row_points, mine)
-
-
-def fourier_kernel(groups, first_group, peers, pair_count, fresh, row_points, mine, theirs, factor, *refs):
-    outs = refs[:peers]
+    )(row_points)
+
+
+def fourier_kernel(groups, first_group, peers, pair_count, fresh, row_points, factor, *refs):
     table, sums, twist = refs[-3:]
-    rows, depth, double = mine.shape
-    width = double // 2
+    blocks, outs = refs[:1 + fresh], refs[1 + fresh:1 + fresh + peers]
+    rows = table.shape[0]
+    width = outs[0].shape[1]
+    depth = table.shape[2] // 3
     held = round_up(pl.cdiv(pair_count, GROUP), GROUP)
     set_index = lax.axis_index("set")
+    values = refs[1 + fresh + peers] if fresh else blocks[0]
     if fresh:
-        values = refs[peers]
-        points = theirs.shape[0] // rows
-        for r in range(rows):
-            store_values(values, r, row_of(theirs, r, rows), (set_index ^ 1) * points, row_points[r])
-    else:
-        values = theirs
+        points = blocks[0].shape[0] // rows
+        for side, block in enumerate(blocks):
+            for r in range(rows):
+                store_values(values, r, side, row_of(block, r, rows), (set_index ^ side) * points, row_points[r])
     lane = lax.broadcasted_iota(jnp.int32, (1, width), 1)
     north = lane < width // 2
     sub = lax.broadcasted_iota(jnp.int32, (GROUP, 1), 0)
     for r in range(rows):
-
-        def fill(index, carry):
+        near = factor[r, 0, :GROUP, :], factor[r, 1, :GROUP, :]
+        last = factor[r, 0, GROUP:2 * GROUP, :], factor[r, 1, GROUP:2 * GROUP, :]
+        for index in range(peers * groups):
             at = 2 * GROUP + index // groups * held + first_group + index % groups
-            base = factor[r, 0, pl.ds(at, 1), :], factor[r, 1, pl.ds(at, 1), :]
-            first = rotate(base, (factor[r, 0, :GROUP, :], factor[r, 1, :GROUP, :]))
-            last = factor[r, 0, GROUP:2 * GROUP, :], factor[r, 1, GROUP:2 * GROUP, :]
+            base = factor[r, 0, at:at + 1, :], factor[r, 1, at:at + 1, :]
+            first = rotate(base, near)
             second = rotate(last, (first[0], -first[1]))
             block = jnp.concatenate([*first, *second], axis=0)
             high, low = split(block[:, :depth])
-            start = pl.multiple_of(index * 4 * GROUP, 4 * GROUP)
-            table[0, pl.ds(start, 4 * GROUP), :] = high
-            table[1, pl.ds(start, 4 * GROUP), :] = low
-            twist[r, pl.ds(start, 4 * GROUP), :] = block[:, depth:]
-            return carry
-
-        lax.fori_loop(0, peers * groups, fill, 0, unroll=2)
-        own = jnp.dot(table[0], mine[r], preferred_element_type=F32)
-        other = jnp.dot(table[0], values[r], preferred_element_type=F32)
-        both = jnp.concatenate([mine[r, :, :width], values[r, :, :width]], axis=1)
-        rest = jnp.dot(table[1], both, preferred_element_type=F32)
-        sums[r, :, :width] = own[:, :width] + own[:, width:] + rest[:, :width]
-        sums[r, :, width:] = other[:, :width] + other[:, width:] + rest[:, width:]
+            lines = slice(index * 4 * GROUP, (index + 1) * 4 * GROUP)
+            for part, piece in enumerate((high, high, low)):
+                table[r, lines, part * depth:(part + 1) * depth] = piece
+            twist[r, lines, :] = block[:, depth:]
+        sums[r] = jnp.dot(table[r], values[r], preferred_element_type=F32)
     for peer in range(peers):
         for g in range(groups):
             base = (set_index ^ (2 * peer)) * pair_count + (first_group + g) * GROUP
@@ -176,28 +168,29 @@
                         outs[peer][to:to + GROUP, :] = jnp.where(usable, block, 0.0)
 
 
-def fourier_sums(row_points, mine, theirs, factor, groups, first_group, peers, pair_count):
-    rows, depth, double = mine.shape
-    width = double // 2
-    fresh = theirs.ndim == 2
+def fourier_sums(row_points, factor, blocks, groups, first_group, peers, pair_count):
+    rows = row_points.shape[0]
+    depth = factor.shape[3] - 128
+    fresh = len(blocks) > 1
+    width = blocks[0].shape[-1] // (1 if fresh else 2)
     out_rows = groups * 4 * rows * GROUP
     tall = peers * groups * 4 * GROUP
     vmem = pl.BlockSpec(memory_space=pltpu.VMEM)
     out_shape = [jax.ShapeDtypeStruct((out_rows, width), F32)] * peers
-    out_shape += [jax.ShapeDtypeStruct(mine.shape, BF16)] if fresh else []
+    out_shape += [jax.ShapeDtypeStruct((rows, 3 * depth, 2 * width), BF16)] if fresh else []
     return pl.pallas_call(
         functools.partial(fourier_kernel, groups, first_group, peers, pair_count, fresh),
         out_shape=out_shape,
-        in_specs=[pl.BlockSpec(memory_space=pltpu.SMEM), vmem, vmem, vmem],
+        in_specs=[pl.BlockSpec(memory_space=pltpu.SMEM), vmem] + [vmem] * len(blocks),
         out_specs=[vmem] * len(out_shape),
         scratch_shapes=[
-            pltpu.VMEM((2, tall, depth), BF16),
-            pltpu.VMEM((rows, tall, double), F32),
+            pltpu.VMEM((rows, tall, 3 * depth), BF16),
+            pltpu.VMEM((rows, tall, 2 * width), F32),
             pltpu.VMEM((rows, tall, 128), F32),
         ],
-        compiler_params=pltpu.CompilerParams(vmem_limit_bytes=48 * 2**20),
+        compiler_params=pltpu.CompilerParams(vmem_limit_bytes=VMEM),
         name="fourier_sums",
-    )(row_points, mine, theirs, factor)
+    )(row_points, factor, *blocks)
 
 
 def weights_kernel(rows, bands, legend, out):
@@ -238,7 +231,7 @@
         out_shape=jax.ShapeDtypeStruct((groups, slots, bands * 4 * rows * GROUP), BF16),
         in_specs=[vmem],
         out_specs=vmem,
-        compiler_params=pltpu.CompilerParams(vmem_limit_bytes=48 * 2**20),
+        compiler_params=pltpu.CompilerParams(vmem_limit_bytes=VMEM),
         name="spread_weights",
     )(legend)
 
@@ -285,7 +278,7 @@
         out_specs=anywhere,
         input_output_aliases={1 + bands: 0} if previous else {},
         scratch_shapes=[pltpu.VMEM((pairs, slots, width), F32), pltpu.SemaphoreType.DMA((pairs // 2,))],
-        compiler_params=pltpu.CompilerParams(vmem_limit_bytes=48 * 2**20),
+        compiler_params=pltpu.CompilerParams(vmem_limit_bytes=VMEM),
         name="spectra_part",
     )(weights, *held, *previous)
 
@@ -307,7 +300,8 @@
     peers = set_size // 2
     flat = grid.transpose(1, 0, 2).reshape(points * rows, width)
     theirs = lax.ppermute(flat, "set", swap("set", set_size, 1))
-    mine, factor = prepare(row_points, flat, peers, pair_count)
+    factor = prepare(row_points, points, peers, pair_count)
+    blocks = [flat, theirs]
     legend = lax.dynamic_slice_in_dim(legendre, lax.axis_index("band") * slots, slots, 2)
     weights = spread_weights(legend, rows, band_size)
     all_groups = pl.cdiv(pair_count, GROUP)
@@ -318,9 +312,9 @@
     gathered = []
     partial = []
     for first_group, groups in chunks:
-        parts = list(fourier_sums(row_points, mine, theirs, factor, groups, first_group, peers, pair_count))
+        parts = list(fourier_sums(row_points, factor, blocks, groups, first_group, peers, pair_count))
         if not partial:
-            theirs = parts.pop()
+            blocks = [parts.pop()]
         partial.append(parts)
     for parts in partial:
         arrived = exchange([parts[k].astype(WIRE) for k in steps], "set", [2 * k for k in steps])

time: 48.2 us -> 42.5 us (0.88)
  Pallas kernels: 18.3 us -> 14.4 us
  waiting for transfers between devices: 3.96 us -> 2.66 us
  local copies, waits for them, and re-layouts: 6.1 us -> 5.14 us
    pallas_call x2, Pallas kernels: 9.21 us -> 5.6 us  [fourier_sums(): pl.pallas_call(functools.partial(fourier_kernel, groups, first_group, pee...]
    ppermute x12, waiting for transfers between devices: 3.96 us -> 2.55 us  [exchange(): lax.ppermute(part, axis, swap(axis, lax.axis_size(axis), step))]
    unnamed x16 -> x12, local copies, waits for them, and re-layouts: 5.87 us -> 4.9 us
  transfers between devices with their start and end apart: 13 -> 13, of which waited for: 3 -> 5; matrix products, arithmetic and copies ran while one was open for 3% -> 3% of each run, Pallas kernels for 21% -> 19%
where the time goes in v3:
time: 42.5 us; the launch traced here: 42.2 us
  starting transfers between devices  18.8 us (44%)
  Pallas kernels  14.4 us (34%)
  local copies, waits for them, and re-layouts  5.14 us (12%)
  waiting for transfers between devices  2.66 us (6%)
  other arithmetic  1.08 us (3%)
    ppermute x12, starting transfers between devices, exchange(): lax.ppermute(part, axis, swap(axis, lax.axis_size(axis), step))  18.4 us
    pallas_call x2, Pallas kernels, spectra_part(): pl.pallas_call(functools.partial(spectra_kernel, bands, first_group, pair...  6.71 us
    pallas_call x2, Pallas kernels, fourier_sums(): pl.pallas_call(functools.partial(fourier_kernel, groups, first_group, pee...  5.6 us
    unnamed x12, local copies, waits for them, and re-layouts  4.9 us
    ppermute x12, waiting for transfers between devices, exchange(): lax.ppermute(part, axis, swap(axis, lax.axis_size(axis), step))  2.55 us
    pallas_call x1, Pallas kernels, prepare(): pl.pallas_call(functools.partial(prepare_kernel, peers, pair_count, point...  1.09 us
    convert_element_type x2, other arithmetic, shards(): rounded = total.astype(BF16)  0.99 us
    pallas_call x1, Pallas kernels, spread_weights(): pl.pallas_call(functools.partial(weights_kernel, rows, bands), out_shape=...  0.97 us
  transfers between devices with their start and end apart: 13, of which 5 were waited for; matrix products, arithmetic and copies ran while one was open for 3% of the time, Pallas kernels for 19%

profile of v3, /device:TPU:0, one launch (start us, length us, event | category | flops | bytes accessed | tf_op | source)
XLA Modules:
  0.0 42.2 jit_solution(18390995379800408647)
XLA Ops:
  0.0 0.5 %collective-permute-start = (f32[1288,128]{1,0:T(8,128)}, f32[1288,128]{1,0:T(8,128)S(1)}, u32[]{:S(2)}, u32[]{:S(2)}) collective-permute-start(f32[1288,128]{1,0:T(8,128)} %bitcast.3), channel_id=1, source_target_pairs={{0,1},{1,0},{2,3},{3,2},{4,5},{5,4},{6,7},{7,6},{8,9},{9,8},{10,11... | collective-permute-start | bytes 1978376 | tf_op jit(solution)/shard_map/ppermute | solution.py:302
  0.5 0.7 %copy-done.4 = s32[2]{0:T(128)S(1)} copy-done((s32[2]{0:T(128)S(1)}, s32[2]{0:T(128)}, u32[]{:S(2)}) %copy-start.4) | copy-done | bytes 32
  1.2 1.1 %prepare.1.factor = f32[2,2,80,896]{3,2,1,0:T(8,128)S(1)} custom-call(s32[2]{0:T(128)S(1)} %copy-done.4), custom_call_target="tpu_custom_call" | custom-call | flops 4194304 | bytes 4194304 | tf_op jit(solution)/shard_map/prepare/pallas_call | solution.py:107
  2.3 0.1 collective-permute-done.refs_1_
  2.4 1.1 %copy-done.3 = f32[2,644,128]{2,0,1:T(2,128)S(1)} copy-done((f32[2,644,128]{2,0,1:T(2,128)S(1)}, f32[2,644,128]{2,0,1:T(2,128)}, u32[]{:S(2)}) %copy-start.3) | copy-done | bytes 659480
  3.5 3.2 %fourier_sums.2 = (f32[320,128]{1,0:T(8,128)S(1)}, f32[320,128]{1,0:T(8,128)S(1)}, f32[320,128]{1,0:T(8,128)S(1)}, f32[320,128]{1,0:T(8,128)S(1)}, bf16[2,2304,256]{2,1,0:T(8,128)(2,1)S(1)}) custom-call(s32[2]{0:T(128)S(1)} %copy-done.4, f32[2,2,80,896]{3,2,1,0:T(8,128)S(1)} %prepare.1.factor, f32[1288,128]{1,0:T(8,128)S(1)} %bitcast.4, ...), custom_call_target="tpu_custom_call" | custom-call | tf_op jit(solution)/shard_map/fourier_sums/pallas_call | solution.py:181
  6.7 0.0 copy-start.1
  6.7 1.4 %copy-done.1 = bf16[2,2304,256]{2,1,0:T(8,128)(2,1)} copy-done((bf16[2,2304,256]{2,1,0:T(8,128)(2,1)}, bf16[2,2304,256]{2,1,0:T(8,128)(2,1)S(1)}, u32[]{:S(2)}) %copy-start.1) | copy-done | bytes 2359320
  8.1 4.0 %collective-permute-start.6 = (f16[320,128]{1,0:T(8,128)(2,1)S(1)}, f16[320,128]{1,0:T(8,128)(2,1)S(1)}, u32[]{:S(2)}, u32[]{:S(2)}) collective-permute-start(f16[320,128]{1,0:T(8,128)(2,1)S(1)} %convert_element_type.49), channel_id=1, source_target_pairs={{0,4},{1,5},{2,6},{3,7},{4,0},{5,1},{6,2},{7,3},{8,12},{9,13},{10,... | collective-permute-start | bytes 245768 | tf_op jit(solution)/shard_map/ppermute | solution.py:291
  12.1 1.4 %collective-permute-start.5 = (f16[320,128]{1,0:T(8,128)(2,1)S(1)}, f16[320,128]{1,0:T(8,128)(2,1)S(1)}, u32[]{:S(2)}, u32[]{:S(2)}) collective-permute-start(f16[320,128]{1,0:T(8,128)(2,1)S(1)} %convert_element_type.47), channel_id=1, source_target_pairs={{0,6},{1,7},{2,4},{3,5},{4,2},{5,3},{6,0},{7,1},{8,14},{9,15},{10,... | collective-permute-start | bytes 245768 | tf_op jit(solution)/shard_map/ppermute | solution.py:291
  13.6 0.3 collective-permute-start.4
  13.9 1.7 %copy-done.2 = bf16[2,2304,256]{2,1,0:T(8,128)(2,1)S(1)} copy-done((bf16[2,2304,256]{2,1,0:T(8,128)(2,1)S(1)}, bf16[2,2304,256]{2,1,0:T(8,128)(2,1)}, u32[]{:S(2)}) %copy-start.2) | copy-done | bytes 2359320
  15.5 2.4 %fourier_sums.3 = (f32[320,128]{1,0:T(8,128)S(1)}, f32[320,128]{1,0:T(8,128)S(1)}, f32[320,128]{1,0:T(8,128)S(1)}, f32[320,128]{1,0:T(8,128)S(1)}) custom-call(s32[2]{0:T(128)S(1)} %copy-done.5, f32[2,2,80,896]{3,2,1,0:T(8,128)S(1)} %prepare.1.factor, bf16[2,2304,256]{2,1,0:T(8,128)(2,1)S(1)} %copy-done.2), custom_call_target="tpu_custom_call" | custom-call | tf_op jit(solution)/shard_map/fourier_sums/pallas_call | solution.py:181
  18.0 2.8 %collective-permute-start.3 = (f16[320,128]{1,0:T(8,128)(2,1)S(1)}, f16[320,128]{1,0:T(8,128)(2,1)S(1)}, u32[]{:S(2)}, u32[]{:S(2)}) collective-permute-start(f16[320,128]{1,0:T(8,128)(2,1)S(1)} %convert_element_type.44), channel_id=1, source_target_pairs={{0,4},{1,5},{2,6},{3,7},{4,0},{5,1},{6,2},{7,3},{8,12},{9,13},{10,... | collective-permute-start | bytes 245768 | tf_op jit(solution)/shard_map/ppermute | solution.py:291
  20.8 1.3 %collective-permute-start.2 = (f16[320,128]{1,0:T(8,128)(2,1)S(1)}, f16[320,128]{1,0:T(8,128)(2,1)S(1)}, u32[]{:S(2)}, u32[]{:S(2)}) collective-permute-start(f16[320,128]{1,0:T(8,128)(2,1)S(1)} %convert_element_type.43), channel_id=1, source_target_pairs={{0,6},{1,7},{2,4},{3,5},{4,2},{5,3},{6,0},{7,1},{8,14},{9,15},{10,... | collective-permute-start | bytes 245768 | tf_op jit(solution)/shard_map/ppermute | solution.py:291
  22.2 0.0 collective-permute-done.4
  22.2 0.9 %add_convert_fusion.1.refs_0_ = bf16[320,128]{1,0:T(8,128)(2,1)S(1)} fusion(f16[320,128]{1,0:T(8,128)(2,1)S(1)} %collective-permute-done.6, f16[320,128]{1,0:T(8,128)(2,1)S(1)} %collective-permute-done.5, f32[320,128]{1,0:T(8,128)S(1)} %get-tuple-element.26, f16[320,128]{1,0:T(8,128)(2,1)} %collective-permute-done.4), kind=kLoop, calls=%fused_computation.1 | loop fusion | flops 286720 | bytes 491520 | tf_op jit(solution)/shard_map/convert_element_type | solution.py:326
  23.2 2.5 %collective-permute-start.9 = (bf16[320,128]{1,0:T(8,128)(2,1)S(1)}, bf16[320,128]{1,0:T(8,128)(2,1)S(1)}, u32[]{:S(2)}, u32[]{:S(2)}) collective-permute-start(bf16[320,128]{1,0:T(8,128)(2,1)S(1)} %add_convert_fusion.1.refs_0_), channel_id=1, source_target_pairs={{0,24},{8,16},{16,8},{24,0},{1,25},{9,17},{17,9},{25,1},{2,26},{10... | collective-permute-start | bytes 245768 | tf_op jit(solution)/shard_map/ppermute | solution.py:291
  25.7 0.5 %collective-permute-start.8 = (bf16[320,128]{1,0:T(8,128)(2,1)S(1)}, bf16[320,128]{1,0:T(8,128)(2,1)S(1)}, u32[]{:S(2)}, u32[]{:S(2)}) collective-permute-start(bf16[320,128]{1,0:T(8,128)(2,1)S(1)} %add_convert_fusion.1.refs_0_), channel_id=1, source_target_pairs={{0,16},{8,24},{16,0},{24,8},{1,17},{9,25},{17,1},{25,9},{2,18},{10... | collective-permute-start | bytes 245768 | tf_op jit(solution)/shard_map/ppermute | solution.py:291
  26.2 0.4 collective-permute-done.3
  26.6 1.5 %collective-permute-start.7 = (bf16[320,128]{1,0:T(8,128)(2,1)S(1)}, bf16[320,128]{1,0:T(8,128)(2,1)S(1)}, u32[]{:S(2)}, u32[]{:S(2)}) collective-permute-start(bf16[320,128]{1,0:T(8,128)(2,1)S(1)} %add_convert_fusion.1.refs_0_), channel_id=1, source_target_pairs={{0,8},{8,0},{16,24},{24,16},{1,9},{9,1},{17,25},{25,17},{2,10},{10... | collective-permute-start | bytes 245768 | tf_op jit(solution)/shard_map/ppermute | solution.py:291
  28.1 0.2 constant_dynamic-slice_fusion.legend
  28.3 1.0 %spread_weights.1.weights = bf16[10,352,256]{2,1,0:T(8,128)(2,1)S(1)} custom-call(bf16[80,8,352]{2,1,0:T(8,128)(2,1)S(1)} %constant_dynamic-slice_fusion.legend), custom_call_target="tpu_custom_call" | custom-call | tf_op jit(solution)/shard_map/spread_weights/pallas_call | solution.py:229
  29.3 0.0 collective-permute-done.1
  29.3 0.8 %collective-permute-done.8.refs_2_ = bf16[320,128]{1,0:T(8,128)(2,1)S(1)} collective-permute-done((bf16[320,128]{1,0:T(8,128)(2,1)S(1)}, bf16[320,128]{1,0:T(8,128)(2,1)S(1)}, u32[]{:S(2)}, u32[]{:S(2)}) %collective-permute-start.8) | collective-permute-done | bytes 81952 | tf_op jit(solution)/shard_map/ppermute | solution.py:291
  30.1 0.9 %collective-permute-done.7.refs_1_ = bf16[320,128]{1,0:T(8,128)(2,1)S(1)} collective-permute-done((bf16[320,128]{1,0:T(8,128)(2,1)S(1)}, bf16[320,128]{1,0:T(8,128)(2,1)S(1)}, u32[]{:S(2)}, u32[]{:S(2)}) %collective-permute-start.7) | collective-permute-done | bytes 81952 | tf_op jit(solution)/shard_map/ppermute | solution.py:291
  31.0 0.1 add_convert_fusion.refs_0_
  31.1 3.3 %collective-permute-start.12 = (bf16[320,128]{1,0:T(8,128)(2,1)S(1)}, bf16[320,128]{1,0:T(8,128)(2,1)S(1)}, u32[]{:S(2)}, u32[]{:S(2)}) collective-permute-start(bf16[320,128]{1,0:T(8,128)(2,1)S(1)} %add_convert_fusion.refs_0_), channel_id=1, source_target_pairs={{0,24},{8,16},{16,8},{24,0},{1,25},{9,17},{17,9},{25,1},{2,26},{10... | collective-permute-start | bytes 245768 | tf_op jit(solution)/shard_map/ppermute | solution.py:291
  34.4 0.6 %collective-permute-start.10 = (bf16[320,128]{1,0:T(8,128)(2,1)S(1)}, bf16[320,128]{1,0:T(8,128)(2,1)S(1)}, u32[]{:S(2)}, u32[]{:S(2)}) collective-permute-start(bf16[320,128]{1,0:T(8,128)(2,1)S(1)} %add_convert_fusion.refs_0_), channel_id=1, source_target_pairs={{0,8},{8,0},{16,24},{24,16},{1,9},{9,1},{17,25},{25,17},{2,10},{10... | collective-permute-start | bytes 245768 | tf_op jit(solution)/shard_map/ppermute | solution.py:291
  35.1 3.4 %spectra_part.2.refs_4_ = f32[80,352,128]{2,1,0:T(8,128)} custom-call(bf16[10,352,256]{2,1,0:T(8,128)(2,1)S(1)} %spread_weights.1.weights, bf16[320,128]{1,0:T(8,128)(2,1)S(1)} %add_convert_fusion.1.refs_0_, bf16[320,128]{1,0:T(8,128)(2,1)S(1)} %collective-permute-done.7.refs_1_, bf16[320,128]{1,0:T(8,128)(2,1)S(1)} %collective-permute-done.8.refs_2_, ...), custom_call_target="tpu_custom_call" | custom-call | tf_op jit(solution)/shard_map/spectra_part/pallas_call | solution.py:274
  38.4 0.4 %collective-permute-done.11.refs_2_ = bf16[320,128]{1,0:T(8,128)(2,1)S(1)} collective-permute-done((bf16[320,128]{1,0:T(8,128)(2,1)S(1)}, bf16[320,128]{1,0:T(8,128)(2,1)S(1)}, u32[]{:S(2)}, u32[]{:S(2)}) %collective-permute-start.11) | collective-permute-done | bytes 81952 | tf_op jit(solution)/shard_map/ppermute | solution.py:291
  38.9 3.4 %spectra_part.3 = f32[80,352,128]{2,1,0:T(8,128)} custom-call(bf16[10,352,256]{2,1,0:T(8,128)(2,1)S(1)} %spread_weights.1.weights, bf16[320,128]{1,0:T(8,128)(2,1)S(1)} %add_convert_fusion.refs_0_, bf16[320,128]{1,0:T(8,128)(2,1)S(1)} %collective-permute-done.10.refs_1_, ...), custom_call_target="tpu_custom_call", output_to_operand_aliasing={{}: (5, {})} | custom-call | tf_op jit(solution)/shard_map/spectra_part/pallas_call | solution.py:274
  (21 shorter events, 0.1 us)
Async XLA Ops:
  0.0 28.1 %copy-start = (bf16[80,8,1408]{2,1,0:T(8,128)(2,1)S(1)}, bf16[80,8,1408]{2,1,0:T(8,128)(2,1)}, u32[]{:S(2)}) copy-start(bf16[80,8,1408]{2,1,0:T(8,128)(2,1)} %param.5) | copy-start | bytes 5406724
  0.0 2.4 %collective-permute-start = (f32[1288,128]{1,0:T(8,128)}, f32[1288,128]{1,0:T(8,128)S(1)}, u32[]{:S(2)}, u32[]{:S(2)}) collective-permute-start(f32[1288,128]{1,0:T(8,128)} %bitcast.3), channel_id=1, source_target_pairs={{0,1},{1,0},{2,3},{3,2},{4,5},{5,4},{6,7},{7,6},{8,9},{9,8},{10,11... | collective-permute-start | bytes 1978376 | tf_op jit(solution)/shard_map/ppermute | solution.py:302
  0.5 0.7 %copy-start.4 = (s32[2]{0:T(128)S(1)}, s32[2]{0:T(128)}, u32[]{:S(2)}) copy-start(s32[2]{0:T(128)} %row_points.5) | copy-start | bytes 28
  2.4 1.1 %copy-start.3 = (f32[2,644,128]{2,0,1:T(2,128)S(1)}, f32[2,644,128]{2,0,1:T(2,128)}, u32[]{:S(2)}) copy-start(f32[2,644,128]{2,0,1:T(2,128)} %param.3) | copy-start | bytes 1978372
  3.5 10.4 %copy-start.5 = (s32[2]{0:T(128)S(1)}, s32[2]{0:T(128)}, u32[]{:S(2)}) copy-start(s32[2]{0:T(128)} %row_points.5) | copy-start | bytes 28
  6.7 1.4 %copy-start.1 = (bf16[2,2304,256]{2,1,0:T(8,128)(2,1)}, bf16[2,2304,256]{2,1,0:T(8,128)(2,1)S(1)}, u32[]{:S(2)}) copy-start(bf16[2,2304,256]{2,1,0:T(8,128)(2,1)S(1)} %get-tuple-element.22.refs_0_) | copy-start | bytes 7077892
  8.1 14.1 %collective-permute-start.6 = (f16[320,128]{1,0:T(8,128)(2,1)S(1)}, f16[320,128]{1,0:T(8,128)(2,1)S(1)}, u32[]{:S(2)}, u32[]{:S(2)}) collective-permute-start(f16[320,128]{1,0:T(8,128)(2,1)S(1)} %convert_element_type.49), channel_id=1, source_target_pairs={{0,4},{1,5},{2,6},{3,7},{4,0},{5,1},{6,2},{7,3},{8,12},{9,13},{10,... | collective-permute-start | bytes 245768 | tf_op jit(solution)/shard_map/ppermute | solution.py:291
  12.1 10.1 %collective-permute-start.5 = (f16[320,128]{1,0:T(8,128)(2,1)S(1)}, f16[320,128]{1,0:T(8,128)(2,1)S(1)}, u32[]{:S(2)}, u32[]{:S(2)}) collective-permute-start(f16[320,128]{1,0:T(8,128)(2,1)S(1)} %convert_element_type.47), channel_id=1, source_target_pairs={{0,6},{1,7},{2,4},{3,5},{4,2},{5,3},{6,0},{7,1},{8,14},{9,15},{10,... | collective-permute-start | bytes 245768 | tf_op jit(solution)/shard_map/ppermute | solution.py:291
  13.6 8.6 %collective-permute-start.4 = (f16[320,128]{1,0:T(8,128)(2,1)S(1)}, f16[320,128]{1,0:T(8,128)(2,1)}, u32[]{:S(2)}, u32[]{:S(2)}) collective-permute-start(f16[320,128]{1,0:T(8,128)(2,1)S(1)} %convert_element_type.45), channel_id=1, source_target_pairs={{0,2},{1,3},{2,0},{3,1},{4,6},{5,7},{6,4},{7,5},{8,10},{9,11},{10,... | collective-permute-start | bytes 245768 | tf_op jit(solution)/shard_map/ppermute | solution.py:291
  13.9 1.7 %copy-start.2 = (bf16[2,2304,256]{2,1,0:T(8,128)(2,1)S(1)}, bf16[2,2304,256]{2,1,0:T(8,128)(2,1)}, u32[]{:S(2)}) copy-start(bf16[2,2304,256]{2,1,0:T(8,128)(2,1)} %copy-done.1) | copy-start | bytes 7077892
  18.0 8.5 %collective-permute-start.3 = (f16[320,128]{1,0:T(8,128)(2,1)S(1)}, f16[320,128]{1,0:T(8,128)(2,1)S(1)}, u32[]{:S(2)}, u32[]{:S(2)}) collective-permute-start(f16[320,128]{1,0:T(8,128)(2,1)S(1)} %convert_element_type.44), channel_id=1, source_target_pairs={{0,4},{1,5},{2,6},{3,7},{4,0},{5,1},{6,2},{7,3},{8,12},{9,13},{10,... | collective-permute-start | bytes 245768 | tf_op jit(solution)/shard_map/ppermute | solution.py:291
  20.8 8.5 %collective-permute-start.2 = (f16[320,128]{1,0:T(8,128)(2,1)S(1)}, f16[320,128]{1,0:T(8,128)(2,1)S(1)}, u32[]{:S(2)}, u32[]{:S(2)}) collective-permute-start(f16[320,128]{1,0:T(8,128)(2,1)S(1)} %convert_element_type.43), channel_id=1, source_target_pairs={{0,6},{1,7},{2,4},{3,5},{4,2},{5,3},{6,0},{7,1},{8,14},{9,15},{10,... | collective-permute-start | bytes 245768 | tf_op jit(solution)/shard_map/ppermute | solution.py:291
  22.2 7.1 %collective-permute-start.1 = (f16[320,128]{1,0:T(8,128)(2,1)S(1)}, f16[320,128]{1,0:T(8,128)(2,1)S(1)}, u32[]{:S(2)}, u32[]{:S(2)}) collective-permute-start(f16[320,128]{1,0:T(8,128)(2,1)S(1)} %convert_element_type.42), channel_id=1, source_target_pairs={{0,2},{1,3},{2,0},{3,1},{4,6},{5,7},{6,4},{7,5},{8,10},{9,11},{10,... | collective-permute-start | bytes 245768 | tf_op jit(solution)/shard_map/ppermute | solution.py:291
  23.2 6.2 %collective-permute-start.9 = (bf16[320,128]{1,0:T(8,128)(2,1)S(1)}, bf16[320,128]{1,0:T(8,128)(2,1)S(1)}, u32[]{:S(2)}, u32[]{:S(2)}) collective-permute-start(bf16[320,128]{1,0:T(8,128)(2,1)S(1)} %add_convert_fusion.1.refs_0_), channel_id=1, source_target_pairs={{0,24},{8,16},{16,8},{24,0},{1,25},{9,17},{17,9},{25,1},{2,26},{10... | collective-permute-start | bytes 245768 | tf_op jit(solution)/shard_map/ppermute | solution.py:291
  25.7 4.4 %collective-permute-start.8 = (bf16[320,128]{1,0:T(8,128)(2,1)S(1)}, bf16[320,128]{1,0:T(8,128)(2,1)S(1)}, u32[]{:S(2)}, u32[]{:S(2)}) collective-permute-start(bf16[320,128]{1,0:T(8,128)(2,1)S(1)} %add_convert_fusion.1.refs_0_), channel_id=1, source_target_pairs={{0,16},{8,24},{16,0},{24,8},{1,17},{9,25},{17,1},{25,9},{2,18},{10... | collective-permute-start | bytes 245768 | tf_op jit(solution)/shard_map/ppermute | solution.py:291
  26.6 4.4 %collective-permute-start.7 = (bf16[320,128]{1,0:T(8,128)(2,1)S(1)}, bf16[320,128]{1,0:T(8,128)(2,1)S(1)}, u32[]{:S(2)}, u32[]{:S(2)}) collective-permute-start(bf16[320,128]{1,0:T(8,128)(2,1)S(1)} %add_convert_fusion.1.refs_0_), channel_id=1, source_target_pairs={{0,8},{8,0},{16,24},{24,16},{1,9},{9,1},{17,25},{25,17},{2,10},{10... | collective-permute-start | bytes 245768 | tf_op jit(solution)/shard_map/ppermute | solution.py:291
  31.1 7.4 %collective-permute-start.12 = (bf16[320,128]{1,0:T(8,128)(2,1)S(1)}, bf16[320,128]{1,0:T(8,128)(2,1)S(1)}, u32[]{:S(2)}, u32[]{:S(2)}) collective-permute-start(bf16[320,128]{1,0:T(8,128)(2,1)S(1)} %add_convert_fusion.refs_0_), channel_id=1, source_target_pairs={{0,24},{8,16},{16,8},{24,0},{1,25},{9,17},{17,9},{25,1},{2,26},{10... | collective-permute-start | bytes 245768 | tf_op jit(solution)/shard_map/ppermute | solution.py:291
  34.4 4.4 %collective-permute-start.11 = (bf16[320,128]{1,0:T(8,128)(2,1)S(1)}, bf16[320,128]{1,0:T(8,128)(2,1)S(1)}, u32[]{:S(2)}, u32[]{:S(2)}) collective-permute-start(bf16[320,128]{1,0:T(8,128)(2,1)S(1)} %add_convert_fusion.refs_0_), channel_id=1, source_target_pairs={{0,16},{8,24},{16,0},{24,8},{1,17},{9,25},{17,1},{25,9},{2,18},{10... | collective-permute-start | bytes 245768 | tf_op jit(solution)/shard_map/ppermute | solution.py:291
  34.4 4.4 %collective-permute-start.10 = (bf16[320,128]{1,0:T(8,128)(2,1)S(1)}, bf16[320,128]{1,0:T(8,128)(2,1)S(1)}, u32[]{:S(2)}, u32[]{:S(2)}) collective-permute-start(bf16[320,128]{1,0:T(8,128)(2,1)S(1)} %add_convert_fusion.refs_0_), channel_id=1, source_target_pairs={{0,8},{8,0},{16,24},{24,16},{1,9},{9,1},{17,25},{25,17},{2,10},{10... | collective-permute-start | bytes 245768 | tf_op jit(solution)/shard_map/ppermute | solution.py:291

commit v4 on v3

--- a/solution.py
+++ b/solution.py
@@ -115,20 +115,18 @@
     )(row_points)
 
 
-def fourier_kernel(groups, first_group, peers, pair_count, fresh, row_points, factor, *refs):
-    table, sums, twist = refs[-3:]
-    blocks, outs = refs[:1 + fresh], refs[1 + fresh:1 + fresh + peers]
+def fourier_kernel(groups, first_group, peers, pair_count, row_points, factor, mine, theirs, *refs):
+    outs = refs[:peers]
+    values, table, sums, twist = refs[peers:]
     rows = table.shape[0]
     width = outs[0].shape[1]
     depth = table.shape[2] // 3
     held = round_up(pl.cdiv(pair_count, GROUP), GROUP)
     set_index = lax.axis_index("set")
-    values = refs[1 + fresh + peers] if fresh else blocks[0]
-    if fresh:
-        points = blocks[0].shape[0] // rows
-        for side, block in enumerate(blocks):
-            for r in range(rows):
-                store_values(values, r, side, row_of(block, r, rows), (set_index ^ side) * points, row_points[r])
+    points = mine.shape[0] // rows
+    for side, block in enumerate((mine, theirs)):
+        for r in range(rows):
+            store_values(values, r, side, row_of(block, r, rows), (set_index ^ side) * points, row_points[r])
     lane = lax.broadcasted_iota(jnp.int32, (1, width), 1)
     north = lane < width // 2
     sub = lax.broadcasted_iota(jnp.int32, (GROUP, 1), 0)
@@ -168,29 +166,27 @@
                         outs[peer][to:to + GROUP, :] = jnp.where(usable, block, 0.0)
 
 
-def fourier_sums(row_points, factor, blocks, groups, first_group, peers, pair_count):
+def fourier_sums(row_points, factor, mine, theirs, groups, first_group, peers, pair_count):
     rows = row_points.shape[0]
     depth = factor.shape[3] - 128
-    fresh = len(blocks) > 1
-    width = blocks[0].shape[-1] // (1 if fresh else 2)
+    width = mine.shape[1]
     out_rows = groups * 4 * rows * GROUP
     tall = peers * groups * 4 * GROUP
     vmem = pl.BlockSpec(memory_space=pltpu.VMEM)
-    out_shape = [jax.ShapeDtypeStruct((out_rows, width), F32)] * peers
-    out_shape += [jax.ShapeDtypeStruct((rows, 3 * depth, 2 * width), BF16)] if fresh else []
     return pl.pallas_call(
-        functools.partial(fourier_kernel, groups, first_group, peers, pair_count, fresh),
-        out_shape=out_shape,
-        in_specs=[pl.BlockSpec(memory_space=pltpu.SMEM), vmem] + [vmem] * len(blocks),
-        out_specs=[vmem] * len(out_shape),
+        functools.partial(fourier_kernel, groups, first_group, peers, pair_count),
+        out_shape=[jax.ShapeDtypeStruct((out_rows, width), F32)] * peers,
+        in_specs=[pl.BlockSpec(memory_space=pltpu.SMEM)] + [vmem] * 3,
+        out_specs=[vmem] * peers,
         scratch_shapes=[
+            pltpu.VMEM((rows, 3 * depth, 2 * width), BF16),
             pltpu.VMEM((rows, tall, 3 * depth), BF16),
             pltpu.VMEM((rows, tall, 2 * width), F32),
             pltpu.VMEM((rows, tall, 128), F32),
         ],
         compiler_params=pltpu.CompilerParams(vmem_limit_bytes=VMEM),
         name="fourier_sums",
-    )(row_points, factor, *blocks)
+    )(row_points, factor, mine, theirs)
 
 
 def weights_kernel(rows, bands, legend, out):
@@ -301,22 +297,18 @@
     flat = grid.transpose(1, 0, 2).reshape(points * rows, width)
     theirs = lax.ppermute(flat, "set", swap("set", set_size, 1))
     factor = prepare(row_points, points, peers, pair_count)
-    blocks = [flat, theirs]
     legend = lax.dynamic_slice_in_dim(legendre, lax.axis_index("band") * slots, slots, 2)
     weights = spread_weights(legend, rows, band_size)
     all_groups = pl.cdiv(pair_count, GROUP)
     cut = (all_groups + 1) // 2
-    out = None
-    steps = list(range(1, peers, 2)) + list(range(2, peers, 2))[::-1]
     chunks = ((0, cut), (cut, all_groups - cut))
     gathered = []
     partial = []
     for first_group, groups in chunks:
-        parts = list(fourier_sums(row_points, factor, blocks, groups, first_group, peers, pair_count))
-        if not partial:
-            blocks = [parts.pop()]
-        partial.append(parts)
+        partial.append(fourier_sums(row_points, factor, flat, theirs, groups, first_group, peers, pair_count))
     for parts in partial:
+        steps = list(range(1, peers))
+        steps = steps[::-1] if gathered else steps[::2] + steps[1::2]
         arrived = exchange([parts[k].astype(WIRE) for k in steps], "set", [2 * k for k in steps])
         if gathered:
             arrived, weights, gathered[0] = lax.optimization_barrier((arrived, weights, gathered[0]))
@@ -326,6 +318,7 @@
         rounded = total.astype(BF16)
         turns = list(range(1, band_size))
         gathered.append([rounded] + exchange([rounded] * len(turns), "band", turns))
+    out = None
     for held, (first_group, groups) in zip(gathered, chunks):
         out = spectra_part(weights, held, out, pair_count, first_group, groups)
     return out

time: 42.5 us -> 41.4 us (0.974)
  starting transfers between devices: 18.8 us -> 17.8 us
  local copies, waits for them, and re-layouts: 5.14 us -> 4.25 us
  Pallas kernels: 14.4 us -> 15 us
    ppermute x12, starting transfers between devices: 18.4 us -> 17.3 us  [exchange(): lax.ppermute(part, axis, swap(axis, lax.axis_size(axis), step))]
    unnamed x12 -> x14, local copies, waits for them, and re-layouts: 4.9 us -> 4.02 us
    pallas_call x2, Pallas kernels: 5.6 us -> 6.25 us  [fourier_sums(): pl.pallas_call(functools.partial(fourier_kernel, groups, first_group, pee...]
  transfers between devices with their start and end apart: 13 -> 13, of which waited for: 5 -> 5; matrix products, arithmetic and copies ran while one was open for 3% -> 3% of each run, Pallas kernels for 19% -> 21%
where the time goes in v4:
time: 41.4 us; the launch traced here: 41.1 us
  starting transfers between devices  17.8 us (43%)
  Pallas kernels  15 us (36%)
  local copies, waits for them, and re-layouts  4.25 us (10%)
  waiting for transfers between devices  2.81 us (7%)
  other arithmetic  1.08 us (3%)
    ppermute x12, starting transfers between devices, exchange(): lax.ppermute(part, axis, swap(axis, lax.axis_size(axis), step))  17.3 us
    pallas_call x2, Pallas kernels, spectra_part(): pl.pallas_call(functools.partial(spectra_kernel, bands, first_group, pair...  6.71 us
    pallas_call x2, Pallas kernels, fourier_sums(): pl.pallas_call(functools.partial(fourier_kernel, groups, first_group, pee...  6.25 us
    unnamed x14, local copies, waits for them, and re-layouts  4.02 us
    ppermute x12, waiting for transfers between devices, exchange(): lax.ppermute(part, axis, swap(axis, lax.axis_size(axis), step))  2.7 us
    pallas_call x1, Pallas kernels, prepare(): pl.pallas_call(functools.partial(prepare_kernel, peers, pair_count, point...  1.09 us
    convert_element_type x2, other arithmetic, shards(): rounded = total.astype(BF16)  0.99 us
    pallas_call x1, Pallas kernels, spread_weights(): pl.pallas_call(functools.partial(weights_kernel, rows, bands), out_shape=...  0.97 us
  transfers between devices with their start and end apart: 13, of which 5 were waited for; matrix products, arithmetic and copies ran while one was open for 3% of the time, Pallas kernels for 21%

profile of v4, /device:TPU:0, one launch (start us, length us, event | category | flops | bytes accessed | tf_op | source)
XLA Modules:
  0.0 41.1 jit_solution(13879507318041740043)
XLA Ops:
  0.0 0.5 %collective-permute-start = (f32[1288,128]{1,0:T(8,128)}, f32[1288,128]{1,0:T(8,128)S(1)}, u32[]{:S(2)}, u32[]{:S(2)}) collective-permute-start(f32[1288,128]{1,0:T(8,128)} %bitcast.3), channel_id=1, source_target_pairs={{0,1},{1,0},{2,3},{3,2},{4,5},{5,4},{6,7},{7,6},{8,9},{9,8},{10,11... | collective-permute-start | bytes 1978376 | tf_op jit(solution)/shard_map/ppermute | solution.py:298
  0.5 0.7 %copy-done.5 = s32[2]{0:T(128)S(1)} copy-done((s32[2]{0:T(128)S(1)}, s32[2]{0:T(128)}, u32[]{:S(2)}) %copy-start.5) | copy-done | bytes 32
  1.2 1.1 %prepare.1.factor = f32[2,2,80,896]{3,2,1,0:T(8,128)S(1)} custom-call(s32[2]{0:T(128)S(1)} %copy-done.5), custom_call_target="tpu_custom_call" | custom-call | flops 4194304 | bytes 4194304 | tf_op jit(solution)/shard_map/prepare/pallas_call | solution.py:107
  2.3 0.1 collective-permute-done.theirs
  2.4 1.1 %copy-done.1 = f32[2,644,128]{2,0,1:T(2,128)S(1)} copy-done((f32[2,644,128]{2,0,1:T(2,128)S(1)}, f32[2,644,128]{2,0,1:T(2,128)}, u32[]{:S(2)}) %copy-start.1) | copy-done | bytes 659480
  3.5 3.1 %fourier_sums.3 = (f32[320,128]{1,0:T(8,128)S(1)}, f32[320,128]{1,0:T(8,128)S(1)}, f32[320,128]{1,0:T(8,128)S(1)}, f32[320,128]{1,0:T(8,128)S(1)}) custom-call(s32[2]{0:T(128)S(1)} %copy-done.5, f32[2,2,80,896]{3,2,1,0:T(8,128)S(1)} %prepare.1.factor, f32[1288,128]{1,0:T(8,128)S(1)} %bitcast.4, f32[1288,128]{1,0:T(8,128)S(1)} %collective-permute-done.theirs), custom_call_target="tpu_custom_call" | custom-call | tf_op jit(solution)/shard_map/fourier_sums/pallas_call | solution.py:176
  6.7 4.0 %collective-permute-start.6 = (f16[320,128]{1,0:T(8,128)(2,1)S(1)}, f16[320,128]{1,0:T(8,128)(2,1)S(1)}, u32[]{:S(2)}, u32[]{:S(2)}) collective-permute-start(f16[320,128]{1,0:T(8,128)(2,1)S(1)} %convert_element_type.49), channel_id=1, source_target_pairs={{0,4},{1,5},{2,6},{3,7},{4,0},{5,1},{6,2},{7,3},{8,12},{9,13},{10,... | collective-permute-start | bytes 245768 | tf_op jit(solution)/shard_map/ppermute | solution.py:287
  10.7 1.4 %collective-permute-start.5 = (f16[320,128]{1,0:T(8,128)(2,1)S(1)}, f16[320,128]{1,0:T(8,128)(2,1)S(1)}, u32[]{:S(2)}, u32[]{:S(2)}) collective-permute-start(f16[320,128]{1,0:T(8,128)(2,1)S(1)} %convert_element_type.47), channel_id=1, source_target_pairs={{0,6},{1,7},{2,4},{3,5},{4,2},{5,3},{6,0},{7,1},{8,14},{9,15},{10,... | collective-permute-start | bytes 245768 | tf_op jit(solution)/shard_map/ppermute | solution.py:287
  12.1 0.3 collective-permute-start.4
  12.4 1.1 %copy-done.2 = f32[2,644,128]{2,0,1:T(2,128)S(1)} copy-done((f32[2,644,128]{2,0,1:T(2,128)S(1)}, f32[2,644,128]{2,0,1:T(2,128)}, u32[]{:S(2)}) %copy-start.2) | copy-done | bytes 659480
  13.5 1.1 %copy-done.4 = f32[1288,128]{1,0:T(8,128)S(1)} copy-done((f32[1288,128]{1,0:T(8,128)S(1)}, f32[1288,128]{1,0:T(8,128)}, u32[]{:S(2)}) %copy-start.4) | copy-done | bytes 659480
  14.6 3.1 %fourier_sums.2 = (f32[320,128]{1,0:T(8,128)S(1)}, f32[320,128]{1,0:T(8,128)S(1)}, f32[320,128]{1,0:T(8,128)S(1)}, f32[320,128]{1,0:T(8,128)S(1)}) custom-call(s32[2]{0:T(128)S(1)} %copy-done.6, f32[2,2,80,896]{3,2,1,0:T(8,128)S(1)} %prepare.1.factor, f32[1288,128]{1,0:T(8,128)S(1)} %bitcast.5, f32[1288,128]{1,0:T(8,128)S(1)} %copy-done.4), custom_call_target="tpu_custom_call" | custom-call | tf_op jit(solution)/shard_map/fourier_sums/pallas_call | solution.py:176
  17.8 1.8 %collective-permute-start.3 = (f16[320,128]{1,0:T(8,128)(2,1)S(1)}, f16[320,128]{1,0:T(8,128)(2,1)S(1)}, u32[]{:S(2)}, u32[]{:S(2)}) collective-permute-start(f16[320,128]{1,0:T(8,128)(2,1)S(1)} %convert_element_type.44), channel_id=1, source_target_pairs={{0,2},{1,3},{2,0},{3,1},{4,6},{5,7},{6,4},{7,5},{8,10},{9,11},{10,... | collective-permute-start | bytes 245768 | tf_op jit(solution)/shard_map/ppermute | solution.py:287
  19.6 1.7 %collective-permute-start.2 = (f16[320,128]{1,0:T(8,128)(2,1)S(1)}, f16[320,128]{1,0:T(8,128)(2,1)S(1)}, u32[]{:S(2)}, u32[]{:S(2)}) collective-permute-start(f16[320,128]{1,0:T(8,128)(2,1)S(1)} %convert_element_type.43), channel_id=1, source_target_pairs={{0,4},{1,5},{2,6},{3,7},{4,0},{5,1},{6,2},{7,3},{8,12},{9,13},{10,... | collective-permute-start | bytes 245768 | tf_op jit(solution)/shard_map/ppermute | solution.py:287
  21.3 0.0 collective-permute-done.6
  21.3 1.0 %collective-permute-start.1 = (f16[320,128]{1,0:T(8,128)(2,1)S(1)}, f16[320,128]{1,0:T(8,128)(2,1)S(1)}, u32[]{:S(2)}, u32[]{:S(2)}) collective-permute-start(f16[320,128]{1,0:T(8,128)(2,1)S(1)} %convert_element_type.42), channel_id=1, source_target_pairs={{0,6},{1,7},{2,4},{3,5},{4,2},{5,3},{6,0},{7,1},{8,14},{9,15},{10,... | collective-permute-start | bytes 245768 | tf_op jit(solution)/shard_map/ppermute | solution.py:287
  22.3 0.0 collective-permute-done.5
  22.3 0.9 %add_convert_fusion.1.refs_0_ = bf16[320,128]{1,0:T(8,128)(2,1)S(1)} fusion(f16[320,128]{1,0:T(8,128)(2,1)S(1)} %collective-permute-done.6, f16[320,128]{1,0:T(8,128)(2,1)S(1)} %collective-permute-done.5, f32[320,128]{1,0:T(8,128)S(1)} %get-tuple-element.24, f16[320,128]{1,0:T(8,128)(2,1)} %collective-permute-done.4), kind=kLoop, calls=%fused_computation.1 | loop fusion | flops 286720 | bytes 491520 | tf_op jit(solution)/shard_map/convert_element_type | solution.py:318
  23.2 2.5 %collective-permute-start.9 = (bf16[320,128]{1,0:T(8,128)(2,1)S(1)}, bf16[320,128]{1,0:T(8,128)(2,1)S(1)}, u32[]{:S(2)}, u32[]{:S(2)}) collective-permute-start(bf16[320,128]{1,0:T(8,128)(2,1)S(1)} %add_convert_fusion.1.refs_0_), channel_id=1, source_target_pairs={{0,24},{8,16},{16,8},{24,0},{1,25},{9,17},{17,9},{25,1},{2,26},{10... | collective-permute-start | bytes 245768 | tf_op jit(solution)/shard_map/ppermute | solution.py:287
  25.7 0.5 %collective-permute-start.8 = (bf16[320,128]{1,0:T(8,128)(2,1)S(1)}, bf16[320,128]{1,0:T(8,128)(2,1)S(1)}, u32[]{:S(2)}, u32[]{:S(2)}) collective-permute-start(bf16[320,128]{1,0:T(8,128)(2,1)S(1)} %add_convert_fusion.1.refs_0_), channel_id=1, source_target_pairs={{0,16},{8,24},{16,0},{24,8},{1,17},{9,25},{17,1},{25,9},{2,18},{10... | collective-permute-start | bytes 245768 | tf_op jit(solution)/shard_map/ppermute | solution.py:287
  26.3 0.5 %collective-permute-start.7 = (bf16[320,128]{1,0:T(8,128)(2,1)S(1)}, bf16[320,128]{1,0:T(8,128)(2,1)S(1)}, u32[]{:S(2)}, u32[]{:S(2)}) collective-permute-start(bf16[320,128]{1,0:T(8,128)(2,1)S(1)} %add_convert_fusion.1.refs_0_), channel_id=1, source_target_pairs={{0,8},{8,0},{16,24},{24,16},{1,9},{9,1},{17,25},{25,17},{2,10},{10... | collective-permute-start | bytes 245768 | tf_op jit(solution)/shard_map/ppermute | solution.py:287
  26.8 0.2 constant_dynamic-slice_fusion.legend
  27.0 1.0 %spread_weights.1.weights = bf16[10,352,256]{2,1,0:T(8,128)(2,1)S(1)} custom-call(bf16[80,8,352]{2,1,0:T(8,128)(2,1)S(1)} %constant_dynamic-slice_fusion.legend), custom_call_target="tpu_custom_call" | custom-call | tf_op jit(solution)/shard_map/spread_weights/pallas_call | solution.py:225
  28.0 0.3 collective-permute-done.2
  28.3 1.0 %collective-permute-done.9.refs_3_ = bf16[320,128]{1,0:T(8,128)(2,1)S(1)} collective-permute-done((bf16[320,128]{1,0:T(8,128)(2,1)S(1)}, bf16[320,128]{1,0:T(8,128)(2,1)S(1)}, u32[]{:S(2)}, u32[]{:S(2)}) %collective-permute-start.9) | collective-permute-done | bytes 81952 | tf_op jit(solution)/shard_map/ppermute | solution.py:287
  29.3 0.9 %collective-permute-done.8.refs_2_ = bf16[320,128]{1,0:T(8,128)(2,1)S(1)} collective-permute-done((bf16[320,128]{1,0:T(8,128)(2,1)S(1)}, bf16[320,128]{1,0:T(8,128)(2,1)S(1)}, u32[]{:S(2)}, u32[]{:S(2)}) %collective-permute-start.8) | collective-permute-done | bytes 81952 | tf_op jit(solution)/shard_map/ppermute | solution.py:287
  30.2 0.5 %collective-permute-done.7.refs_1_ = bf16[320,128]{1,0:T(8,128)(2,1)S(1)} collective-permute-done((bf16[320,128]{1,0:T(8,128)(2,1)S(1)}, bf16[320,128]{1,0:T(8,128)(2,1)S(1)}, u32[]{:S(2)}, u32[]{:S(2)}) %collective-permute-start.7) | collective-permute-done | bytes 81952 | tf_op jit(solution)/shard_map/ppermute | solution.py:287
  30.7 1.6 %collective-permute-start.12 = (bf16[320,128]{1,0:T(8,128)(2,1)S(1)}, bf16[320,128]{1,0:T(8,128)(2,1)S(1)}, u32[]{:S(2)}, u32[]{:S(2)}) collective-permute-start(bf16[320,128]{1,0:T(8,128)(2,1)S(1)} %add_convert_fusion.refs_0_), channel_id=1, source_target_pairs={{0,24},{8,16},{16,8},{24,0},{1,25},{9,17},{17,9},{25,1},{2,26},{10... | collective-permute-start | bytes 245768 | tf_op jit(solution)/shard_map/ppermute | solution.py:287
  32.3 0.5 %collective-permute-start.11 = (bf16[320,128]{1,0:T(8,128)(2,1)S(1)}, bf16[320,128]{1,0:T(8,128)(2,1)S(1)}, u32[]{:S(2)}, u32[]{:S(2)}) collective-permute-start(bf16[320,128]{1,0:T(8,128)(2,1)S(1)} %add_convert_fusion.refs_0_), channel_id=1, source_target_pairs={{0,16},{8,24},{16,0},{24,8},{1,17},{9,25},{17,1},{25,9},{2,18},{10... | collective-permute-start | bytes 245768 | tf_op jit(solution)/shard_map/ppermute | solution.py:287
  32.8 1.5 %collective-permute-start.10 = (bf16[320,128]{1,0:T(8,128)(2,1)S(1)}, bf16[320,128]{1,0:T(8,128)(2,1)S(1)}, u32[]{:S(2)}, u32[]{:S(2)}) collective-permute-start(bf16[320,128]{1,0:T(8,128)(2,1)S(1)} %add_convert_fusion.refs_0_), channel_id=1, source_target_pairs={{0,8},{8,0},{16,24},{24,16},{1,9},{9,1},{17,25},{25,17},{2,10},{10... | collective-permute-start | bytes 245768 | tf_op jit(solution)/shard_map/ppermute | solution.py:287
  34.3 3.4 %spectra_part.2.refs_4_ = f32[80,352,128]{2,1,0:T(8,128)} custom-call(bf16[10,352,256]{2,1,0:T(8,128)(2,1)S(1)} %spread_weights.1.weights, bf16[320,128]{1,0:T(8,128)(2,1)S(1)} %add_convert_fusion.1.refs_0_, bf16[320,128]{1,0:T(8,128)(2,1)S(1)} %collective-permute-done.7.refs_1_, bf16[320,128]{1,0:T(8,128)(2,1)S(1)} %collective-permute-done.8.refs_2_, ...), custom_call_target="tpu_custom_call" | custom-call | tf_op jit(solution)/shard_map/spectra_part/pallas_call | solution.py:270
  37.7 3.4 %spectra_part.3 = f32[80,352,128]{2,1,0:T(8,128)} custom-call(bf16[10,352,256]{2,1,0:T(8,128)(2,1)S(1)} %spread_weights.1.weights, bf16[320,128]{1,0:T(8,128)(2,1)S(1)} %add_convert_fusion.refs_0_, bf16[320,128]{1,0:T(8,128)(2,1)S(1)} %collective-permute-done.10.refs_1_, ...), custom_call_target="tpu_custom_call", output_to_operand_aliasing={{}: (5, {})} | custom-call | tf_op jit(solution)/shard_map/spectra_part/pallas_call | solution.py:270
  (23 shorter events, 0.2 us)
Async XLA Ops:
  0.0 26.8 %copy-start = (bf16[80,8,1408]{2,1,0:T(8,128)(2,1)S(1)}, bf16[80,8,1408]{2,1,0:T(8,128)(2,1)}, u32[]{:S(2)}) copy-start(bf16[80,8,1408]{2,1,0:T(8,128)(2,1)} %param.5) | copy-start | bytes 5406724
  0.0 2.4 %collective-permute-start = (f32[1288,128]{1,0:T(8,128)}, f32[1288,128]{1,0:T(8,128)S(1)}, u32[]{:S(2)}, u32[]{:S(2)}) collective-permute-start(f32[1288,128]{1,0:T(8,128)} %bitcast.3), channel_id=1, source_target_pairs={{0,1},{1,0},{2,3},{3,2},{4,5},{5,4},{6,7},{7,6},{8,9},{9,8},{10,11... | collective-permute-start | bytes 1978376 | tf_op jit(solution)/shard_map/ppermute | solution.py:298
  0.5 0.7 %copy-start.5 = (s32[2]{0:T(128)S(1)}, s32[2]{0:T(128)}, u32[]{:S(2)}) copy-start(s32[2]{0:T(128)} %row_points.5) | copy-start | bytes 28
  2.4 1.1 %copy-start.1 = (f32[2,644,128]{2,0,1:T(2,128)S(1)}, f32[2,644,128]{2,0,1:T(2,128)}, u32[]{:S(2)}) copy-start(f32[2,644,128]{2,0,1:T(2,128)} %param.3) | copy-start | bytes 1978372
  3.5 3.1 %copy-start.3 = (f32[1288,128]{1,0:T(8,128)}, f32[1288,128]{1,0:T(8,128)S(1)}, u32[]{:S(2)}) copy-start(f32[1288,128]{1,0:T(8,128)S(1)} %collective-permute-done.theirs) | copy-start | bytes 1978372
  3.5 9.0 %copy-start.6 = (s32[2]{0:T(128)S(1)}, s32[2]{0:T(128)}, u32[]{:S(2)}) copy-start(s32[2]{0:T(128)} %row_points.5) | copy-start | bytes 28
  6.7 14.6 %collective-permute-start.6 = (f16[320,128]{1,0:T(8,128)(2,1)S(1)}, f16[320,128]{1,0:T(8,128)(2,1)S(1)}, u32[]{:S(2)}, u32[]{:S(2)}) collective-permute-start(f16[320,128]{1,0:T(8,128)(2,1)S(1)} %convert_element_type.49), channel_id=1, source_target_pairs={{0,4},{1,5},{2,6},{3,7},{4,0},{5,1},{6,2},{7,3},{8,12},{9,13},{10,... | collective-permute-start | bytes 245768 | tf_op jit(solution)/shard_map/ppermute | solution.py:287
  10.7 11.6 %collective-permute-start.5 = (f16[320,128]{1,0:T(8,128)(2,1)S(1)}, f16[320,128]{1,0:T(8,128)(2,1)S(1)}, u32[]{:S(2)}, u32[]{:S(2)}) collective-permute-start(f16[320,128]{1,0:T(8,128)(2,1)S(1)} %convert_element_type.47), channel_id=1, source_target_pairs={{0,6},{1,7},{2,4},{3,5},{4,2},{5,3},{6,0},{7,1},{8,14},{9,15},{10,... | collective-permute-start | bytes 245768 | tf_op jit(solution)/shard_map/ppermute | solution.py:287
  12.1 10.2 %collective-permute-start.4 = (f16[320,128]{1,0:T(8,128)(2,1)S(1)}, f16[320,128]{1,0:T(8,128)(2,1)}, u32[]{:S(2)}, u32[]{:S(2)}) collective-permute-start(f16[320,128]{1,0:T(8,128)(2,1)S(1)} %convert_element_type.45), channel_id=1, source_target_pairs={{0,2},{1,3},{2,0},{3,1},{4,6},{5,7},{6,4},{7,5},{8,10},{9,11},{10,... | collective-permute-start | bytes 245768 | tf_op jit(solution)/shard_map/ppermute | solution.py:287
  12.4 1.1 %copy-start.2 = (f32[2,644,128]{2,0,1:T(2,128)S(1)}, f32[2,644,128]{2,0,1:T(2,128)}, u32[]{:S(2)}) copy-start(f32[2,644,128]{2,0,1:T(2,128)} %param.3) | copy-start | bytes 1978372
  13.5 1.1 %copy-start.4 = (f32[1288,128]{1,0:T(8,128)S(1)}, f32[1288,128]{1,0:T(8,128)}, u32[]{:S(2)}) copy-start(f32[1288,128]{1,0:T(8,128)} %copy-done.3) | copy-start | bytes 1978372
  17.8 8.4 %collective-permute-start.3 = (f16[320,128]{1,0:T(8,128)(2,1)S(1)}, f16[320,128]{1,0:T(8,128)(2,1)S(1)}, u32[]{:S(2)}, u32[]{:S(2)}) collective-permute-start(f16[320,128]{1,0:T(8,128)(2,1)S(1)} %convert_element_type.44), channel_id=1, source_target_pairs={{0,2},{1,3},{2,0},{3,1},{4,6},{5,7},{6,4},{7,5},{8,10},{9,11},{10,... | collective-permute-start | bytes 245768 | tf_op jit(solution)/shard_map/ppermute | solution.py:287
  19.6 8.7 %collective-permute-start.2 = (f16[320,128]{1,0:T(8,128)(2,1)S(1)}, f16[320,128]{1,0:T(8,128)(2,1)S(1)}, u32[]{:S(2)}, u32[]{:S(2)}) collective-permute-start(f16[320,128]{1,0:T(8,128)(2,1)S(1)} %convert_element_type.43), channel_id=1, source_target_pairs={{0,4},{1,5},{2,6},{3,7},{4,0},{5,1},{6,2},{7,3},{8,12},{9,13},{10,... | collective-permute-start | bytes 245768 | tf_op jit(solution)/shard_map/ppermute | solution.py:287
  21.3 7.0 %collective-permute-start.1 = (f16[320,128]{1,0:T(8,128)(2,1)S(1)}, f16[320,128]{1,0:T(8,128)(2,1)S(1)}, u32[]{:S(2)}, u32[]{:S(2)}) collective-permute-start(f16[320,128]{1,0:T(8,128)(2,1)S(1)} %convert_element_type.42), channel_id=1, source_target_pairs={{0,6},{1,7},{2,4},{3,5},{4,2},{5,3},{6,0},{7,1},{8,14},{9,15},{10,... | collective-permute-start | bytes 245768 | tf_op jit(solution)/shard_map/ppermute | solution.py:287
  23.2 6.1 %collective-permute-start.9 = (bf16[320,128]{1,0:T(8,128)(2,1)S(1)}, bf16[320,128]{1,0:T(8,128)(2,1)S(1)}, u32[]{:S(2)}, u32[]{:S(2)}) collective-permute-start(bf16[320,128]{1,0:T(8,128)(2,1)S(1)} %add_convert_fusion.1.refs_0_), channel_id=1, source_target_pairs={{0,24},{8,16},{16,8},{24,0},{1,25},{9,17},{17,9},{25,1},{2,26},{10... | collective-permute-start | bytes 245768 | tf_op jit(solution)/shard_map/ppermute | solution.py:287
  25.7 4.4 %collective-permute-start.8 = (bf16[320,128]{1,0:T(8,128)(2,1)S(1)}, bf16[320,128]{1,0:T(8,128)(2,1)S(1)}, u32[]{:S(2)}, u32[]{:S(2)}) collective-permute-start(bf16[320,128]{1,0:T(8,128)(2,1)S(1)} %add_convert_fusion.1.refs_0_), channel_id=1, source_target_pairs={{0,16},{8,24},{16,0},{24,8},{1,17},{9,25},{17,1},{25,9},{2,18},{10... | collective-permute-start | bytes 245768 | tf_op jit(solution)/shard_map/ppermute | solution.py:287
  26.3 4.4 %collective-permute-start.7 = (bf16[320,128]{1,0:T(8,128)(2,1)S(1)}, bf16[320,128]{1,0:T(8,128)(2,1)S(1)}, u32[]{:S(2)}, u32[]{:S(2)}) collective-permute-start(bf16[320,128]{1,0:T(8,128)(2,1)S(1)} %add_convert_fusion.1.refs_0_), channel_id=1, source_target_pairs={{0,8},{8,0},{16,24},{24,16},{1,9},{9,1},{17,25},{25,17},{2,10},{10... | collective-permute-start | bytes 245768 | tf_op jit(solution)/shard_map/ppermute | solution.py:287
  30.7 6.9 %collective-permute-start.12 = (bf16[320,128]{1,0:T(8,128)(2,1)S(1)}, bf16[320,128]{1,0:T(8,128)(2,1)S(1)}, u32[]{:S(2)}, u32[]{:S(2)}) collective-permute-start(bf16[320,128]{1,0:T(8,128)(2,1)S(1)} %add_convert_fusion.refs_0_), channel_id=1, source_target_pairs={{0,24},{8,16},{16,8},{24,0},{1,25},{9,17},{17,9},{25,1},{2,26},{10... | collective-permute-start | bytes 245768 | tf_op jit(solution)/shard_map/ppermute | solution.py:287
  32.3 5.4 %collective-permute-start.11 = (bf16[320,128]{1,0:T(8,128)(2,1)S(1)}, bf16[320,128]{1,0:T(8,128)(2,1)S(1)}, u32[]{:S(2)}, u32[]{:S(2)}) collective-permute-start(bf16[320,128]{1,0:T(8,128)(2,1)S(1)} %add_convert_fusion.refs_0_), channel_id=1, source_target_pairs={{0,16},{8,24},{16,0},{24,8},{1,17},{9,25},{17,1},{25,9},{2,18},{10... | collective-permute-start | bytes 245768 | tf_op jit(solution)/shard_map/ppermute | solution.py:287
  32.8 4.9 %collective-permute-start.10 = (bf16[320,128]{1,0:T(8,128)(2,1)S(1)}, bf16[320,128]{1,0:T(8,128)(2,1)S(1)}, u32[]{:S(2)}, u32[]{:S(2)}) collective-permute-start(bf16[320,128]{1,0:T(8,128)(2,1)S(1)} %add_convert_fusion.refs_0_), channel_id=1, source_target_pairs={{0,8},{8,0},{16,24},{24,16},{1,9},{9,1},{17,25},{25,17},{2,10},{10... | collective-permute-start | bytes 245768 | tf_op jit(solution)/shard_map/ppermute | solution.py:287

commit v5 on v4

--- a/solution.py
+++ b/solution.py
@@ -38,6 +38,10 @@
     return real, imag
 
 
+def micros(count):
+    return pl.CostEstimate(flops=0, bytes_accessed=count * 3 * 10**6, transcendentals=0)
+
+
 def rotate(a, b):
     return a[0] * b[0] - a[1] * b[1], a[0] * b[1] + a[1] * b[0]
 
@@ -73,55 +77,44 @@
 
 def prepare_kernel(peers, pair_count, points, row_points, factor):
     rows, _, tall, depth = factor.shape
-    held = round_up(pl.cdiv(pair_count, GROUP), GROUP)
     set_index = lax.axis_index("set")
     start = set_index * points
     beside = (set_index ^ 1) * points - start
     slot = lax.broadcasted_iota(jnp.int32, (1, depth), 1)
     point = jnp.where(slot < round_up(points, 128), start + slot, beside)
     heads = round_up(peers + 1, GROUP)
-    sub = lax.broadcasted_iota(jnp.int32, (GROUP + heads + held, 1), 0)
+    sub = lax.broadcasted_iota(jnp.int32, (tall, 1), 0)
     order = sub - GROUP
     head = jnp.where(order < peers, (set_index ^ (2 * order)) * pair_count, TRUNC)
     multiplier = jnp.where(sub < GROUP, sub, jnp.where(order < heads, head, (order - heads) * GROUP))
     for r in range(rows):
         length = row_points[r].astype(F32)
-        real, imag = unit_circle(multiplier, point, length, 1.0 / length)
-        factor[r, 0, :GROUP, :] = real[:GROUP]
-        factor[r, 1, :GROUP, :] = imag[:GROUP]
-        last = GROUP + peers
-        factor[r, 0, GROUP:2 * GROUP, :] = jnp.broadcast_to(real[last:last + 1], (GROUP, depth))
-        factor[r, 1, GROUP:2 * GROUP, :] = jnp.broadcast_to(imag[last:last + 1], (GROUP, depth))
-        tail = real[GROUP + heads:], imag[GROUP + heads:]
-        for peer in range(peers):
-            at = GROUP + peer
-            base = rotate((real[at:at + 1], imag[at:at + 1]), tail)
-            to = 2 * GROUP + peer * held
-            factor[r, 0, to:to + held, :] = base[0]
-            factor[r, 1, to:to + held, :] = base[1]
+        factor[r, 0], factor[r, 1] = unit_circle(multiplier, point, length, 1.0 / length)
 
 
 def prepare(row_points, points, peers, pair_count):
     rows = row_points.shape[0]
-    tall = 2 * GROUP + peers * round_up(pl.cdiv(pair_count, GROUP), GROUP)
+    tall = GROUP + round_up(peers + 1, GROUP) + round_up(pl.cdiv(pair_count, GROUP), GROUP)
     return pl.pallas_call(
         functools.partial(prepare_kernel, peers, pair_count, points),
         out_shape=jax.ShapeDtypeStruct((rows, 2, tall, round_up(points, 128) + 128), F32),
         in_specs=[pl.BlockSpec(memory_space=pltpu.SMEM)],
         out_specs=pl.BlockSpec(memory_space=pltpu.VMEM),
         compiler_params=pltpu.CompilerParams(vmem_limit_bytes=VMEM),
-        cost_estimate=pl.CostEstimate(flops=1 << 22, bytes_accessed=1 << 22, transcendentals=0),
+        cost_estimate=micros(1),
         name="prepare",
     )(row_points)
 
 
 def fourier_kernel(groups, first_group, peers, pair_count, row_points, factor, mine, theirs, *refs):
     outs = refs[:peers]
-    values, table, sums, twist = refs[peers:]
+    values, table, sums, twist, bases = refs[peers:]
     rows = table.shape[0]
     width = outs[0].shape[1]
     depth = table.shape[2] // 3
     held = round_up(pl.cdiv(pair_count, GROUP), GROUP)
+    tail = factor.shape[2] - held
+    last_at = GROUP + peers
     set_index = lax.axis_index("set")
     points = mine.shape[0] // rows
     for side, block in enumerate((mine, theirs)):
@@ -132,10 +125,16 @@
     sub = lax.broadcasted_iota(jnp.int32, (GROUP, 1), 0)
     for r in range(rows):
         near = factor[r, 0, :GROUP, :], factor[r, 1, :GROUP, :]
-        last = factor[r, 0, GROUP:2 * GROUP, :], factor[r, 1, GROUP:2 * GROUP, :]
+        last = factor[r, 0, last_at:last_at + 1, :], factor[r, 1, last_at:last_at + 1, :]
+        for peer in range(peers):
+            at = GROUP + peer
+            head = factor[r, 0, at:at + 1, :], factor[r, 1, at:at + 1, :]
+            base = rotate(head, (factor[r, 0, tail:, :], factor[r, 1, tail:, :]))
+            bases[r, 0, peer * held:(peer + 1) * held, :] = base[0]
+            bases[r, 1, peer * held:(peer + 1) * held, :] = base[1]
         for index in range(peers * groups):
-            at = 2 * GROUP + index // groups * held + first_group + index % groups
-            base = factor[r, 0, at:at + 1, :], factor[r, 1, at:at + 1, :]
+            at = index // groups * held + first_group + index % groups
+            base = bases[r, 0, at:at + 1, :], bases[r, 1, at:at + 1, :]
             first = rotate(base, near)
             second = rotate(last, (first[0], -first[1]))
             block = jnp.concatenate([*first, *second], axis=0)
@@ -183,8 +182,10 @@
             pltpu.VMEM((rows, tall, 3 * depth), BF16),
             pltpu.VMEM((rows, tall, 2 * width), F32),
             pltpu.VMEM((rows, tall, 128), F32),
+            pltpu.VMEM((rows, 2, peers * round_up(pl.cdiv(pair_count, GROUP), GROUP), depth + 128), F32),
         ],
         compiler_params=pltpu.CompilerParams(vmem_limit_bytes=VMEM),
+        cost_estimate=micros(3),
         name="fourier_sums",
     )(row_points, factor, mine, theirs)
 
@@ -228,6 +229,7 @@
         in_specs=[vmem],
         out_specs=vmem,
         compiler_params=pltpu.CompilerParams(vmem_limit_bytes=VMEM),
+        cost_estimate=micros(1),
         name="spread_weights",
     )(legend)
 
@@ -275,6 +277,7 @@
         input_output_aliases={1 + bands: 0} if previous else {},
         scratch_shapes=[pltpu.VMEM((pairs, slots, width), F32), pltpu.SemaphoreType.DMA((pairs // 2,))],
         compiler_params=pltpu.CompilerParams(vmem_limit_bytes=VMEM),
+        cost_estimate=micros(3),
         name="spectra_part",
     )(weights, *held, *previous)
 
@@ -298,6 +301,7 @@
     theirs = lax.ppermute(flat, "set", swap("set", set_size, 1))
     factor = prepare(row_points, points, peers, pair_count)
     legend = lax.dynamic_slice_in_dim(legendre, lax.axis_index("band") * slots, slots, 2)
+    legend, theirs = lax.optimization_barrier((legend, theirs))
     weights = spread_weights(legend, rows, band_size)
     all_groups = pl.cdiv(pair_count, GROUP)
     cut = (all_groups + 1) // 2
@@ -311,7 +315,7 @@
         steps = steps[::-1] if gathered else steps[::2] + steps[1::2]
         arrived = exchange([parts[k].astype(WIRE) for k in steps], "set", [2 * k for k in steps])
         if gathered:
-            arrived, weights, gathered[0] = lax.optimization_barrier((arrived, weights, gathered[0]))
+            arrived, weights = lax.optimization_barrier((arrived, weights))
         total = parts[0]
         for part in arrived:
             total = total + part.astype(F32)

time: 41.4 us -> 38.6 us (0.932)
  local copies, waits for them, and re-layouts: 4.25 us -> 1.77 us
  Pallas kernels: 15 us -> 16.2 us
  other arithmetic: 1.08 us -> 0.18 us
  waiting for transfers between devices: 2.81 us -> 2.3 us
    unnamed x14 -> x8, local copies, waits for them, and re-layouts: 4.02 us -> 1.53 us
    pallas_call x2, Pallas kernels: 6.25 us -> 7.54 us  [fourier_sums(): pl.pallas_call(functools.partial(fourier_kernel, groups, first_group, pee...]
    convert_element_type x2, other arithmetic: 0.99 us -> 0.09 us  [shards(): rounded = total.astype(BF16)]
  transfers between devices with their start and end apart: 13 -> 13, of which waited for: 5 -> 3; matrix products, arithmetic and copies ran while one was open for 3% -> 1% of each run, Pallas kernels for 21% -> 24%
where the time goes in v5:
time: 38.6 us; the launch traced here: 38.4 us
  starting transfers between devices  17.8 us (46%)
  Pallas kernels  16.2 us (42%)
  waiting for transfers between devices  2.3 us (6%)
  local copies, waits for them, and re-layouts  1.77 us (5%)
    ppermute x12, starting transfers between devices, exchange(): lax.ppermute(part, axis, swap(axis, lax.axis_size(axis), step))  17.3 us
    pallas_call x2, Pallas kernels, fourier_sums(): pl.pallas_call(functools.partial(fourier_kernel, groups, first_group, pee...  7.54 us
    pallas_call x2, Pallas kernels, spectra_part(): pl.pallas_call(functools.partial(spectra_kernel, bands, first_group, pair...  6.71 us
    ppermute x12, waiting for transfers between devices, exchange(): lax.ppermute(part, axis, swap(axis, lax.axis_size(axis), step))  2.3 us
    unnamed x8, local copies, waits for them, and re-layouts  1.53 us
    pallas_call x1, Pallas kernels, spread_weights(): pl.pallas_call(functools.partial(weights_kernel, rows, bands), out_shape=...  0.97 us
    pallas_call x1, Pallas kernels, prepare(): pl.pallas_call(functools.partial(prepare_kernel, peers, pair_count, point...  0.95 us
  transfers between devices with their start and end apart: 13, of which 3 were waited for; matrix products, arithmetic and copies ran while one was open for 1% of the time, Pallas kernels for 24%

profile of v5, /device:TPU:0, one launch (start us, length us, event | category | flops | bytes accessed | tf_op | source)
XLA Modules:
  0.0 38.4 jit_solution(5331751794103977984)
XLA Ops:
  0.0 0.5 %collective-permute-start = (f32[1288,128]{1,0:T(8,128)}, f32[1288,128]{1,0:T(8,128)}, u32[]{:S(2)}, u32[]{:S(2)}) collective-permute-start(f32[1288,128]{1,0:T(8,128)} %bitcast.3), channel_id=1, source_target_pairs={{0,1},{1,0},{2,3},{3,2},{4,5},{5,4},{6,7},{7,6},{8,9},{9,8},{10,11... | collective-permute-start | bytes 1978376 | tf_op jit(solution)/shard_map/ppermute | solution.py:301
  0.5 0.9 %copy-done.2 = s32[2]{0:T(128)S(1)} copy-done((s32[2]{0:T(128)S(1)}, s32[2]{0:T(128)}, u32[]{:S(2)}) %copy-start.2) | copy-done | bytes 32
  1.3 0.9 %prepare.1.factor = f32[2,2,32,896]{3,2,1,0:T(8,128)S(1)} custom-call(s32[2]{0:T(128)S(1)} %copy-done.2), custom_call_target="tpu_custom_call" | custom-call | bytes 3000000 | tf_op jit(solution)/shard_map/prepare/pallas_call | solution.py:98
  2.3 0.2 constant_dynamic-slice_fusion.legend
  2.5 0.0 collective-permute-done.theirs
  2.6 0.0 copy-start.3
  2.6 0.6 %copy-done.3 = s32[2]{0:T(128)S(1)} copy-done((s32[2]{0:T(128)S(1)}, s32[2]{0:T(128)}, u32[]{:S(2)}) %copy-start.3) | copy-done | bytes 32
  3.2 3.8 %fourier_sums.3 = (f32[320,128]{1,0:T(8,128)S(1)}, f32[320,128]{1,0:T(8,128)S(1)}, f32[320,128]{1,0:T(8,128)S(1)}, f32[320,128]{1,0:T(8,128)S(1)}) custom-call(s32[2]{0:T(128)S(1)} %copy-done.3, f32[2,2,32,896]{3,2,1,0:T(8,128)S(1)} %prepare.1.factor, f32[1288,128]{1,0:T(8,128)S(1)} %bitcast.4, f32[1288,128]{1,0:T(8,128)} %collective-permute-done.theirs), custom_call_target="tpu_custom_call" | custom-call | bytes 9000000 | tf_op jit(solution)/shard_map/fourier_sums/pallas_call | solution.py:175
  7.0 4.0 %collective-permute-start.9 = (f16[320,128]{1,0:T(8,128)(2,1)S(1)}, f16[320,128]{1,0:T(8,128)(2,1)S(1)}, u32[]{:S(2)}, u32[]{:S(2)}) collective-permute-start(f16[320,128]{1,0:T(8,128)(2,1)S(1)} %convert_element_type.53), channel_id=1, source_target_pairs={{0,4},{1,5},{2,6},{3,7},{4,0},{5,1},{6,2},{7,3},{8,12},{9,13},{10,... | collective-permute-start | bytes 245768 | tf_op jit(solution)/shard_map/ppermute | solution.py:290
  11.0 1.4 %collective-permute-start.8 = (f16[320,128]{1,0:T(8,128)(2,1)S(1)}, f16[320,128]{1,0:T(8,128)(2,1)S(1)}, u32[]{:S(2)}, u32[]{:S(2)}) collective-permute-start(f16[320,128]{1,0:T(8,128)(2,1)S(1)} %convert_element_type.51), channel_id=1, source_target_pairs={{0,6},{1,7},{2,4},{3,5},{4,2},{5,3},{6,0},{7,1},{8,14},{9,15},{10,... | collective-permute-start | bytes 245768 | tf_op jit(solution)/shard_map/ppermute | solution.py:290
  12.4 0.3 collective-permute-start.7
  12.8 3.8 %fourier_sums.2 = (f32[320,128]{1,0:T(8,128)S(1)}, f32[320,128]{1,0:T(8,128)S(1)}, f32[320,128]{1,0:T(8,128)S(1)}, f32[320,128]{1,0:T(8,128)S(1)}) custom-call(s32[2]{0:T(128)S(1)} %copy-done.3, f32[2,2,32,896]{3,2,1,0:T(8,128)S(1)} %prepare.1.factor, f32[1288,128]{1,0:T(8,128)S(1)} %bitcast.5, f32[1288,128]{1,0:T(8,128)} %collective-permute-done.theirs), custom_call_target="tpu_custom_call" | custom-call | bytes 9000000 | tf_op jit(solution)/shard_map/fourier_sums/pallas_call | solution.py:175
  16.6 1.8 %collective-permute-start.3 = (f16[320,128]{1,0:T(8,128)(2,1)S(1)}, f16[320,128]{1,0:T(8,128)(2,1)S(1)}, u32[]{:S(2)}, u32[]{:S(2)}) collective-permute-start(f16[320,128]{1,0:T(8,128)(2,1)S(1)} %convert_element_type.44), channel_id=1, source_target_pairs={{0,2},{1,3},{2,0},{3,1},{4,6},{5,7},{6,4},{7,5},{8,10},{9,11},{10,... | collective-permute-start | bytes 245768 | tf_op jit(solution)/shard_map/ppermute | solution.py:290
  18.4 1.7 %collective-permute-start.2 = (f16[320,128]{1,0:T(8,128)(2,1)S(1)}, f16[320,128]{1,0:T(8,128)(2,1)S(1)}, u32[]{:S(2)}, u32[]{:S(2)}) collective-permute-start(f16[320,128]{1,0:T(8,128)(2,1)S(1)} %convert_element_type.43), channel_id=1, source_target_pairs={{0,4},{1,5},{2,6},{3,7},{4,0},{5,1},{6,2},{7,3},{8,12},{9,13},{10,... | collective-permute-start | bytes 245768 | tf_op jit(solution)/shard_map/ppermute | solution.py:290
  20.1 1.0 %spread_weights.1.weights = bf16[10,352,256]{2,1,0:T(8,128)(2,1)S(1)} custom-call(bf16[80,8,352]{2,1,0:T(8,128)(2,1)S(1)} %constant_dynamic-slice_fusion.legend), custom_call_target="tpu_custom_call" | custom-call | bytes 3000000 | tf_op jit(solution)/shard_map/spread_weights/pallas_call | solution.py:226
  21.1 0.0 collective-permute-done.9
  21.1 1.0 %collective-permute-start.1 = (f16[320,128]{1,0:T(8,128)(2,1)S(1)}, f16[320,128]{1,0:T(8,128)(2,1)S(1)}, u32[]{:S(2)}, u32[]{:S(2)}) collective-permute-start(f16[320,128]{1,0:T(8,128)(2,1)S(1)} %convert_element_type.42), channel_id=1, source_target_pairs={{0,6},{1,7},{2,4},{3,5},{4,2},{5,3},{6,0},{7,1},{8,14},{9,15},{10,... | collective-permute-start | bytes 245768 | tf_op jit(solution)/shard_map/ppermute | solution.py:290
  22.2 2.5 %collective-permute-start.12 = (bf16[320,128]{1,0:T(8,128)(2,1)S(1)}, bf16[320,128]{1,0:T(8,128)(2,1)S(1)}, u32[]{:S(2)}, u32[]{:S(2)}) collective-permute-start(bf16[320,128]{1,0:T(8,128)(2,1)S(1)} %add_convert_fusion.refs_0_), channel_id=1, source_target_pairs={{0,24},{8,16},{16,8},{24,0},{1,25},{9,17},{17,9},{25,1},{2,26},{10... | collective-permute-start | bytes 245768 | tf_op jit(solution)/shard_map/ppermute | solution.py:290
  24.7 0.5 %collective-permute-start.11 = (bf16[320,128]{1,0:T(8,128)(2,1)S(1)}, bf16[320,128]{1,0:T(8,128)(2,1)S(1)}, u32[]{:S(2)}, u32[]{:S(2)}) collective-permute-start(bf16[320,128]{1,0:T(8,128)(2,1)S(1)} %add_convert_fusion.refs_0_), channel_id=1, source_target_pairs={{0,16},{8,24},{16,0},{24,8},{1,17},{9,25},{17,1},{25,9},{2,18},{10... | collective-permute-start | bytes 245768 | tf_op jit(solution)/shard_map/ppermute | solution.py:290
  25.2 0.5 %collective-permute-start.10 = (bf16[320,128]{1,0:T(8,128)(2,1)S(1)}, bf16[320,128]{1,0:T(8,128)(2,1)S(1)}, u32[]{:S(2)}, u32[]{:S(2)}) collective-permute-start(bf16[320,128]{1,0:T(8,128)(2,1)S(1)} %add_convert_fusion.refs_0_), channel_id=1, source_target_pairs={{0,8},{8,0},{16,24},{24,16},{1,9},{9,1},{17,25},{25,17},{2,10},{10... | collective-permute-start | bytes 245768 | tf_op jit(solution)/shard_map/ppermute | solution.py:290
  25.7 0.3 collective-permute-done.2
  26.1 1.4 %collective-permute-done.1 = f16[320,128]{1,0:T(8,128)(2,1)S(1)} collective-permute-done((f16[320,128]{1,0:T(8,128)(2,1)S(1)}, f16[320,128]{1,0:T(8,128)(2,1)S(1)}, u32[]{:S(2)}, u32[]{:S(2)}) %collective-permute-start.1) | collective-permute-done | bytes 81952 | tf_op jit(solution)/shard_map/ppermute | solution.py:290
  27.6 2.5 %collective-permute-start.6 = (bf16[320,128]{1,0:T(8,128)(2,1)S(1)}, bf16[320,128]{1,0:T(8,128)(2,1)S(1)}, u32[]{:S(2)}, u32[]{:S(2)}) collective-permute-start(bf16[320,128]{1,0:T(8,128)(2,1)S(1)} %add_convert_fusion.1.refs_0_), channel_id=1, source_target_pairs={{0,24},{8,16},{16,8},{24,0},{1,25},{9,17},{17,9},{25,1},{2,26},{10... | collective-permute-start | bytes 245768 | tf_op jit(solution)/shard_map/ppermute | solution.py:290
  30.1 0.5 %collective-permute-start.5 = (bf16[320,128]{1,0:T(8,128)(2,1)S(1)}, bf16[320,128]{1,0:T(8,128)(2,1)S(1)}, u32[]{:S(2)}, u32[]{:S(2)}) collective-permute-start(bf16[320,128]{1,0:T(8,128)(2,1)S(1)} %add_convert_fusion.1.refs_0_), channel_id=1, source_target_pairs={{0,16},{8,24},{16,0},{24,8},{1,17},{9,25},{17,1},{25,9},{2,18},{10... | collective-permute-start | bytes 245768 | tf_op jit(solution)/shard_map/ppermute | solution.py:290
  30.6 0.0 collective-permute-done.12.refs_3_
  30.6 0.5 %collective-permute-start.4 = (bf16[320,128]{1,0:T(8,128)(2,1)S(1)}, bf16[320,128]{1,0:T(8,128)(2,1)S(1)}, u32[]{:S(2)}, u32[]{:S(2)}) collective-permute-start(bf16[320,128]{1,0:T(8,128)(2,1)S(1)} %add_convert_fusion.1.refs_0_), channel_id=1, source_target_pairs={{0,8},{8,0},{16,24},{24,16},{1,9},{9,1},{17,25},{25,17},{2,10},{10... | collective-permute-start | bytes 245768 | tf_op jit(solution)/shard_map/ppermute | solution.py:290
  31.1 0.0 collective-permute-done.11.refs_2_
  31.1 0.0 collective-permute-done.10.refs_1_
  31.1 3.4 %spectra_part.2.refs_4_ = f32[80,352,128]{2,1,0:T(8,128)} custom-call(bf16[10,352,256]{2,1,0:T(8,128)(2,1)S(1)} %spread_weights.1.weights, bf16[320,128]{1,0:T(8,128)(2,1)S(1)} %add_convert_fusion.refs_0_, bf16[320,128]{1,0:T(8,128)(2,1)S(1)} %collective-permute-done.10.refs_1_, bf16[320,128]{1,0:T(8,128)(2,1)S(1)} %collective-permute-done.11.refs_2_, ...), custom_call_target="tpu_custom_call" | custom-call | bytes 9000000 | tf_op jit(solution)/shard_map/spectra_part/pallas_call | solution.py:272
  34.5 0.0 collective-permute-done.5.refs_2_
  34.5 0.5 %collective-permute-done.4.refs_1_ = bf16[320,128]{1,0:T(8,128)(2,1)S(1)} collective-permute-done((bf16[320,128]{1,0:T(8,128)(2,1)S(1)}, bf16[320,128]{1,0:T(8,128)(2,1)S(1)}, u32[]{:S(2)}, u32[]{:S(2)}) %collective-permute-start.4) | collective-permute-done | bytes 81952 | tf_op jit(solution)/shard_map/ppermute | solution.py:290
  35.0 3.4 %spectra_part.3 = f32[80,352,128]{2,1,0:T(8,128)} custom-call(bf16[10,352,256]{2,1,0:T(8,128)(2,1)S(1)} %spread_weights.1.weights, bf16[320,128]{1,0:T(8,128)(2,1)S(1)} %add_convert_fusion.1.refs_0_, bf16[320,128]{1,0:T(8,128)(2,1)S(1)} %collective-permute-done.4.refs_1_, ...), custom_call_target="tpu_custom_call", output_to_operand_aliasing={{}: (5, {})} | custom-call | bytes 9000000 | tf_op jit(solution)/shard_map/spectra_part/pallas_call | solution.py:272
  (17 shorter events, 0.2 us)
Async XLA Ops:
  0.0 2.3 %copy-start = (bf16[80,8,1408]{2,1,0:T(8,128)(2,1)S(1)}, bf16[80,8,1408]{2,1,0:T(8,128)(2,1)}, u32[]{:S(2)}) copy-start(bf16[80,8,1408]{2,1,0:T(8,128)(2,1)} %param.5) | copy-start | bytes 5406724
  0.0 2.6 %copy-start.1 = (f32[2,644,128]{2,0,1:T(2,128)S(1)}, f32[2,644,128]{2,0,1:T(2,128)}, u32[]{:S(2)}) copy-start(f32[2,644,128]{2,0,1:T(2,128)} %param.3) | copy-start | bytes 1978372
  0.0 2.5 %collective-permute-start = (f32[1288,128]{1,0:T(8,128)}, f32[1288,128]{1,0:T(8,128)}, u32[]{:S(2)}, u32[]{:S(2)}) collective-permute-start(f32[1288,128]{1,0:T(8,128)} %bitcast.3), channel_id=1, source_target_pairs={{0,1},{1,0},{2,3},{3,2},{4,5},{5,4},{6,7},{7,6},{8,9},{9,8},{10,11... | collective-permute-start | bytes 1978376 | tf_op jit(solution)/shard_map/ppermute | solution.py:301
  0.5 0.9 %copy-start.2 = (s32[2]{0:T(128)S(1)}, s32[2]{0:T(128)}, u32[]{:S(2)}) copy-start(s32[2]{0:T(128)} %row_points.5) | copy-start | bytes 28
  2.6 0.7 %copy-start.3 = (s32[2]{0:T(128)S(1)}, s32[2]{0:T(128)}, u32[]{:S(2)}) copy-start(s32[2]{0:T(128)} %row_points.5) | copy-start | bytes 28
  7.0 14.1 %collective-permute-start.9 = (f16[320,128]{1,0:T(8,128)(2,1)S(1)}, f16[320,128]{1,0:T(8,128)(2,1)S(1)}, u32[]{:S(2)}, u32[]{:S(2)}) collective-permute-start(f16[320,128]{1,0:T(8,128)(2,1)S(1)} %convert_element_type.53), channel_id=1, source_target_pairs={{0,4},{1,5},{2,6},{3,7},{4,0},{5,1},{6,2},{7,3},{8,12},{9,13},{10,... | collective-permute-start | bytes 245768 | tf_op jit(solution)/shard_map/ppermute | solution.py:290
  11.0 11.1 %collective-permute-start.8 = (f16[320,128]{1,0:T(8,128)(2,1)S(1)}, f16[320,128]{1,0:T(8,128)(2,1)S(1)}, u32[]{:S(2)}, u32[]{:S(2)}) collective-permute-start(f16[320,128]{1,0:T(8,128)(2,1)S(1)} %convert_element_type.51), channel_id=1, source_target_pairs={{0,6},{1,7},{2,4},{3,5},{4,2},{5,3},{6,0},{7,1},{8,14},{9,15},{10,... | collective-permute-start | bytes 245768 | tf_op jit(solution)/shard_map/ppermute | solution.py:290
  12.4 9.7 %collective-permute-start.7 = (f16[320,128]{1,0:T(8,128)(2,1)S(1)}, f16[320,128]{1,0:T(8,128)(2,1)S(1)}, u32[]{:S(2)}, u32[]{:S(2)}) collective-permute-start(f16[320,128]{1,0:T(8,128)(2,1)S(1)} %convert_element_type.49), channel_id=1, source_target_pairs={{0,2},{1,3},{2,0},{3,1},{4,6},{5,7},{6,4},{7,5},{8,10},{9,11},{10,... | collective-permute-start | bytes 245768 | tf_op jit(solution)/shard_map/ppermute | solution.py:290
  16.6 8.6 %collective-permute-start.3 = (f16[320,128]{1,0:T(8,128)(2,1)S(1)}, f16[320,128]{1,0:T(8,128)(2,1)S(1)}, u32[]{:S(2)}, u32[]{:S(2)}) collective-permute-start(f16[320,128]{1,0:T(8,128)(2,1)S(1)} %convert_element_type.44), channel_id=1, source_target_pairs={{0,2},{1,3},{2,0},{3,1},{4,6},{5,7},{6,4},{7,5},{8,10},{9,11},{10,... | collective-permute-start | bytes 245768 | tf_op jit(solution)/shard_map/ppermute | solution.py:290
  18.4 7.7 %collective-permute-start.2 = (f16[320,128]{1,0:T(8,128)(2,1)S(1)}, f16[320,128]{1,0:T(8,128)(2,1)S(1)}, u32[]{:S(2)}, u32[]{:S(2)}) collective-permute-start(f16[320,128]{1,0:T(8,128)(2,1)S(1)} %convert_element_type.43), channel_id=1, source_target_pairs={{0,4},{1,5},{2,6},{3,7},{4,0},{5,1},{6,2},{7,3},{8,12},{9,13},{10,... | collective-permute-start | bytes 245768 | tf_op jit(solution)/shard_map/ppermute | solution.py:290
  21.1 6.4 %collective-permute-start.1 = (f16[320,128]{1,0:T(8,128)(2,1)S(1)}, f16[320,128]{1,0:T(8,128)(2,1)S(1)}, u32[]{:S(2)}, u32[]{:S(2)}) collective-permute-start(f16[320,128]{1,0:T(8,128)(2,1)S(1)} %convert_element_type.42), channel_id=1, source_target_pairs={{0,6},{1,7},{2,4},{3,5},{4,2},{5,3},{6,0},{7,1},{8,14},{9,15},{10,... | collective-permute-start | bytes 245768 | tf_op jit(solution)/shard_map/ppermute | solution.py:290
  22.2 8.4 %collective-permute-start.12 = (bf16[320,128]{1,0:T(8,128)(2,1)S(1)}, bf16[320,128]{1,0:T(8,128)(2,1)S(1)}, u32[]{:S(2)}, u32[]{:S(2)}) collective-permute-start(bf16[320,128]{1,0:T(8,128)(2,1)S(1)} %add_convert_fusion.refs_0_), channel_id=1, source_target_pairs={{0,24},{8,16},{16,8},{24,0},{1,25},{9,17},{17,9},{25,1},{2,26},{10... | collective-permute-start | bytes 245768 | tf_op jit(solution)/shard_map/ppermute | solution.py:290
  24.7 6.4 %collective-permute-start.11 = (bf16[320,128]{1,0:T(8,128)(2,1)S(1)}, bf16[320,128]{1,0:T(8,128)(2,1)S(1)}, u32[]{:S(2)}, u32[]{:S(2)}) collective-permute-start(bf16[320,128]{1,0:T(8,128)(2,1)S(1)} %add_convert_fusion.refs_0_), channel_id=1, source_target_pairs={{0,16},{8,24},{16,0},{24,8},{1,17},{9,25},{17,1},{25,9},{2,18},{10... | collective-permute-start | bytes 245768 | tf_op jit(solution)/shard_map/ppermute | solution.py:290
  25.2 5.9 %collective-permute-start.10 = (bf16[320,128]{1,0:T(8,128)(2,1)S(1)}, bf16[320,128]{1,0:T(8,128)(2,1)S(1)}, u32[]{:S(2)}, u32[]{:S(2)}) collective-permute-start(bf16[320,128]{1,0:T(8,128)(2,1)S(1)} %add_convert_fusion.refs_0_), channel_id=1, source_target_pairs={{0,8},{8,0},{16,24},{24,16},{1,9},{9,1},{17,25},{25,17},{2,10},{10... | collective-permute-start | bytes 245768 | tf_op jit(solution)/shard_map/ppermute | solution.py:290
  27.6 6.9 %collective-permute-start.6 = (bf16[320,128]{1,0:T(8,128)(2,1)S(1)}, bf16[320,128]{1,0:T(8,128)(2,1)S(1)}, u32[]{:S(2)}, u32[]{:S(2)}) collective-permute-start(bf16[320,128]{1,0:T(8,128)(2,1)S(1)} %add_convert_fusion.1.refs_0_), channel_id=1, source_target_pairs={{0,24},{8,16},{16,8},{24,0},{1,25},{9,17},{17,9},{25,1},{2,26},{10... | collective-permute-start | bytes 245768 | tf_op jit(solution)/shard_map/ppermute | solution.py:290
  30.1 4.4 %collective-permute-start.5 = (bf16[320,128]{1,0:T(8,128)(2,1)S(1)}, bf16[320,128]{1,0:T(8,128)(2,1)S(1)}, u32[]{:S(2)}, u32[]{:S(2)}) collective-permute-start(bf16[320,128]{1,0:T(8,128)(2,1)S(1)} %add_convert_fusion.1.refs_0_), channel_id=1, source_target_pairs={{0,16},{8,24},{16,0},{24,8},{1,17},{9,25},{17,1},{25,9},{2,18},{10... | collective-permute-start | bytes 245768 | tf_op jit(solution)/shard_map/ppermute | solution.py:290
  30.6 4.4 %collective-permute-start.4 = (bf16[320,128]{1,0:T(8,128)(2,1)S(1)}, bf16[320,128]{1,0:T(8,128)(2,1)S(1)}, u32[]{:S(2)}, u32[]{:S(2)}) collective-permute-start(bf16[320,128]{1,0:T(8,128)(2,1)S(1)} %add_convert_fusion.1.refs_0_), channel_id=1, source_target_pairs={{0,8},{8,0},{16,24},{24,16},{1,9},{9,1},{17,25},{25,17},{2,10},{10... | collective-permute-start | bytes 245768 | tf_op jit(solution)/shard_map/ppermute | solution.py:290

commit v6 on v5

--- a/solution.py
+++ b/solution.py
@@ -51,24 +51,28 @@
     return high, (values - high.astype(F32)).astype(BF16)
 
 
-def prepare_values(raw, start, length, length_int):
-    width = raw.shape[1]
+def layout(points):
+    rest = points % 128
+    return points - rest, rest, round_up(3 * rest, 128)
+
+
+def store_values(out, side, raw, start, length):
+    points, width = raw.shape
+    body, rest, extra = layout(points)
     lane = lax.broadcasted_iota(jnp.int32, (1, width), 1)
-    where = start + lax.broadcasted_iota(jnp.int32, (raw.shape[0], 1), 0)
-    folded = pltpu.roll(raw, width // 2, 1) + jnp.where(lane < width // 2, raw, -raw)
-    scale = lax.rsqrt(jnp.full((1, width), length, F32))
-    return split(jnp.where(where < length_int, folded * scale, 0.0))
-
-
-def store_values(out, r, side, raw, start, length_int):
-    points, width = raw.shape
-    depth = out.shape[1] // 3
+    sign = jnp.where(lane < width // 2, 1.0, -1.0)
+    where = start + lax.broadcasted_iota(jnp.int32, (points, 1), 0)
+    folded = pltpu.roll(raw, width // 2, 1) + raw * sign
+    folded = jnp.where(where.astype(F32) < length, folded, 0.0)
     lanes = slice(side * width, (side + 1) * width)
-    high, low = prepare_values(raw, start, length_int.astype(F32), length_int)
-    for part, values in enumerate((high, low, high)):
-        out[r, part * depth:part * depth + points, lanes] = values
-        rest = jnp.zeros((depth - points, width), BF16)
-        out[r, part * depth + points:(part + 1) * depth, lanes] = rest
+    high, low = split(folded[:body])
+    for part, piece in enumerate((high, low, high)):
+        out[part * body:(part + 1) * body, lanes] = piece
+    if rest:
+        high, low = split(folded[body:])
+        parts = [piece.astype(F32) for piece in (high, low, high)]
+        parts.append(jnp.zeros((extra - 3 * rest, width), F32))
+        out[3 * body:, lanes] = jnp.concatenate(parts, axis=0).astype(BF16)
 
 
 def row_of(block, r, rows):
@@ -76,12 +80,14 @@
 
 
 def prepare_kernel(peers, pair_count, points, row_points, factor):
-    rows, _, tall, depth = factor.shape
+    rows, _, tall, wide = factor.shape
+    body, rest, extra = layout(points)
     set_index = lax.axis_index("set")
     start = set_index * points
     beside = (set_index ^ 1) * points - start
-    slot = lax.broadcasted_iota(jnp.int32, (1, depth), 1)
-    point = jnp.where(slot < round_up(points, 128), start + slot, beside)
+    slot = lax.broadcasted_iota(jnp.int32, (1, wide), 1)
+    point = start + jnp.where(slot < body, slot, body + (slot - body) % max(rest, 1))
+    point = jnp.where(slot < body + extra, point, beside)
     heads = round_up(peers + 1, GROUP)
     sub = lax.broadcasted_iota(jnp.int32, (tall, 1), 0)
     order = sub - GROUP
@@ -89,15 +95,23 @@
     multiplier = jnp.where(sub < GROUP, sub, jnp.where(order < heads, head, (order - heads) * GROUP))
     for r in range(rows):
         length = row_points[r].astype(F32)
-        factor[r, 0], factor[r, 1] = unit_circle(multiplier, point, length, 1.0 / length)
+        scale = jnp.where(slot < body + extra, lax.rsqrt(jnp.full((1, wide), length, F32)), 1.0)
+        scale = jnp.where(sub < GROUP, scale, 1.0)
+        real, imag = unit_circle(multiplier, point, length, 1.0 / length)
+        factor[r, 0] = jnp.where(order == heads - 1, length, real * scale)
+        factor[r, 1] = imag * scale
+
+
+def table_rows(peers, pair_count):
+    return GROUP + round_up(peers + 2, GROUP), round_up(pl.cdiv(pair_count, GROUP), GROUP)
 
 
 def prepare(row_points, points, peers, pair_count):
     rows = row_points.shape[0]
-    tall = GROUP + round_up(peers + 1, GROUP) + round_up(pl.cdiv(pair_count, GROUP), GROUP)
+    body, _, extra = layout(points)
     return pl.pallas_call(
         functools.partial(prepare_kernel, peers, pair_count, points),
-        out_shape=jax.ShapeDtypeStruct((rows, 2, tall, round_up(points, 128) + 128), F32),
+        out_shape=jax.ShapeDtypeStruct((rows, 2, sum(table_rows(peers, pair_count)), body + extra + 128), F32),
         in_specs=[pl.BlockSpec(memory_space=pltpu.SMEM)],
         out_specs=pl.BlockSpec(memory_space=pltpu.VMEM),
         compiler_params=pltpu.CompilerParams(vmem_limit_bytes=VMEM),
@@ -106,88 +120,85 @@
     )(row_points)
 
 
-def fourier_kernel(groups, first_group, peers, pair_count, row_points, factor, mine, theirs, *refs):
+def fourier_kernel(groups, first_group, peers, pair_count, factor, mine, theirs, *refs):
     outs = refs[:peers]
-    values, table, sums, twist, bases = refs[peers:]
-    rows = table.shape[0]
-    width = outs[0].shape[1]
-    depth = table.shape[2] // 3
-    held = round_up(pl.cdiv(pair_count, GROUP), GROUP)
-    tail = factor.shape[2] - held
+    rows = factor.shape[0]
+    scratch = refs[peers:]
+    points = mine.shape[0] // rows
+    width = mine.shape[1]
+    body, rest, extra = layout(points)
+    tail, _ = table_rows(peers, pair_count)
     last_at = GROUP + peers
     set_index = lax.axis_index("set")
-    points = mine.shape[0] // rows
-    for side, block in enumerate((mine, theirs)):
-        for r in range(rows):
-            store_values(values, r, side, row_of(block, r, rows), (set_index ^ side) * points, row_points[r])
-    lane = lax.broadcasted_iota(jnp.int32, (1, width), 1)
-    north = lane < width // 2
     sub = lax.broadcasted_iota(jnp.int32, (GROUP, 1), 0)
+    whole = lax.broadcasted_iota(jnp.int32, (1, extra), 1) < 2 * rest
+    size = 4 * GROUP * groups
     for r in range(rows):
+        values, table, sums, twist = scratch[4 * r:4 * r + 4]
+        length = factor[r, 0, tail - 1:tail, :width]
+        for side, block in enumerate((mine, theirs)):
+            store_values(values, side, row_of(block, r, rows), (set_index ^ side) * points, length)
         near = factor[r, 0, :GROUP, :], factor[r, 1, :GROUP, :]
         last = factor[r, 0, last_at:last_at + 1, :], factor[r, 1, last_at:last_at + 1, :]
         for peer in range(peers):
             at = GROUP + peer
             head = factor[r, 0, at:at + 1, :], factor[r, 1, at:at + 1, :]
-            base = rotate(head, (factor[r, 0, tail:, :], factor[r, 1, tail:, :]))
-            bases[r, 0, peer * held:(peer + 1) * held, :] = base[0]
-            bases[r, 1, peer * held:(peer + 1) * held, :] = base[1]
-        for index in range(peers * groups):
-            at = index // groups * held + first_group + index % groups
-            base = bases[r, 0, at:at + 1, :], bases[r, 1, at:at + 1, :]
-            first = rotate(base, near)
-            second = rotate(last, (first[0], -first[1]))
-            block = jnp.concatenate([*first, *second], axis=0)
-            high, low = split(block[:, :depth])
-            lines = slice(index * 4 * GROUP, (index + 1) * 4 * GROUP)
-            for part, piece in enumerate((high, high, low)):
-                table[r, lines, part * depth:(part + 1) * depth] = piece
-            twist[r, lines, :] = block[:, depth:]
-        sums[r] = jnp.dot(table[r], values[r], preferred_element_type=F32)
-    for peer in range(peers):
-        for g in range(groups):
-            base = (set_index ^ (2 * peer)) * pair_count + (first_group + g) * GROUP
-            for side in range(2):
-                wave = base + sub
-                wave = TRUNC - wave if side else wave
-                at = ((peer * groups + g) * 2 + side) * 2 * GROUP
-                for r in range(rows):
-                    turn = twist[r, at:at + GROUP, :], twist[r, at + GROUP:at + 2 * GROUP, :]
-                    far = sums[r, at:at + GROUP, width:], sums[r, at + GROUP:at + 2 * GROUP, width:]
-                    far = rotate(turn, far)
-                    real = sums[r, at:at + GROUP, :width] + far[0]
-                    imag = sums[r, at + GROUP:at + 2 * GROUP, :width] + far[1]
-                    usable = wave <= (row_points[r] - 1) // 2
-                    even = jnp.where(north, real, pltpu.roll(imag, width // 2, 1))
-                    odd = jnp.where(north, pltpu.roll(real, width // 2, 1), imag)
-                    for parity, block in enumerate((even, odd)):
-                        to = (((g * 2 + side) * 2 + parity) * rows + r) * GROUP
-                        outs[peer][to:to + GROUP, :] = jnp.where(usable, block, 0.0)
-
-
-def fourier_sums(row_points, factor, mine, theirs, groups, first_group, peers, pair_count):
-    rows = row_points.shape[0]
-    depth = factor.shape[3] - 128
+            for g in range(groups):
+                at = tail + first_group + g
+                base = rotate(head, (factor[r, 0, at:at + 1, :], factor[r, 1, at:at + 1, :]))
+                first = rotate(base, near)
+                second = rotate(last, (first[0], -first[1]))
+                block = jnp.concatenate([*first, *second], axis=0)
+                lines = slice(peer * size + g * 4 * GROUP, peer * size + (g + 1) * 4 * GROUP)
+                high, low = split(block[:, :body])
+                for part, piece in enumerate((high, high, low)):
+                    table[lines, part * body:(part + 1) * body] = piece
+                if rest:
+                    end = block[:, body:body + extra]
+                    end = jnp.where(whole, end, end - end.astype(BF16).astype(F32))
+                    table[lines, 3 * body:] = end.astype(BF16)
+                twist[lines, :] = block[:, body + extra:]
+        sums[...] = jnp.dot(table[...], values[...], preferred_element_type=F32)
+    for r in range(rows):
+        values, table, sums, twist = scratch[4 * r:4 * r + 4]
+        length = factor[r, 0, tail - 1:tail, :width]
+        for peer in range(peers):
+            for g in range(groups):
+                base = (set_index ^ (2 * peer)) * pair_count + (first_group + g) * GROUP
+                for side in range(2):
+                    wave = base + sub
+                    wave = TRUNC - wave if side else wave
+                    usable = (2 * wave + 1).astype(F32) <= length
+                    at = ((peer * groups + g) * 2 + side) * 2 * GROUP
+                    real, imag = slice(at, at + GROUP), slice(at + GROUP, at + 2 * GROUP)
+                    far = rotate((twist[real, :], twist[imag, :]), (sums[real, width:], sums[imag, width:]))
+                    for e, lines in enumerate((real, imag)):
+                        to = (((g * 2 + side) * 2 + e) * rows + r) * GROUP
+                        outs[peer][to:to + GROUP, :] = jnp.where(usable, sums[lines, :width] + far[e], 0.0)
+
+
+def fourier_sums(factor, mine, theirs, groups, first_group, peers, pair_count):
+    rows = factor.shape[0]
     width = mine.shape[1]
+    body, _, extra = layout(mine.shape[0] // rows)
     out_rows = groups * 4 * rows * GROUP
     tall = peers * groups * 4 * GROUP
     vmem = pl.BlockSpec(memory_space=pltpu.VMEM)
     return pl.pallas_call(
         functools.partial(fourier_kernel, groups, first_group, peers, pair_count),
         out_shape=[jax.ShapeDtypeStruct((out_rows, width), F32)] * peers,
-        in_specs=[pl.BlockSpec(memory_space=pltpu.SMEM)] + [vmem] * 3,
+        in_specs=[vmem] * 3,
         out_specs=[vmem] * peers,
         scratch_shapes=[
-            pltpu.VMEM((rows, 3 * depth, 2 * width), BF16),
-            pltpu.VMEM((rows, tall, 3 * depth), BF16),
-            pltpu.VMEM((rows, tall, 2 * width), F32),
-            pltpu.VMEM((rows, tall, 128), F32),
-            pltpu.VMEM((rows, 2, peers * round_up(pl.cdiv(pair_count, GROUP), GROUP), depth + 128), F32),
-        ],
+            pltpu.VMEM((3 * body + extra, 2 * width), BF16),
+            pltpu.VMEM((tall, 3 * body + extra), BF16),
+            pltpu.VMEM((tall, 2 * width), F32),
+            pltpu.VMEM((tall, 128), F32),
+        ] * rows,
         compiler_params=pltpu.CompilerParams(vmem_limit_bytes=VMEM),
         cost_estimate=micros(3),
         name="fourier_sums",
-    )(row_points, factor, mine, theirs)
+    )(factor, mine, theirs)
 
 
 def weights_kernel(rows, bands, legend, out):
@@ -234,6 +245,19 @@
     )(legend)
 
 
+def arrange(block):
+    width = block.shape[1]
+    tall = block.shape[0] // 4
+    north = lax.broadcasted_iota(jnp.int32, (1, width), 1) < width // 2
+    done = []
+    for side in range(2):
+        real = block[2 * side * tall:(2 * side + 1) * tall, :].astype(F32)
+        imag = block[(2 * side + 1) * tall:(2 * side + 2) * tall, :].astype(F32)
+        done.append(jnp.where(north, real, pltpu.roll(imag, width // 2, 1)))
+        done.append(jnp.where(north, pltpu.roll(real, width // 2, 1), imag))
+    return jnp.concatenate(done, axis=0).astype(BF16)
+
+
 def spectra_kernel(bands, first_group, pairs, weights, *refs):
     held = refs[:bands]
     out, block, sems = refs[-3:]
@@ -245,7 +269,7 @@
     masks = [jnp.tile((member == i).astype(F32).astype(BF16), (bands * part // (2 * GROUP), 1)) for i in range(GROUP)]
     copies = []
     for g in range(groups):
-        stacked = jnp.concatenate([ref[g * part:(g + 1) * part, :] for ref in held], axis=0)
+        stacked = jnp.concatenate([arrange(ref[g * part:(g + 1) * part, :]) for ref in held], axis=0)
         for at in range(0, min(GROUP, pairs - g * GROUP), 2):
             both = jnp.concatenate([stacked * masks[at], stacked * masks[at + 1]], axis=1)
             product = jnp.dot(weights[first_group + g], both, preferred_element_type=F32)
@@ -302,14 +326,14 @@
     factor = prepare(row_points, points, peers, pair_count)
     legend = lax.dynamic_slice_in_dim(legendre, lax.axis_index("band") * slots, slots, 2)
     legend, theirs = lax.optimization_barrier((legend, theirs))
-    weights = spread_weights(legend, rows, band_size)
+    weights = None
     all_groups = pl.cdiv(pair_count, GROUP)
     cut = (all_groups + 1) // 2
     chunks = ((0, cut), (cut, all_groups - cut))
     gathered = []
     partial = []
     for first_group, groups in chunks:
-        partial.append(fourier_sums(row_points, factor, flat, theirs, groups, first_group, peers, pair_count))
+        partial.append(fourier_sums(factor, flat, theirs, groups, first_group, peers, pair_count))
     for parts in partial:
         steps = list(range(1, peers))
         steps = steps[::-1] if gathered else steps[::2] + steps[1::2]
@@ -320,6 +344,9 @@
         for part in arrived:
             total = total + part.astype(F32)
         rounded = total.astype(BF16)
+        if not gathered:
+            legend, rounded = lax.optimization_barrier((legend, rounded))
+            weights = spread_weights(legend, rows, band_size)
         turns = list(range(1, band_size))
         gathered.append([rounded] + exchange([rounded] * len(turns), "band", turns))
     out = None

time: 38.6 us -> 37.3 us (0.966)
  local copies, waits for them, and re-layouts: 1.77 us -> 1.12 us
  waiting for transfers between devices: 2.3 us -> 1.79 us
    unnamed x8 -> x6, local copies, waits for them, and re-layouts: 1.53 us -> 0.88 us
    ppermute x12, waiting for transfers between devices: 2.3 us -> 1.79 us  [exchange(): lax.ppermute(part, axis, swap(axis, lax.axis_size(axis), step))]
  transfers between devices with their start and end apart: 13 -> 13, of which waited for: 3 -> 2; matrix products, arithmetic and copies ran while one was open for 1% -> 1% of each run, Pallas kernels for 24% -> 24%
where the time goes in v6:
time: 37.3 us; the launch traced here: 37.1 us
  starting transfers between devices  17.8 us (48%)
  Pallas kernels  16.1 us (43%)
  waiting for transfers between devices  1.79 us (5%)
  local copies, waits for them, and re-layouts  1.12 us (3%)
    ppermute x12, starting transfers between devices, exchange(): lax.ppermute(part, axis, swap(axis, lax.axis_size(axis), step))  17.3 us
    pallas_call x2, Pallas kernels, fourier_sums(): pl.pallas_call(functools.partial(fourier_kernel, groups, first_group, pee...  7.3 us
    pallas_call x2, Pallas kernels, spectra_part(): pl.pallas_call(functools.partial(spectra_kernel, bands, first_group, pair...  6.85 us
    ppermute x12, waiting for transfers between devices, exchange(): lax.ppermute(part, axis, swap(axis, lax.axis_size(axis), step))  1.79 us
    pallas_call x1, Pallas kernels, spread_weights(): pl.pallas_call(functools.partial(weights_kernel, rows, bands), out_shape=...  0.97 us
    pallas_call x1, Pallas kernels, prepare(): pl.pallas_call(functools.partial(prepare_kernel, peers, pair_count, point...  0.96 us
    unnamed x6, local copies, waits for them, and re-layouts  0.88 us
  transfers between devices with their start and end apart: 13, of which 2 were waited for; matrix products, arithmetic and copies ran while one was open for 1% of the time, Pallas kernels for 24%

profile of v6, /device:TPU:0, one launch (start us, length us, event | category | flops | bytes accessed | tf_op | source)
XLA Modules:
  0.0 37.1 jit_solution(4911205624944420804)
XLA Ops:
  0.0 0.5 %collective-permute-start = (f32[1288,128]{1,0:T(8,128)}, f32[1288,128]{1,0:T(8,128)}, u32[]{:S(2)}, u32[]{:S(2)}) collective-permute-start(f32[1288,128]{1,0:T(8,128)} %bitcast.3), channel_id=1, source_target_pairs={{0,1},{1,0},{2,3},{3,2},{4,5},{5,4},{6,7},{7,6},{8,9},{9,8},{10,11... | collective-permute-start | bytes 1978376 | tf_op jit(solution)/shard_map/ppermute | solution.py:325
  0.5 0.9 %copy-done.2 = s32[2]{0:T(128)S(1)} copy-done((s32[2]{0:T(128)S(1)}, s32[2]{0:T(128)}, u32[]{:S(2)}) %copy-start.2) | copy-done | bytes 32
  1.3 1.0 %prepare.1.factor = f32[2,2,32,896]{3,2,1,0:T(8,128)S(1)} custom-call(s32[2]{0:T(128)S(1)} %copy-done.2), custom_call_target="tpu_custom_call" | custom-call | bytes 3000000 | tf_op jit(solution)/shard_map/prepare/pallas_call | solution.py:112
  2.3 0.2 constant_dynamic-slice_fusion.legend
  2.6 0.0 collective-permute-done.theirs
  2.6 3.7 %fourier_sums.3 = (f32[320,128]{1,0:T(8,128)S(1)}, f32[320,128]{1,0:T(8,128)S(1)}, f32[320,128]{1,0:T(8,128)S(1)}, f32[320,128]{1,0:T(8,128)S(1)}) custom-call(f32[2,2,32,896]{3,2,1,0:T(8,128)S(1)} %prepare.1.factor, f32[1288,128]{1,0:T(8,128)S(1)} %bitcast.4, f32[1288,128]{1,0:T(8,128)} %collective-permute-done.theirs), custom_call_target="tpu_custom_call" | custom-call | bytes 9000000 | tf_op jit(solution)/shard_map/fourier_sums/pallas_call | solution.py:187
  6.3 4.0 %collective-permute-start.6 = (f16[320,128]{1,0:T(8,128)(2,1)S(1)}, f16[320,128]{1,0:T(8,128)(2,1)S(1)}, u32[]{:S(2)}, u32[]{:S(2)}) collective-permute-start(f16[320,128]{1,0:T(8,128)(2,1)S(1)} %convert_element_type.49), channel_id=1, source_target_pairs={{0,4},{1,5},{2,6},{3,7},{4,0},{5,1},{6,2},{7,3},{8,12},{9,13},{10,... | collective-permute-start | bytes 245768 | tf_op jit(solution)/shard_map/ppermute | solution.py:314
  10.3 1.4 %collective-permute-start.5 = (f16[320,128]{1,0:T(8,128)(2,1)S(1)}, f16[320,128]{1,0:T(8,128)(2,1)S(1)}, u32[]{:S(2)}, u32[]{:S(2)}) collective-permute-start(f16[320,128]{1,0:T(8,128)(2,1)S(1)} %convert_element_type.47), channel_id=1, source_target_pairs={{0,6},{1,7},{2,4},{3,5},{4,2},{5,3},{6,0},{7,1},{8,14},{9,15},{10,... | collective-permute-start | bytes 245768 | tf_op jit(solution)/shard_map/ppermute | solution.py:314
  11.7 0.3 collective-permute-start.4
  12.0 3.6 %fourier_sums.2 = (f32[320,128]{1,0:T(8,128)S(1)}, f32[320,128]{1,0:T(8,128)S(1)}, f32[320,128]{1,0:T(8,128)S(1)}, f32[320,128]{1,0:T(8,128)S(1)}) custom-call(f32[2,2,32,896]{3,2,1,0:T(8,128)S(1)} %prepare.1.factor, f32[1288,128]{1,0:T(8,128)S(1)} %bitcast.5, f32[1288,128]{1,0:T(8,128)} %collective-permute-done.theirs), custom_call_target="tpu_custom_call" | custom-call | bytes 9000000 | tf_op jit(solution)/shard_map/fourier_sums/pallas_call | solution.py:187
  15.7 1.8 %collective-permute-start.3 = (f16[320,128]{1,0:T(8,128)(2,1)S(1)}, f16[320,128]{1,0:T(8,128)(2,1)S(1)}, u32[]{:S(2)}, u32[]{:S(2)}) collective-permute-start(f16[320,128]{1,0:T(8,128)(2,1)S(1)} %convert_element_type.44), channel_id=1, source_target_pairs={{0,2},{1,3},{2,0},{3,1},{4,6},{5,7},{6,4},{7,5},{8,10},{9,11},{10,... | collective-permute-start | bytes 245768 | tf_op jit(solution)/shard_map/ppermute | solution.py:314
  17.5 1.7 %collective-permute-start.2 = (f16[320,128]{1,0:T(8,128)(2,1)S(1)}, f16[320,128]{1,0:T(8,128)(2,1)S(1)}, u32[]{:S(2)}, u32[]{:S(2)}) collective-permute-start(f16[320,128]{1,0:T(8,128)(2,1)S(1)} %convert_element_type.43), channel_id=1, source_target_pairs={{0,4},{1,5},{2,6},{3,7},{4,0},{5,1},{6,2},{7,3},{8,12},{9,13},{10,... | collective-permute-start | bytes 245768 | tf_op jit(solution)/shard_map/ppermute | solution.py:314
  19.2 0.0 collective-permute-done.6
  19.2 1.0 %collective-permute-start.1 = (f16[320,128]{1,0:T(8,128)(2,1)S(1)}, f16[320,128]{1,0:T(8,128)(2,1)S(1)}, u32[]{:S(2)}, u32[]{:S(2)}) collective-permute-start(f16[320,128]{1,0:T(8,128)(2,1)S(1)} %convert_element_type.42), channel_id=1, source_target_pairs={{0,6},{1,7},{2,4},{3,5},{4,2},{5,3},{6,0},{7,1},{8,14},{9,15},{10,... | collective-permute-start | bytes 245768 | tf_op jit(solution)/shard_map/ppermute | solution.py:314
  20.2 0.0 collective-permute-done.5
  20.2 0.0 collective-permute-done.4
  20.2 2.5 %collective-permute-start.12 = (bf16[320,128]{1,0:T(8,128)(2,1)S(1)}, bf16[320,128]{1,0:T(8,128)(2,1)S(1)}, u32[]{:S(2)}, u32[]{:S(2)}) collective-permute-start(bf16[320,128]{1,0:T(8,128)(2,1)S(1)} %add_convert_fusion.1.refs_0_), channel_id=1, source_target_pairs={{0,24},{8,16},{16,8},{24,0},{1,25},{9,17},{17,9},{25,1},{2,26},{10... | collective-permute-start | bytes 245768 | tf_op jit(solution)/shard_map/ppermute | solution.py:314
  22.7 0.5 %collective-permute-start.11 = (bf16[320,128]{1,0:T(8,128)(2,1)S(1)}, bf16[320,128]{1,0:T(8,128)(2,1)S(1)}, u32[]{:S(2)}, u32[]{:S(2)}) collective-permute-start(bf16[320,128]{1,0:T(8,128)(2,1)S(1)} %add_convert_fusion.1.refs_0_), channel_id=1, source_target_pairs={{0,16},{8,24},{16,0},{24,8},{1,17},{9,25},{17,1},{25,9},{2,18},{10... | collective-permute-start | bytes 245768 | tf_op jit(solution)/shard_map/ppermute | solution.py:314
  23.2 1.0 %spread_weights.1.weights = bf16[10,352,256]{2,1,0:T(8,128)(2,1)S(1)} custom-call(bf16[80,8,352]{2,1,0:T(8,128)(2,1)S(1)} %constant_dynamic-slice_fusion.legend), custom_call_target="tpu_custom_call" | custom-call | bytes 3000000 | tf_op jit(solution)/shard_map/spread_weights/pallas_call | solution.py:237
  24.2 0.0 collective-permute-done.3
  24.2 0.6 %collective-permute-start.10 = (bf16[320,128]{1,0:T(8,128)(2,1)S(1)}, bf16[320,128]{1,0:T(8,128)(2,1)S(1)}, u32[]{:S(2)}, u32[]{:S(2)}) collective-permute-start(bf16[320,128]{1,0:T(8,128)(2,1)S(1)} %add_convert_fusion.1.refs_0_), channel_id=1, source_target_pairs={{0,8},{8,0},{16,24},{24,16},{1,9},{9,1},{17,25},{25,17},{2,10},{10... | collective-permute-start | bytes 245768 | tf_op jit(solution)/shard_map/ppermute | solution.py:314
  24.8 1.3 %collective-permute-done.2 = f16[320,128]{1,0:T(8,128)(2,1)S(1)} collective-permute-done((f16[320,128]{1,0:T(8,128)(2,1)S(1)}, f16[320,128]{1,0:T(8,128)(2,1)S(1)}, u32[]{:S(2)}, u32[]{:S(2)}) %collective-permute-start.2) | collective-permute-done | bytes 81952 | tf_op jit(solution)/shard_map/ppermute | solution.py:314
  26.2 0.0 collective-permute-done.1
  26.2 2.5 %collective-permute-start.9 = (bf16[320,128]{1,0:T(8,128)(2,1)S(1)}, bf16[320,128]{1,0:T(8,128)(2,1)S(1)}, u32[]{:S(2)}, u32[]{:S(2)}) collective-permute-start(bf16[320,128]{1,0:T(8,128)(2,1)S(1)} %add_convert_fusion.refs_0_), channel_id=1, source_target_pairs={{0,24},{8,16},{16,8},{24,0},{1,25},{9,17},{17,9},{25,1},{2,26},{10... | collective-permute-start | bytes 245768 | tf_op jit(solution)/shard_map/ppermute | solution.py:314
  28.7 0.5 %collective-permute-start.8 = (bf16[320,128]{1,0:T(8,128)(2,1)S(1)}, bf16[320,128]{1,0:T(8,128)(2,1)S(1)}, u32[]{:S(2)}, u32[]{:S(2)}) collective-permute-start(bf16[320,128]{1,0:T(8,128)(2,1)S(1)} %add_convert_fusion.refs_0_), channel_id=1, source_target_pairs={{0,16},{8,24},{16,0},{24,8},{1,17},{9,25},{17,1},{25,9},{2,18},{10... | collective-permute-start | bytes 245768 | tf_op jit(solution)/shard_map/ppermute | solution.py:314
  29.2 0.0 collective-permute-done.12.refs_3_
  29.2 0.5 %collective-permute-start.7 = (bf16[320,128]{1,0:T(8,128)(2,1)S(1)}, bf16[320,128]{1,0:T(8,128)(2,1)S(1)}, u32[]{:S(2)}, u32[]{:S(2)}) collective-permute-start(bf16[320,128]{1,0:T(8,128)(2,1)S(1)} %add_convert_fusion.refs_0_), channel_id=1, source_target_pairs={{0,8},{8,0},{16,24},{24,16},{1,9},{9,1},{17,25},{25,17},{2,10},{10... | collective-permute-start | bytes 245768 | tf_op jit(solution)/shard_map/ppermute | solution.py:314
  29.8 0.0 collective-permute-done.11.refs_2_
  29.8 0.0 collective-permute-done.10.refs_1_
  29.8 3.4 %spectra_part.2.refs_4_ = f32[80,352,128]{2,1,0:T(8,128)} custom-call(bf16[10,352,256]{2,1,0:T(8,128)(2,1)S(1)} %spread_weights.1.weights, bf16[320,128]{1,0:T(8,128)(2,1)S(1)} %add_convert_fusion.1.refs_0_, bf16[320,128]{1,0:T(8,128)(2,1)S(1)} %collective-permute-done.10.refs_1_, bf16[320,128]{1,0:T(8,128)(2,1)S(1)} %collective-permute-done.11.refs_2_, ...), custom_call_target="tpu_custom_call" | custom-call | bytes 9000000 | tf_op jit(solution)/shard_map/spectra_part/pallas_call | solution.py:296
  33.2 0.4 %collective-permute-done.7.refs_1_ = bf16[320,128]{1,0:T(8,128)(2,1)S(1)} collective-permute-done((bf16[320,128]{1,0:T(8,128)(2,1)S(1)}, bf16[320,128]{1,0:T(8,128)(2,1)S(1)}, u32[]{:S(2)}, u32[]{:S(2)}) %collective-permute-start.7) | collective-permute-done | bytes 81952 | tf_op jit(solution)/shard_map/ppermute | solution.py:314
  33.7 3.4 %spectra_part.3 = f32[80,352,128]{2,1,0:T(8,128)} custom-call(bf16[10,352,256]{2,1,0:T(8,128)(2,1)S(1)} %spread_weights.1.weights, bf16[320,128]{1,0:T(8,128)(2,1)S(1)} %add_convert_fusion.refs_0_, bf16[320,128]{1,0:T(8,128)(2,1)S(1)} %collective-permute-done.7.refs_1_, ...), custom_call_target="tpu_custom_call", output_to_operand_aliasing={{}: (5, {})} | custom-call | bytes 9000000 | tf_op jit(solution)/shard_map/spectra_part/pallas_call | solution.py:296
  (15 shorter events, 0.2 us)
Async XLA Ops:
  0.0 2.3 %copy-start = (bf16[80,8,1408]{2,1,0:T(8,128)(2,1)S(1)}, bf16[80,8,1408]{2,1,0:T(8,128)(2,1)}, u32[]{:S(2)}) copy-start(bf16[80,8,1408]{2,1,0:T(8,128)(2,1)} %param.5) | copy-start | bytes 5406724
  0.0 2.6 %copy-start.1 = (f32[2,644,128]{2,0,1:T(2,128)S(1)}, f32[2,644,128]{2,0,1:T(2,128)}, u32[]{:S(2)}) copy-start(f32[2,644,128]{2,0,1:T(2,128)} %param.3) | copy-start | bytes 1978372
  0.0 2.6 %collective-permute-start = (f32[1288,128]{1,0:T(8,128)}, f32[1288,128]{1,0:T(8,128)}, u32[]{:S(2)}, u32[]{:S(2)}) collective-permute-start(f32[1288,128]{1,0:T(8,128)} %bitcast.3), channel_id=1, source_target_pairs={{0,1},{1,0},{2,3},{3,2},{4,5},{5,4},{6,7},{7,6},{8,9},{9,8},{10,11... | collective-permute-start | bytes 1978376 | tf_op jit(solution)/shard_map/ppermute | solution.py:325
  0.5 0.9 %copy-start.2 = (s32[2]{0:T(128)S(1)}, s32[2]{0:T(128)}, u32[]{:S(2)}) copy-start(s32[2]{0:T(128)} %row_points.1) | copy-start | bytes 28
  6.3 12.9 %collective-permute-start.6 = (f16[320,128]{1,0:T(8,128)(2,1)S(1)}, f16[320,128]{1,0:T(8,128)(2,1)S(1)}, u32[]{:S(2)}, u32[]{:S(2)}) collective-permute-start(f16[320,128]{1,0:T(8,128)(2,1)S(1)} %convert_element_type.49), channel_id=1, source_target_pairs={{0,4},{1,5},{2,6},{3,7},{4,0},{5,1},{6,2},{7,3},{8,12},{9,13},{10,... | collective-permute-start | bytes 245768 | tf_op jit(solution)/shard_map/ppermute | solution.py:314
  10.3 9.9 %collective-permute-start.5 = (f16[320,128]{1,0:T(8,128)(2,1)S(1)}, f16[320,128]{1,0:T(8,128)(2,1)S(1)}, u32[]{:S(2)}, u32[]{:S(2)}) collective-permute-start(f16[320,128]{1,0:T(8,128)(2,1)S(1)} %convert_element_type.47), channel_id=1, source_target_pairs={{0,6},{1,7},{2,4},{3,5},{4,2},{5,3},{6,0},{7,1},{8,14},{9,15},{10,... | collective-permute-start | bytes 245768 | tf_op jit(solution)/shard_map/ppermute | solution.py:314
  11.7 8.5 %collective-permute-start.4 = (f16[320,128]{1,0:T(8,128)(2,1)S(1)}, f16[320,128]{1,0:T(8,128)(2,1)S(1)}, u32[]{:S(2)}, u32[]{:S(2)}) collective-permute-start(f16[320,128]{1,0:T(8,128)(2,1)S(1)} %convert_element_type.45), channel_id=1, source_target_pairs={{0,2},{1,3},{2,0},{3,1},{4,6},{5,7},{6,4},{7,5},{8,10},{9,11},{10,... | collective-permute-start | bytes 245768 | tf_op jit(solution)/shard_map/ppermute | solution.py:314
  15.7 8.5 %collective-permute-start.3 = (f16[320,128]{1,0:T(8,128)(2,1)S(1)}, f16[320,128]{1,0:T(8,128)(2,1)S(1)}, u32[]{:S(2)}, u32[]{:S(2)}) collective-permute-start(f16[320,128]{1,0:T(8,128)(2,1)S(1)} %convert_element_type.44), channel_id=1, source_target_pairs={{0,2},{1,3},{2,0},{3,1},{4,6},{5,7},{6,4},{7,5},{8,10},{9,11},{10,... | collective-permute-start | bytes 245768 | tf_op jit(solution)/shard_map/ppermute | solution.py:314
  17.5 8.7 %collective-permute-start.2 = (f16[320,128]{1,0:T(8,128)(2,1)S(1)}, f16[320,128]{1,0:T(8,128)(2,1)S(1)}, u32[]{:S(2)}, u32[]{:S(2)}) collective-permute-start(f16[320,128]{1,0:T(8,128)(2,1)S(1)} %convert_element_type.43), channel_id=1, source_target_pairs={{0,4},{1,5},{2,6},{3,7},{4,0},{5,1},{6,2},{7,3},{8,12},{9,13},{10,... | collective-permute-start | bytes 245768 | tf_op jit(solution)/shard_map/ppermute | solution.py:314
  19.2 7.0 %collective-permute-start.1 = (f16[320,128]{1,0:T(8,128)(2,1)S(1)}, f16[320,128]{1,0:T(8,128)(2,1)S(1)}, u32[]{:S(2)}, u32[]{:S(2)}) collective-permute-start(f16[320,128]{1,0:T(8,128)(2,1)S(1)} %convert_element_type.42), channel_id=1, source_target_pairs={{0,6},{1,7},{2,4},{3,5},{4,2},{5,3},{6,0},{7,1},{8,14},{9,15},{10,... | collective-permute-start | bytes 245768 | tf_op jit(solution)/shard_map/ppermute | solution.py:314
  20.2 9.0 %collective-permute-start.12 = (bf16[320,128]{1,0:T(8,128)(2,1)S(1)}, bf16[320,128]{1,0:T(8,128)(2,1)S(1)}, u32[]{:S(2)}, u32[]{:S(2)}) collective-permute-start(bf16[320,128]{1,0:T(8,128)(2,1)S(1)} %add_convert_fusion.1.refs_0_), channel_id=1, source_target_pairs={{0,24},{8,16},{16,8},{24,0},{1,25},{9,17},{17,9},{25,1},{2,26},{10... | collective-permute-start | bytes 245768 | tf_op jit(solution)/shard_map/ppermute | solution.py:314
  22.7 7.0 %collective-permute-start.11 = (bf16[320,128]{1,0:T(8,128)(2,1)S(1)}, bf16[320,128]{1,0:T(8,128)(2,1)S(1)}, u32[]{:S(2)}, u32[]{:S(2)}) collective-permute-start(bf16[320,128]{1,0:T(8,128)(2,1)S(1)} %add_convert_fusion.1.refs_0_), channel_id=1, source_target_pairs={{0,16},{8,24},{16,0},{24,8},{1,17},{9,25},{17,1},{25,9},{2,18},{10... | collective-permute-start | bytes 245768 | tf_op jit(solution)/shard_map/ppermute | solution.py:314
  24.2 5.5 %collective-permute-start.10 = (bf16[320,128]{1,0:T(8,128)(2,1)S(1)}, bf16[320,128]{1,0:T(8,128)(2,1)S(1)}, u32[]{:S(2)}, u32[]{:S(2)}) collective-permute-start(bf16[320,128]{1,0:T(8,128)(2,1)S(1)} %add_convert_fusion.1.refs_0_), channel_id=1, source_target_pairs={{0,8},{8,0},{16,24},{24,16},{1,9},{9,1},{17,25},{25,17},{2,10},{10... | collective-permute-start | bytes 245768 | tf_op jit(solution)/shard_map/ppermute | solution.py:314
  26.2 7.0 %collective-permute-start.9 = (bf16[320,128]{1,0:T(8,128)(2,1)S(1)}, bf16[320,128]{1,0:T(8,128)(2,1)S(1)}, u32[]{:S(2)}, u32[]{:S(2)}) collective-permute-start(bf16[320,128]{1,0:T(8,128)(2,1)S(1)} %add_convert_fusion.refs_0_), channel_id=1, source_target_pairs={{0,24},{8,16},{16,8},{24,0},{1,25},{9,17},{17,9},{25,1},{2,26},{10... | collective-permute-start | bytes 245768 | tf_op jit(solution)/shard_map/ppermute | solution.py:314
  28.7 4.5 %collective-permute-start.8 = (bf16[320,128]{1,0:T(8,128)(2,1)S(1)}, bf16[320,128]{1,0:T(8,128)(2,1)S(1)}, u32[]{:S(2)}, u32[]{:S(2)}) collective-permute-start(bf16[320,128]{1,0:T(8,128)(2,1)S(1)} %add_convert_fusion.refs_0_), channel_id=1, source_target_pairs={{0,16},{8,24},{16,0},{24,8},{1,17},{9,25},{17,1},{25,9},{2,18},{10... | collective-permute-start | bytes 245768 | tf_op jit(solution)/shard_map/ppermute | solution.py:314
  29.2 4.4 %collective-permute-start.7 = (bf16[320,128]{1,0:T(8,128)(2,1)S(1)}, bf16[320,128]{1,0:T(8,128)(2,1)S(1)}, u32[]{:S(2)}, u32[]{:S(2)}) collective-permute-start(bf16[320,128]{1,0:T(8,128)(2,1)S(1)} %add_convert_fusion.refs_0_), channel_id=1, source_target_pairs={{0,8},{8,0},{16,24},{24,16},{1,9},{9,1},{17,25},{25,17},{2,10},{10... | collective-permute-start | bytes 245768 | tf_op jit(solution)/shard_map/ppermute | solution.py:314

commit v7 on v6

--- a/solution.py
+++ b/solution.py
@@ -88,7 +88,7 @@
     slot = lax.broadcasted_iota(jnp.int32, (1, wide), 1)
     point = start + jnp.where(slot < body, slot, body + (slot - body) % max(rest, 1))
     point = jnp.where(slot < body + extra, point, beside)
-    heads = round_up(peers + 1, GROUP)
+    heads = peers + 2
     sub = lax.broadcasted_iota(jnp.int32, (tall, 1), 0)
     order = sub - GROUP
     head = jnp.where(order < peers, (set_index ^ (2 * order)) * pair_count, TRUNC)
@@ -103,7 +103,8 @@
 
 
 def table_rows(peers, pair_count):
-    return GROUP + round_up(peers + 2, GROUP), round_up(pl.cdiv(pair_count, GROUP), GROUP)
+    heads, groups = peers + 2, pl.cdiv(pair_count, GROUP)
+    return GROUP + heads, round_up(heads + groups, GROUP) - heads
 
 
 def prepare(row_points, points, peers, pair_count):

time: 37.3 us -> 36.4 us (0.976)
  Pallas kernels: 16.1 us -> 13.8 us
  starting transfers between devices: 17.8 us -> 18.9 us
  local copies, waits for them, and re-layouts: 1.12 us -> 2.07 us
  waiting for transfers between devices: 1.79 us -> 1.08 us
    pallas_call x2, Pallas kernels: 7.3 us -> 5.15 us  [fourier_sums(): pl.pallas_call(functools.partial(fourier_kernel, groups, first_group, pee...]
    ppermute x12, starting transfers between devices: 17.3 us -> 18.4 us  [exchange(): lax.ppermute(part, axis, swap(axis, lax.axis_size(axis), step))]
    unnamed x6, local copies, waits for them, and re-layouts: 0.88 us -> 1.83 us
    ppermute x12, waiting for transfers between devices: 1.79 us -> 1 us  [exchange(): lax.ppermute(part, axis, swap(axis, lax.axis_size(axis), step))]
  transfers between devices with their start and end apart: 13 -> 13, of which waited for: 2 -> 3; matrix products, arithmetic and copies ran while one was open for 1% -> 1% of each run, Pallas kernels for 24% -> 22%
where the time goes in v7:
time: 36.4 us; the launch traced here: 36.2 us
  starting transfers between devices  18.9 us (52%)
  Pallas kernels  13.8 us (38%)
  local copies, waits for them, and re-layouts  2.07 us (6%)
  waiting for transfers between devices  1.08 us (3%)
    ppermute x12, starting transfers between devices, exchange(): lax.ppermute(part, axis, swap(axis, lax.axis_size(axis), step))  18.4 us
    pallas_call x2, Pallas kernels, spectra_part(): pl.pallas_call(functools.partial(spectra_kernel, bands, first_group, pair...  6.85 us
    pallas_call x2, Pallas kernels, fourier_sums(): pl.pallas_call(functools.partial(fourier_kernel, groups, first_group, pee...  5.15 us
    unnamed x6, local copies, waits for them, and re-layouts  1.83 us
    ppermute x12, waiting for transfers between devices, exchange(): lax.ppermute(part, axis, swap(axis, lax.axis_size(axis), step))  1 us
    pallas_call x1, Pallas kernels, spread_weights(): pl.pallas_call(functools.partial(weights_kernel, rows, bands), out_shape=...  0.97 us
    pallas_call x1, Pallas kernels, prepare(): pl.pallas_call(functools.partial(prepare_kernel, peers, pair_count, point...  0.86 us
  transfers between devices with their start and end apart: 13, of which 3 were waited for; matrix products, arithmetic and copies ran while one was open for 1% of the time, Pallas kernels for 22%

profile of v7, /device:TPU:0, one launch (start us, length us, event | category | flops | bytes accessed | tf_op | source)
XLA Modules:
  0.0 36.2 jit_solution(12712679221418230414)
XLA Ops:
  0.0 0.5 %collective-permute-start = (f32[1288,128]{1,0:T(8,128)}, f32[1288,128]{1,0:T(8,128)S(1)}, u32[]{:S(2)}, u32[]{:S(2)}) collective-permute-start(f32[1288,128]{1,0:T(8,128)} %bitcast.3), channel_id=1, source_target_pairs={{0,1},{1,0},{2,3},{3,2},{4,5},{5,4},{6,7},{7,6},{8,9},{9,8},{10,11... | collective-permute-start | bytes 1978376 | tf_op jit(solution)/shard_map/ppermute | solution.py:326
  0.5 0.7 %copy-done.2 = s32[2]{0:T(128)S(1)} copy-done((s32[2]{0:T(128)S(1)}, s32[2]{0:T(128)}, u32[]{:S(2)}) %copy-start.2) | copy-done | bytes 32
  1.2 0.9 %prepare.1.factor = f32[2,2,24,896]{3,2,1,0:T(8,128)S(1)} custom-call(s32[2]{0:T(128)S(1)} %copy-done.2), custom_call_target="tpu_custom_call" | custom-call | bytes 3000000 | tf_op jit(solution)/shard_map/prepare/pallas_call | solution.py:113
  2.1 0.2 constant_dynamic-slice_fusion.legend
  2.3 0.1 collective-permute-done.theirs
  2.4 1.1 %copy-done.1 = f32[2,644,128]{2,0,1:T(2,128)S(1)} copy-done((f32[2,644,128]{2,0,1:T(2,128)S(1)}, f32[2,644,128]{2,0,1:T(2,128)}, u32[]{:S(2)}) %copy-start.1) | copy-done | bytes 659480
  3.5 2.6 %fourier_sums.3 = (f32[320,128]{1,0:T(8,128)S(1)}, f32[320,128]{1,0:T(8,128)S(1)}, f32[320,128]{1,0:T(8,128)S(1)}, f32[320,128]{1,0:T(8,128)S(1)}) custom-call(f32[2,2,24,896]{3,2,1,0:T(8,128)S(1)} %prepare.1.factor, f32[1288,128]{1,0:T(8,128)S(1)} %bitcast.4, f32[1288,128]{1,0:T(8,128)S(1)} %collective-permute-done.theirs), custom_call_target="tpu_custom_call" | custom-call | bytes 9000000 | tf_op jit(solution)/shard_map/fourier_sums/pallas_call | solution.py:188
  6.1 4.0 %collective-permute-start.6 = (f16[320,128]{1,0:T(8,128)(2,1)S(1)}, f16[320,128]{1,0:T(8,128)(2,1)S(1)}, u32[]{:S(2)}, u32[]{:S(2)}) collective-permute-start(f16[320,128]{1,0:T(8,128)(2,1)S(1)} %convert_element_type.49), channel_id=1, source_target_pairs={{0,4},{1,5},{2,6},{3,7},{4,0},{5,1},{6,2},{7,3},{8,12},{9,13},{10,... | collective-permute-start | bytes 245768 | tf_op jit(solution)/shard_map/ppermute | solution.py:315
  10.2 1.4 %collective-permute-start.5 = (f16[320,128]{1,0:T(8,128)(2,1)S(1)}, f16[320,128]{1,0:T(8,128)(2,1)S(1)}, u32[]{:S(2)}, u32[]{:S(2)}) collective-permute-start(f16[320,128]{1,0:T(8,128)(2,1)S(1)} %convert_element_type.47), channel_id=1, source_target_pairs={{0,6},{1,7},{2,4},{3,5},{4,2},{5,3},{6,0},{7,1},{8,14},{9,15},{10,... | collective-permute-start | bytes 245768 | tf_op jit(solution)/shard_map/ppermute | solution.py:315
  11.6 0.3 collective-permute-start.4
  11.9 2.6 %fourier_sums.2 = (f32[320,128]{1,0:T(8,128)S(1)}, f32[320,128]{1,0:T(8,128)S(1)}, f32[320,128]{1,0:T(8,128)S(1)}, f32[320,128]{1,0:T(8,128)S(1)}) custom-call(f32[2,2,24,896]{3,2,1,0:T(8,128)S(1)} %prepare.1.factor, f32[1288,128]{1,0:T(8,128)S(1)} %bitcast.5, f32[1288,128]{1,0:T(8,128)S(1)} %collective-permute-done.theirs), custom_call_target="tpu_custom_call" | custom-call | bytes 9000000 | tf_op jit(solution)/shard_map/fourier_sums/pallas_call | solution.py:188
  14.5 1.8 %collective-permute-start.3 = (f16[320,128]{1,0:T(8,128)(2,1)S(1)}, f16[320,128]{1,0:T(8,128)(2,1)S(1)}, u32[]{:S(2)}, u32[]{:S(2)}) collective-permute-start(f16[320,128]{1,0:T(8,128)(2,1)S(1)} %convert_element_type.44), channel_id=1, source_target_pairs={{0,2},{1,3},{2,0},{3,1},{4,6},{5,7},{6,4},{7,5},{8,10},{9,11},{10,... | collective-permute-start | bytes 245768 | tf_op jit(solution)/shard_map/ppermute | solution.py:315
  16.3 1.7 %collective-permute-start.2 = (f16[320,128]{1,0:T(8,128)(2,1)S(1)}, f16[320,128]{1,0:T(8,128)(2,1)S(1)}, u32[]{:S(2)}, u32[]{:S(2)}) collective-permute-start(f16[320,128]{1,0:T(8,128)(2,1)S(1)} %convert_element_type.43), channel_id=1, source_target_pairs={{0,4},{1,5},{2,6},{3,7},{4,0},{5,1},{6,2},{7,3},{8,12},{9,13},{10,... | collective-permute-start | bytes 245768 | tf_op jit(solution)/shard_map/ppermute | solution.py:315
  18.0 0.0 collective-permute-done.6
  18.0 2.1 %collective-permute-start.1 = (f16[320,128]{1,0:T(8,128)(2,1)S(1)}, f16[320,128]{1,0:T(8,128)(2,1)S(1)}, u32[]{:S(2)}, u32[]{:S(2)}) collective-permute-start(f16[320,128]{1,0:T(8,128)(2,1)S(1)} %convert_element_type.42), channel_id=1, source_target_pairs={{0,6},{1,7},{2,4},{3,5},{4,2},{5,3},{6,0},{7,1},{8,14},{9,15},{10,... | collective-permute-start | bytes 245768 | tf_op jit(solution)/shard_map/ppermute | solution.py:315
  20.1 2.5 %collective-permute-start.12 = (bf16[320,128]{1,0:T(8,128)(2,1)S(1)}, bf16[320,128]{1,0:T(8,128)(2,1)S(1)}, u32[]{:S(2)}, u32[]{:S(2)}) collective-permute-start(bf16[320,128]{1,0:T(8,128)(2,1)S(1)} %add_convert_fusion.1.refs_0_), channel_id=1, source_target_pairs={{0,24},{8,16},{16,8},{24,0},{1,25},{9,17},{17,9},{25,1},{2,26},{10... | collective-permute-start | bytes 245768 | tf_op jit(solution)/shard_map/ppermute | solution.py:315
  22.6 0.5 %collective-permute-start.11 = (bf16[320,128]{1,0:T(8,128)(2,1)S(1)}, bf16[320,128]{1,0:T(8,128)(2,1)S(1)}, u32[]{:S(2)}, u32[]{:S(2)}) collective-permute-start(bf16[320,128]{1,0:T(8,128)(2,1)S(1)} %add_convert_fusion.1.refs_0_), channel_id=1, source_target_pairs={{0,16},{8,24},{16,0},{24,8},{1,17},{9,25},{17,1},{25,9},{2,18},{10... | collective-permute-start | bytes 245768 | tf_op jit(solution)/shard_map/ppermute | solution.py:315
  23.1 1.0 %spread_weights.1.weights = bf16[10,352,256]{2,1,0:T(8,128)(2,1)S(1)} custom-call(bf16[80,8,352]{2,1,0:T(8,128)(2,1)S(1)} %constant_dynamic-slice_fusion.legend), custom_call_target="tpu_custom_call" | custom-call | bytes 3000000 | tf_op jit(solution)/shard_map/spread_weights/pallas_call | solution.py:238
  24.1 0.0 collective-permute-done.3
  24.1 0.6 %collective-permute-start.10 = (bf16[320,128]{1,0:T(8,128)(2,1)S(1)}, bf16[320,128]{1,0:T(8,128)(2,1)S(1)}, u32[]{:S(2)}, u32[]{:S(2)}) collective-permute-start(bf16[320,128]{1,0:T(8,128)(2,1)S(1)} %add_convert_fusion.1.refs_0_), channel_id=1, source_target_pairs={{0,8},{8,0},{16,24},{24,16},{1,9},{9,1},{17,25},{25,17},{2,10},{10... | collective-permute-start | bytes 245768 | tf_op jit(solution)/shard_map/ppermute | solution.py:315
  24.7 0.2 collective-permute-done.2
  25.0 0.1 add_convert_fusion.refs_0_
  25.0 2.5 %collective-permute-start.9 = (bf16[320,128]{1,0:T(8,128)(2,1)S(1)}, bf16[320,128]{1,0:T(8,128)(2,1)S(1)}, u32[]{:S(2)}, u32[]{:S(2)}) collective-permute-start(bf16[320,128]{1,0:T(8,128)(2,1)S(1)} %add_convert_fusion.refs_0_), channel_id=1, source_target_pairs={{0,24},{8,16},{16,8},{24,0},{1,25},{9,17},{17,9},{25,1},{2,26},{10... | collective-permute-start | bytes 245768 | tf_op jit(solution)/shard_map/ppermute | solution.py:315
  27.5 0.5 %collective-permute-start.8 = (bf16[320,128]{1,0:T(8,128)(2,1)S(1)}, bf16[320,128]{1,0:T(8,128)(2,1)S(1)}, u32[]{:S(2)}, u32[]{:S(2)}) collective-permute-start(bf16[320,128]{1,0:T(8,128)(2,1)S(1)} %add_convert_fusion.refs_0_), channel_id=1, source_target_pairs={{0,16},{8,24},{16,0},{24,8},{1,17},{9,25},{17,1},{25,9},{2,18},{10... | collective-permute-start | bytes 245768 | tf_op jit(solution)/shard_map/ppermute | solution.py:315
  28.0 0.0 collective-permute-done.12.refs_3_
  28.0 0.5 %collective-permute-start.7 = (bf16[320,128]{1,0:T(8,128)(2,1)S(1)}, bf16[320,128]{1,0:T(8,128)(2,1)S(1)}, u32[]{:S(2)}, u32[]{:S(2)}) collective-permute-start(bf16[320,128]{1,0:T(8,128)(2,1)S(1)} %add_convert_fusion.refs_0_), channel_id=1, source_target_pairs={{0,8},{8,0},{16,24},{24,16},{1,9},{9,1},{17,25},{25,17},{2,10},{10... | collective-permute-start | bytes 245768 | tf_op jit(solution)/shard_map/ppermute | solution.py:315
  28.6 0.0 collective-permute-done.11.refs_2_
  28.6 0.7 %collective-permute-done.10.refs_1_ = bf16[320,128]{1,0:T(8,128)(2,1)S(1)} collective-permute-done((bf16[320,128]{1,0:T(8,128)(2,1)S(1)}, bf16[320,128]{1,0:T(8,128)(2,1)S(1)}, u32[]{:S(2)}, u32[]{:S(2)}) %collective-permute-start.10) | collective-permute-done | bytes 81952 | tf_op jit(solution)/shard_map/ppermute | solution.py:315
  29.3 3.4 %spectra_part.2.refs_4_ = f32[80,352,128]{2,1,0:T(8,128)} custom-call(bf16[10,352,256]{2,1,0:T(8,128)(2,1)S(1)} %spread_weights.1.weights, bf16[320,128]{1,0:T(8,128)(2,1)S(1)} %add_convert_fusion.1.refs_0_, bf16[320,128]{1,0:T(8,128)(2,1)S(1)} %collective-permute-done.10.refs_1_, bf16[320,128]{1,0:T(8,128)(2,1)S(1)} %collective-permute-done.11.refs_2_, ...), custom_call_target="tpu_custom_call" | custom-call | bytes 9000000 | tf_op jit(solution)/shard_map/spectra_part/pallas_call | solution.py:297
  32.8 0.0 collective-permute-done.8.refs_2_
  32.8 0.0 collective-permute-done.7.refs_1_
  32.8 3.4 %spectra_part.3 = f32[80,352,128]{2,1,0:T(8,128)} custom-call(bf16[10,352,256]{2,1,0:T(8,128)(2,1)S(1)} %spread_weights.1.weights, bf16[320,128]{1,0:T(8,128)(2,1)S(1)} %add_convert_fusion.refs_0_, bf16[320,128]{1,0:T(8,128)(2,1)S(1)} %collective-permute-done.7.refs_1_, ...), custom_call_target="tpu_custom_call", output_to_operand_aliasing={{}: (5, {})} | custom-call | bytes 9000000 | tf_op jit(solution)/shard_map/spectra_part/pallas_call | solution.py:297
  (15 shorter events, 0.2 us)
Async XLA Ops:
  0.0 2.1 %copy-start = (bf16[80,8,1408]{2,1,0:T(8,128)(2,1)S(1)}, bf16[80,8,1408]{2,1,0:T(8,128)(2,1)}, u32[]{:S(2)}) copy-start(bf16[80,8,1408]{2,1,0:T(8,128)(2,1)} %param.5) | copy-start | bytes 5406724
  0.0 2.4 %collective-permute-start = (f32[1288,128]{1,0:T(8,128)}, f32[1288,128]{1,0:T(8,128)S(1)}, u32[]{:S(2)}, u32[]{:S(2)}) collective-permute-start(f32[1288,128]{1,0:T(8,128)} %bitcast.3), channel_id=1, source_target_pairs={{0,1},{1,0},{2,3},{3,2},{4,5},{5,4},{6,7},{7,6},{8,9},{9,8},{10,11... | collective-permute-start | bytes 1978376 | tf_op jit(solution)/shard_map/ppermute | solution.py:326
  0.5 0.7 %copy-start.2 = (s32[2]{0:T(128)S(1)}, s32[2]{0:T(128)}, u32[]{:S(2)}) copy-start(s32[2]{0:T(128)} %row_points.1) | copy-start | bytes 28
  2.4 1.1 %copy-start.1 = (f32[2,644,128]{2,0,1:T(2,128)S(1)}, f32[2,644,128]{2,0,1:T(2,128)}, u32[]{:S(2)}) copy-start(f32[2,644,128]{2,0,1:T(2,128)} %param.3) | copy-start | bytes 1978372
  6.1 11.9 %collective-permute-start.6 = (f16[320,128]{1,0:T(8,128)(2,1)S(1)}, f16[320,128]{1,0:T(8,128)(2,1)S(1)}, u32[]{:S(2)}, u32[]{:S(2)}) collective-permute-start(f16[320,128]{1,0:T(8,128)(2,1)S(1)} %convert_element_type.49), channel_id=1, source_target_pairs={{0,4},{1,5},{2,6},{3,7},{4,0},{5,1},{6,2},{7,3},{8,12},{9,13},{10,... | collective-permute-start | bytes 245768 | tf_op jit(solution)/shard_map/ppermute | solution.py:315
  10.2 9.9 %collective-permute-start.5 = (f16[320,128]{1,0:T(8,128)(2,1)S(1)}, f16[320,128]{1,0:T(8,128)(2,1)S(1)}, u32[]{:S(2)}, u32[]{:S(2)}) collective-permute-start(f16[320,128]{1,0:T(8,128)(2,1)S(1)} %convert_element_type.47), channel_id=1, source_target_pairs={{0,6},{1,7},{2,4},{3,5},{4,2},{5,3},{6,0},{7,1},{8,14},{9,15},{10,... | collective-permute-start | bytes 245768 | tf_op jit(solution)/shard_map/ppermute | solution.py:315
  11.6 8.5 %collective-permute-start.4 = (f16[320,128]{1,0:T(8,128)(2,1)S(1)}, f16[320,128]{1,0:T(8,128)(2,1)S(1)}, u32[]{:S(2)}, u32[]{:S(2)}) collective-permute-start(f16[320,128]{1,0:T(8,128)(2,1)S(1)} %convert_element_type.45), channel_id=1, source_target_pairs={{0,2},{1,3},{2,0},{3,1},{4,6},{5,7},{6,4},{7,5},{8,10},{9,11},{10,... | collective-permute-start | bytes 245768 | tf_op jit(solution)/shard_map/ppermute | solution.py:315
  14.5 9.6 %collective-permute-start.3 = (f16[320,128]{1,0:T(8,128)(2,1)S(1)}, f16[320,128]{1,0:T(8,128)(2,1)S(1)}, u32[]{:S(2)}, u32[]{:S(2)}) collective-permute-start(f16[320,128]{1,0:T(8,128)(2,1)S(1)} %convert_element_type.44), channel_id=1, source_target_pairs={{0,2},{1,3},{2,0},{3,1},{4,6},{5,7},{6,4},{7,5},{8,10},{9,11},{10,... | collective-permute-start | bytes 245768 | tf_op jit(solution)/shard_map/ppermute | solution.py:315
  16.3 8.7 %collective-permute-start.2 = (f16[320,128]{1,0:T(8,128)(2,1)S(1)}, f16[320,128]{1,0:T(8,128)(2,1)S(1)}, u32[]{:S(2)}, u32[]{:S(2)}) collective-permute-start(f16[320,128]{1,0:T(8,128)(2,1)S(1)} %convert_element_type.43), channel_id=1, source_target_pairs={{0,4},{1,5},{2,6},{3,7},{4,0},{5,1},{6,2},{7,3},{8,12},{9,13},{10,... | collective-permute-start | bytes 245768 | tf_op jit(solution)/shard_map/ppermute | solution.py:315
  18.0 7.0 %collective-permute-start.1 = (f16[320,128]{1,0:T(8,128)(2,1)S(1)}, f16[320,128]{1,0:T(8,128)(2,1)S(1)}, u32[]{:S(2)}, u32[]{:S(2)}) collective-permute-start(f16[320,128]{1,0:T(8,128)(2,1)S(1)} %convert_element_type.42), channel_id=1, source_target_pairs={{0,6},{1,7},{2,4},{3,5},{4,2},{5,3},{6,0},{7,1},{8,14},{9,15},{10,... | collective-permute-start | bytes 245768 | tf_op jit(solution)/shard_map/ppermute | solution.py:315
  20.1 7.9 %collective-permute-start.12 = (bf16[320,128]{1,0:T(8,128)(2,1)S(1)}, bf16[320,128]{1,0:T(8,128)(2,1)S(1)}, u32[]{:S(2)}, u32[]{:S(2)}) collective-permute-start(bf16[320,128]{1,0:T(8,128)(2,1)S(1)} %add_convert_fusion.1.refs_0_), channel_id=1, source_target_pairs={{0,24},{8,16},{16,8},{24,0},{1,25},{9,17},{17,9},{25,1},{2,26},{10... | collective-permute-start | bytes 245768 | tf_op jit(solution)/shard_map/ppermute | solution.py:315
  22.6 6.0 %collective-permute-start.11 = (bf16[320,128]{1,0:T(8,128)(2,1)S(1)}, bf16[320,128]{1,0:T(8,128)(2,1)S(1)}, u32[]{:S(2)}, u32[]{:S(2)}) collective-permute-start(bf16[320,128]{1,0:T(8,128)(2,1)S(1)} %add_convert_fusion.1.refs_0_), channel_id=1, source_target_pairs={{0,16},{8,24},{16,0},{24,8},{1,17},{9,25},{17,1},{25,9},{2,18},{10... | collective-permute-start | bytes 245768 | tf_op jit(solution)/shard_map/ppermute | solution.py:315
  24.1 5.2 %collective-permute-start.10 = (bf16[320,128]{1,0:T(8,128)(2,1)S(1)}, bf16[320,128]{1,0:T(8,128)(2,1)S(1)}, u32[]{:S(2)}, u32[]{:S(2)}) collective-permute-start(bf16[320,128]{1,0:T(8,128)(2,1)S(1)} %add_convert_fusion.1.refs_0_), channel_id=1, source_target_pairs={{0,8},{8,0},{16,24},{24,16},{1,9},{9,1},{17,25},{25,17},{2,10},{10... | collective-permute-start | bytes 245768 | tf_op jit(solution)/shard_map/ppermute | solution.py:315
  25.0 7.7 %collective-permute-start.9 = (bf16[320,128]{1,0:T(8,128)(2,1)S(1)}, bf16[320,128]{1,0:T(8,128)(2,1)S(1)}, u32[]{:S(2)}, u32[]{:S(2)}) collective-permute-start(bf16[320,128]{1,0:T(8,128)(2,1)S(1)} %add_convert_fusion.refs_0_), channel_id=1, source_target_pairs={{0,24},{8,16},{16,8},{24,0},{1,25},{9,17},{17,9},{25,1},{2,26},{10... | collective-permute-start | bytes 245768 | tf_op jit(solution)/shard_map/ppermute | solution.py:315
  27.5 5.2 %collective-permute-start.8 = (bf16[320,128]{1,0:T(8,128)(2,1)S(1)}, bf16[320,128]{1,0:T(8,128)(2,1)S(1)}, u32[]{:S(2)}, u32[]{:S(2)}) collective-permute-start(bf16[320,128]{1,0:T(8,128)(2,1)S(1)} %add_convert_fusion.refs_0_), channel_id=1, source_target_pairs={{0,16},{8,24},{16,0},{24,8},{1,17},{9,25},{17,1},{25,9},{2,18},{10... | collective-permute-start | bytes 245768 | tf_op jit(solution)/shard_map/ppermute | solution.py:315
  28.0 4.7 %collective-permute-start.7 = (bf16[320,128]{1,0:T(8,128)(2,1)S(1)}, bf16[320,128]{1,0:T(8,128)(2,1)S(1)}, u32[]{:S(2)}, u32[]{:S(2)}) collective-permute-start(bf16[320,128]{1,0:T(8,128)(2,1)S(1)} %add_convert_fusion.refs_0_), channel_id=1, source_target_pairs={{0,8},{8,0},{16,24},{24,16},{1,9},{9,1},{17,25},{25,17},{2,10},{10... | collective-permute-start | bytes 245768 | tf_op jit(solution)/shard_map/ppermute | solution.py:315

commit v8 on v7

--- a/solution.py
+++ b/solution.py
@@ -56,11 +56,14 @@
     return points - rest, rest, round_up(3 * rest, 128)
 
 
+def hemisphere_sign(width):
+    return jnp.where(lax.broadcasted_iota(jnp.int32, (1, width), 1) < width // 2, 1.0, -1.0)
+
+
 def store_values(out, side, raw, start, length):
     points, width = raw.shape
     body, rest, extra = layout(points)
-    lane = lax.broadcasted_iota(jnp.int32, (1, width), 1)
-    sign = jnp.where(lane < width // 2, 1.0, -1.0)
+    sign = hemisphere_sign(width)
     where = start + lax.broadcasted_iota(jnp.int32, (points, 1), 0)
     folded = pltpu.roll(raw, width // 2, 1) + raw * sign
     folded = jnp.where(where.astype(F32) < length, folded, 0.0)
@@ -75,11 +78,11 @@
         out[3 * body:, lanes] = jnp.concatenate(parts, axis=0).astype(BF16)
 
 
-def row_of(block, r, rows):
-    return block[pl.ds(r, block.shape[0] // rows, stride=rows), :]
-
-
-def prepare_kernel(peers, pair_count, points, row_points, factor):
+def row_of(block, r, rows, points):
+    return block[pl.ds(r, points, stride=rows), :]
+
+
+def prepare_kernel(peers, pair_count, points, lengths, factor):
     rows, _, tall, wide = factor.shape
     body, rest, extra = layout(points)
     set_index = lax.axis_index("set")
@@ -94,8 +97,8 @@
     head = jnp.where(order < peers, (set_index ^ (2 * order)) * pair_count, TRUNC)
     multiplier = jnp.where(sub < GROUP, sub, jnp.where(order < heads, head, (order - heads) * GROUP))
     for r in range(rows):
-        length = row_points[r].astype(F32)
-        scale = jnp.where(slot < body + extra, lax.rsqrt(jnp.full((1, wide), length, F32)), 1.0)
+        length = lengths[r:r + 1, :1]
+        scale = jnp.where(slot < body + extra, lax.rsqrt(jnp.broadcast_to(length, (1, wide))), 1.0)
         scale = jnp.where(sub < GROUP, scale, 1.0)
         real, imag = unit_circle(multiplier, point, length, 1.0 / length)
         factor[r, 0] = jnp.where(order == heads - 1, length, real * scale)
@@ -107,25 +110,25 @@
     return GROUP + heads, round_up(heads + groups, GROUP) - heads
 
 
-def prepare(row_points, points, peers, pair_count):
-    rows = row_points.shape[0]
+def prepare(lengths, points, peers, pair_count):
+    rows = lengths.shape[0]
     body, _, extra = layout(points)
     return pl.pallas_call(
         functools.partial(prepare_kernel, peers, pair_count, points),
         out_shape=jax.ShapeDtypeStruct((rows, 2, sum(table_rows(peers, pair_count)), body + extra + 128), F32),
-        in_specs=[pl.BlockSpec(memory_space=pltpu.SMEM)],
+        in_specs=[pl.BlockSpec(memory_space=pltpu.VMEM)],
         out_specs=pl.BlockSpec(memory_space=pltpu.VMEM),
         compiler_params=pltpu.CompilerParams(vmem_limit_bytes=VMEM),
         cost_estimate=micros(1),
         name="prepare",
-    )(row_points)
+    )(lengths)
 
 
 def fourier_kernel(groups, first_group, peers, pair_count, factor, mine, theirs, *refs):
     outs = refs[:peers]
     rows = factor.shape[0]
     scratch = refs[peers:]
-    points = mine.shape[0] // rows
+    points = theirs.shape[0] // rows
     width = mine.shape[1]
     body, rest, extra = layout(points)
     tail, _ = table_rows(peers, pair_count)
@@ -138,7 +141,7 @@
         values, table, sums, twist = scratch[4 * r:4 * r + 4]
         length = factor[r, 0, tail - 1:tail, :width]
         for side, block in enumerate((mine, theirs)):
-            store_values(values, side, row_of(block, r, rows), (set_index ^ side) * points, length)
+            store_values(values, side, row_of(block, r, rows, points), (set_index ^ side) * points, length)
         near = factor[r, 0, :GROUP, :], factor[r, 1, :GROUP, :]
         last = factor[r, 0, last_at:last_at + 1, :], factor[r, 1, last_at:last_at + 1, :]
         for peer in range(peers):
@@ -181,7 +184,7 @@
 def fourier_sums(factor, mine, theirs, groups, first_group, peers, pair_count):
     rows = factor.shape[0]
     width = mine.shape[1]
-    body, _, extra = layout(mine.shape[0] // rows)
+    body, _, extra = layout(theirs.shape[0] // rows)
     out_rows = groups * 4 * rows * GROUP
     tall = peers * groups * 4 * GROUP
     vmem = pl.BlockSpec(memory_space=pltpu.VMEM)
@@ -324,7 +327,9 @@
     peers = set_size // 2
     flat = grid.transpose(1, 0, 2).reshape(points * rows, width)
     theirs = lax.ppermute(flat, "set", swap("set", set_size, 1))
-    factor = prepare(row_points, points, peers, pair_count)
+    lengths = jnp.broadcast_to(row_points.astype(F32)[:, None], (rows, width))
+    mine = flat
+    factor = prepare(lengths, points, peers, pair_count)
     legend = lax.dynamic_slice_in_dim(legendre, lax.axis_index("band") * slots, slots, 2)
     legend, theirs = lax.optimization_barrier((legend, theirs))
     weights = None
@@ -334,20 +339,19 @@
     gathered = []
     partial = []
     for first_group, groups in chunks:
-        partial.append(fourier_sums(factor, flat, theirs, groups, first_group, peers, pair_count))
+        partial.append(fourier_sums(factor, mine, theirs, groups, first_group, peers, pair_count))
     for parts in partial:
         steps = list(range(1, peers))
         steps = steps[::-1] if gathered else steps[::2] + steps[1::2]
         arrived = exchange([parts[k].astype(WIRE) for k in steps], "set", [2 * k for k in steps])
         if gathered:
+            legend, arrived[-1] = lax.optimization_barrier((legend, arrived[-1]))
+            weights = spread_weights(legend, rows, band_size)
             arrived, weights = lax.optimization_barrier((arrived, weights))
         total = parts[0]
         for part in arrived:
             total = total + part.astype(F32)
         rounded = total.astype(BF16)
-        if not gathered:
-            legend, rounded = lax.optimization_barrier((legend, rounded))
-            weights = spread_weights(legend, rows, band_size)
         turns = list(range(1, band_size))
         gathered.append([rounded] + exchange([rounded] * len(turns), "band", turns))
     out = None

time: 36.4 us -> 35 us (0.962)
  local copies, waits for them, and re-layouts: 2.07 us -> 0.32 us
  other arithmetic: 0.19 us -> 1.05 us
  Pallas kernels: 13.8 us -> 13.3 us
    unnamed x6 -> x4, local copies, waits for them, and re-layouts: 1.83 us -> 0.01 us
    convert_element_type x0 -> x1, other arithmetic: none -> 0.88 us  [shards(): lengths = jnp.broadcast_to(row_points.astype(F32)[:, None], (rows, width))]
    pallas_call x1, Pallas kernels: 0.86 us -> 0.32 us  [prepare(): pl.pallas_call(functools.partial(prepare_kernel, peers, pair_count, point...]
  transfers between devices with their start and end apart: 13 -> 13, of which waited for: 3 -> 3; matrix products, arithmetic and copies ran while one was open for 1% -> 4% of each run, Pallas kernels for 22% -> 21%
where the time goes in v8:
time: 35 us; the launch traced here: 34.9 us
  starting transfers between devices  18.8 us (54%)
  Pallas kernels  13.3 us (38%)
  waiting for transfers between devices  1.23 us (4%)
  other arithmetic  1.05 us (3%)
    ppermute x12, starting transfers between devices, exchange(): lax.ppermute(part, axis, swap(axis, lax.axis_size(axis), step))  18.4 us
    pallas_call x2, Pallas kernels, spectra_part(): pl.pallas_call(functools.partial(spectra_kernel, bands, first_group, pair...  6.85 us
    pallas_call x2, Pallas kernels, fourier_sums(): pl.pallas_call(functools.partial(fourier_kernel, groups, first_group, pee...  5.19 us
    pallas_call x1, Pallas kernels, spread_weights(): pl.pallas_call(functools.partial(weights_kernel, rows, bands), out_shape=...  0.97 us
    convert_element_type x1, other arithmetic, shards(): lengths = jnp.broadcast_to(row_points.astype(F32)[:, None], (rows, width))  0.88 us
    ppermute x12, waiting for transfers between devices, exchange(): lax.ppermute(part, axis, swap(axis, lax.axis_size(axis), step))  0.82 us
  transfers between devices with their start and end apart: 13, of which 3 were waited for; matrix products, arithmetic and copies ran while one was open for 4% of the time, Pallas kernels for 21%

profile of v8, /device:TPU:0, one launch (start us, length us, event | category | flops | bytes accessed | tf_op | source)
XLA Modules:
  0.0 34.9 jit_solution(1401273105068351107)
XLA Ops:
  0.0 0.5 %collective-permute-start = (f32[1288,128]{1,0:T(8,128)}, f32[1288,128]{1,0:T(8,128)S(1)}, u32[]{:S(2)}, u32[]{:S(2)}) collective-permute-start(f32[1288,128]{1,0:T(8,128)} %bitcast.3), channel_id=1, source_target_pairs={{0,1},{1,0},{2,3},{3,2},{4,5},{5,4},{6,7},{7,6},{8,9},{9,8},{10,11... | collective-permute-start | bytes 1978376 | tf_op jit(solution)/shard_map/ppermute | solution.py:329
  0.5 0.9 %convert_element_type.45 = f32[2]{0:T(128)S(1)} convert(s32[2]{0:T(128)} %param.4) | non-fusion elementwise | flops 2 | bytes 16 | tf_op jit(solution)/shard_map/convert_element_type | solution.py:330
  1.3 0.1 broadcast_in_dim.2.lengths
  1.4 0.3 prepare.1.factor
  1.7 0.2 constant_dynamic-slice_fusion.legend
  2.0 0.4 %collective-permute-done.theirs = f32[1288,128]{1,0:T(8,128)S(1)} collective-permute-done((f32[1288,128]{1,0:T(8,128)}, f32[1288,128]{1,0:T(8,128)S(1)}, u32[]{:S(2)}, u32[]{:S(2)}) %collective-permute-start) | collective-permute-done | bytes 659488 | tf_op jit(solution)/shard_map/ppermute | solution.py:329
  2.4 2.6 %fourier_sums.3 = (f32[320,128]{1,0:T(8,128)S(1)}, f32[320,128]{1,0:T(8,128)S(1)}, f32[320,128]{1,0:T(8,128)S(1)}, f32[320,128]{1,0:T(8,128)S(1)}) custom-call(f32[2,2,24,896]{3,2,1,0:T(8,128)S(1)} %prepare.1.factor, f32[1288,128]{1,0:T(8,128)S(1)} %bitcast.4, f32[1288,128]{1,0:T(8,128)S(1)} %collective-permute-done.theirs), custom_call_target="tpu_custom_call" | custom-call | bytes 9000000 | tf_op jit(solution)/shard_map/fourier_sums/pallas_call | solution.py:191
  5.0 4.0 %collective-permute-start.9 = (f16[320,128]{1,0:T(8,128)(2,1)S(1)}, f16[320,128]{1,0:T(8,128)(2,1)S(1)}, u32[]{:S(2)}, u32[]{:S(2)}) collective-permute-start(f16[320,128]{1,0:T(8,128)(2,1)S(1)} %convert_element_type.57), channel_id=1, source_target_pairs={{0,4},{1,5},{2,6},{3,7},{4,0},{5,1},{6,2},{7,3},{8,12},{9,13},{10,... | collective-permute-start | bytes 245768 | tf_op jit(solution)/shard_map/ppermute | solution.py:318
  9.1 1.4 %collective-permute-start.8 = (f16[320,128]{1,0:T(8,128)(2,1)S(1)}, f16[320,128]{1,0:T(8,128)(2,1)S(1)}, u32[]{:S(2)}, u32[]{:S(2)}) collective-permute-start(f16[320,128]{1,0:T(8,128)(2,1)S(1)} %convert_element_type.55), channel_id=1, source_target_pairs={{0,6},{1,7},{2,4},{3,5},{4,2},{5,3},{6,0},{7,1},{8,14},{9,15},{10,... | collective-permute-start | bytes 245768 | tf_op jit(solution)/shard_map/ppermute | solution.py:318
  10.5 0.3 collective-permute-start.7
  10.8 2.6 %fourier_sums.2 = (f32[320,128]{1,0:T(8,128)S(1)}, f32[320,128]{1,0:T(8,128)S(1)}, f32[320,128]{1,0:T(8,128)S(1)}, f32[320,128]{1,0:T(8,128)S(1)}) custom-call(f32[2,2,24,896]{3,2,1,0:T(8,128)S(1)} %prepare.1.factor, f32[1288,128]{1,0:T(8,128)S(1)} %bitcast.5, f32[1288,128]{1,0:T(8,128)S(1)} %collective-permute-done.theirs), custom_call_target="tpu_custom_call" | custom-call | bytes 9000000 | tf_op jit(solution)/shard_map/fourier_sums/pallas_call | solution.py:191
  13.5 1.8 %collective-permute-start.3 = (f16[320,128]{1,0:T(8,128)(2,1)S(1)}, f16[320,128]{1,0:T(8,128)(2,1)S(1)}, u32[]{:S(2)}, u32[]{:S(2)}) collective-permute-start(f16[320,128]{1,0:T(8,128)(2,1)S(1)} %convert_element_type.48), channel_id=1, source_target_pairs={{0,2},{1,3},{2,0},{3,1},{4,6},{5,7},{6,4},{7,5},{8,10},{9,11},{10,... | collective-permute-start | bytes 245768 | tf_op jit(solution)/shard_map/ppermute | solution.py:318
  15.3 1.7 %collective-permute-start.2 = (f16[320,128]{1,0:T(8,128)(2,1)S(1)}, f16[320,128]{1,0:T(8,128)(2,1)S(1)}, u32[]{:S(2)}, u32[]{:S(2)}) collective-permute-start(f16[320,128]{1,0:T(8,128)(2,1)S(1)} %convert_element_type.47), channel_id=1, source_target_pairs={{0,4},{1,5},{2,6},{3,7},{4,0},{5,1},{6,2},{7,3},{8,12},{9,13},{10,... | collective-permute-start | bytes 245768 | tf_op jit(solution)/shard_map/ppermute | solution.py:318
  17.0 0.0 collective-permute-done.9
  17.0 2.0 %collective-permute-start.1 = (f16[320,128]{1,0:T(8,128)(2,1)S(1)}, f16[320,128]{1,0:T(8,128)(2,1)S(1)}, u32[]{:S(2)}, u32[]{:S(2)}) collective-permute-start(f16[320,128]{1,0:T(8,128)(2,1)S(1)} %convert_element_type.46), channel_id=1, source_target_pairs={{0,6},{1,7},{2,4},{3,5},{4,2},{5,3},{6,0},{7,1},{8,14},{9,15},{10,... | collective-permute-start | bytes 245768 | tf_op jit(solution)/shard_map/ppermute | solution.py:318
  19.0 0.0 collective-permute-done.8
  19.0 0.0 collective-permute-done.7
  19.0 2.5 %collective-permute-start.12 = (bf16[320,128]{1,0:T(8,128)(2,1)S(1)}, bf16[320,128]{1,0:T(8,128)(2,1)S(1)}, u32[]{:S(2)}, u32[]{:S(2)}) collective-permute-start(bf16[320,128]{1,0:T(8,128)(2,1)S(1)} %add_convert_fusion.refs_0_), channel_id=1, source_target_pairs={{0,24},{8,16},{16,8},{24,0},{1,25},{9,17},{17,9},{25,1},{2,26},{10... | collective-permute-start | bytes 245768 | tf_op jit(solution)/shard_map/ppermute | solution.py:318
  21.6 0.5 %collective-permute-start.11 = (bf16[320,128]{1,0:T(8,128)(2,1)S(1)}, bf16[320,128]{1,0:T(8,128)(2,1)S(1)}, u32[]{:S(2)}, u32[]{:S(2)}) collective-permute-start(bf16[320,128]{1,0:T(8,128)(2,1)S(1)} %add_convert_fusion.refs_0_), channel_id=1, source_target_pairs={{0,16},{8,24},{16,0},{24,8},{1,17},{9,25},{17,1},{25,9},{2,18},{10... | collective-permute-start | bytes 245768 | tf_op jit(solution)/shard_map/ppermute | solution.py:318
  22.1 0.0 collective-permute-done.3
  22.1 0.5 %collective-permute-start.10 = (bf16[320,128]{1,0:T(8,128)(2,1)S(1)}, bf16[320,128]{1,0:T(8,128)(2,1)S(1)}, u32[]{:S(2)}, u32[]{:S(2)}) collective-permute-start(bf16[320,128]{1,0:T(8,128)(2,1)S(1)} %add_convert_fusion.refs_0_), channel_id=1, source_target_pairs={{0,8},{8,0},{16,24},{24,16},{1,9},{9,1},{17,25},{25,17},{2,10},{10... | collective-permute-start | bytes 245768 | tf_op jit(solution)/shard_map/ppermute | solution.py:318
  22.6 1.0 %spread_weights.1.weights = bf16[10,352,256]{2,1,0:T(8,128)(2,1)S(1)} custom-call(bf16[80,8,352]{2,1,0:T(8,128)(2,1)S(1)} %constant_dynamic-slice_fusion.legend), custom_call_target="tpu_custom_call" | custom-call | bytes 3000000 | tf_op jit(solution)/shard_map/spread_weights/pallas_call | solution.py:241
  23.6 0.3 collective-permute-done.2
  23.9 0.0 collective-permute-done.1
  24.0 2.5 %collective-permute-start.6 = (bf16[320,128]{1,0:T(8,128)(2,1)S(1)}, bf16[320,128]{1,0:T(8,128)(2,1)S(1)}, u32[]{:S(2)}, u32[]{:S(2)}) collective-permute-start(bf16[320,128]{1,0:T(8,128)(2,1)S(1)} %add_convert_fusion.1.refs_0_), channel_id=1, source_target_pairs={{0,24},{8,16},{16,8},{24,0},{1,25},{9,17},{17,9},{25,1},{2,26},{10... | collective-permute-start | bytes 245768 | tf_op jit(solution)/shard_map/ppermute | solution.py:318
  26.5 0.5 %collective-permute-start.5 = (bf16[320,128]{1,0:T(8,128)(2,1)S(1)}, bf16[320,128]{1,0:T(8,128)(2,1)S(1)}, u32[]{:S(2)}, u32[]{:S(2)}) collective-permute-start(bf16[320,128]{1,0:T(8,128)(2,1)S(1)} %add_convert_fusion.1.refs_0_), channel_id=1, source_target_pairs={{0,16},{8,24},{16,0},{24,8},{1,17},{9,25},{17,1},{25,9},{2,18},{10... | collective-permute-start | bytes 245768 | tf_op jit(solution)/shard_map/ppermute | solution.py:318
  27.0 0.5 %collective-permute-start.4 = (bf16[320,128]{1,0:T(8,128)(2,1)S(1)}, bf16[320,128]{1,0:T(8,128)(2,1)S(1)}, u32[]{:S(2)}, u32[]{:S(2)}) collective-permute-start(bf16[320,128]{1,0:T(8,128)(2,1)S(1)} %add_convert_fusion.1.refs_0_), channel_id=1, source_target_pairs={{0,8},{8,0},{16,24},{24,16},{1,9},{9,1},{17,25},{25,17},{2,10},{10... | collective-permute-start | bytes 245768 | tf_op jit(solution)/shard_map/ppermute | solution.py:318
  27.5 3.4 %spectra_part.2.refs_4_ = f32[80,352,128]{2,1,0:T(8,128)} custom-call(bf16[10,352,256]{2,1,0:T(8,128)(2,1)S(1)} %spread_weights.1.weights, bf16[320,128]{1,0:T(8,128)(2,1)S(1)} %add_convert_fusion.refs_0_, bf16[320,128]{1,0:T(8,128)(2,1)S(1)} %collective-permute-done.10.refs_1_, bf16[320,128]{1,0:T(8,128)(2,1)S(1)} %collective-permute-done.11.refs_2_, ...), custom_call_target="tpu_custom_call" | custom-call | bytes 9000000 | tf_op jit(solution)/shard_map/spectra_part/pallas_call | solution.py:300
  31.0 0.0 collective-permute-done.6.refs_3_
  31.0 0.0 collective-permute-done.5.refs_2_
  31.0 0.4 %collective-permute-done.4.refs_1_ = bf16[320,128]{1,0:T(8,128)(2,1)S(1)} collective-permute-done((bf16[320,128]{1,0:T(8,128)(2,1)S(1)}, bf16[320,128]{1,0:T(8,128)(2,1)S(1)}, u32[]{:S(2)}, u32[]{:S(2)}) %collective-permute-start.4) | collective-permute-done | bytes 81952 | tf_op jit(solution)/shard_map/ppermute | solution.py:318
  31.4 3.4 %spectra_part.3 = f32[80,352,128]{2,1,0:T(8,128)} custom-call(bf16[10,352,256]{2,1,0:T(8,128)(2,1)S(1)} %spread_weights.1.weights, bf16[320,128]{1,0:T(8,128)(2,1)S(1)} %add_convert_fusion.1.refs_0_, bf16[320,128]{1,0:T(8,128)(2,1)S(1)} %collective-permute-done.4.refs_1_, ...), custom_call_target="tpu_custom_call", output_to_operand_aliasing={{}: (5, {})} | custom-call | bytes 9000000 | tf_op jit(solution)/shard_map/spectra_part/pallas_call | solution.py:300
  (15 shorter events, 0.2 us)
Async XLA Ops:
  0.0 1.7 %copy-start = (bf16[80,8,1408]{2,1,0:T(8,128)(2,1)S(1)}, bf16[80,8,1408]{2,1,0:T(8,128)(2,1)}, u32[]{:S(2)}) copy-start(bf16[80,8,1408]{2,1,0:T(8,128)(2,1)} %param.5) | copy-start | bytes 5406724
  0.0 2.4 %copy-start.1 = (f32[2,644,128]{2,0,1:T(2,128)S(1)}, f32[2,644,128]{2,0,1:T(2,128)}, u32[]{:S(2)}) copy-start(f32[2,644,128]{2,0,1:T(2,128)} %param.3) | copy-start | bytes 1978372
  0.0 2.4 %collective-permute-start = (f32[1288,128]{1,0:T(8,128)}, f32[1288,128]{1,0:T(8,128)S(1)}, u32[]{:S(2)}, u32[]{:S(2)}) collective-permute-start(f32[1288,128]{1,0:T(8,128)} %bitcast.3), channel_id=1, source_target_pairs={{0,1},{1,0},{2,3},{3,2},{4,5},{5,4},{6,7},{7,6},{8,9},{9,8},{10,11... | collective-permute-start | bytes 1978376 | tf_op jit(solution)/shard_map/ppermute | solution.py:329
  5.0 11.9 %collective-permute-start.9 = (f16[320,128]{1,0:T(8,128)(2,1)S(1)}, f16[320,128]{1,0:T(8,128)(2,1)S(1)}, u32[]{:S(2)}, u32[]{:S(2)}) collective-permute-start(f16[320,128]{1,0:T(8,128)(2,1)S(1)} %convert_element_type.57), channel_id=1, source_target_pairs={{0,4},{1,5},{2,6},{3,7},{4,0},{5,1},{6,2},{7,3},{8,12},{9,13},{10,... | collective-permute-start | bytes 245768 | tf_op jit(solution)/shard_map/ppermute | solution.py:318
  9.1 9.9 %collective-permute-start.8 = (f16[320,128]{1,0:T(8,128)(2,1)S(1)}, f16[320,128]{1,0:T(8,128)(2,1)S(1)}, u32[]{:S(2)}, u32[]{:S(2)}) collective-permute-start(f16[320,128]{1,0:T(8,128)(2,1)S(1)} %convert_element_type.55), channel_id=1, source_target_pairs={{0,6},{1,7},{2,4},{3,5},{4,2},{5,3},{6,0},{7,1},{8,14},{9,15},{10,... | collective-permute-start | bytes 245768 | tf_op jit(solution)/shard_map/ppermute | solution.py:318
  10.5 8.5 %collective-permute-start.7 = (f16[320,128]{1,0:T(8,128)(2,1)S(1)}, f16[320,128]{1,0:T(8,128)(2,1)S(1)}, u32[]{:S(2)}, u32[]{:S(2)}) collective-permute-start(f16[320,128]{1,0:T(8,128)(2,1)S(1)} %convert_element_type.53), channel_id=1, source_target_pairs={{0,2},{1,3},{2,0},{3,1},{4,6},{5,7},{6,4},{7,5},{8,10},{9,11},{10,... | collective-permute-start | bytes 245768 | tf_op jit(solution)/shard_map/ppermute | solution.py:318
  13.5 8.6 %collective-permute-start.3 = (f16[320,128]{1,0:T(8,128)(2,1)S(1)}, f16[320,128]{1,0:T(8,128)(2,1)S(1)}, u32[]{:S(2)}, u32[]{:S(2)}) collective-permute-start(f16[320,128]{1,0:T(8,128)(2,1)S(1)} %convert_element_type.48), channel_id=1, source_target_pairs={{0,2},{1,3},{2,0},{3,1},{4,6},{5,7},{6,4},{7,5},{8,10},{9,11},{10,... | collective-permute-start | bytes 245768 | tf_op jit(solution)/shard_map/ppermute | solution.py:318
  15.3 8.7 %collective-permute-start.2 = (f16[320,128]{1,0:T(8,128)(2,1)S(1)}, f16[320,128]{1,0:T(8,128)(2,1)S(1)}, u32[]{:S(2)}, u32[]{:S(2)}) collective-permute-start(f16[320,128]{1,0:T(8,128)(2,1)S(1)} %convert_element_type.47), channel_id=1, source_target_pairs={{0,4},{1,5},{2,6},{3,7},{4,0},{5,1},{6,2},{7,3},{8,12},{9,13},{10,... | collective-permute-start | bytes 245768 | tf_op jit(solution)/shard_map/ppermute | solution.py:318
  17.0 7.0 %collective-permute-start.1 = (f16[320,128]{1,0:T(8,128)(2,1)S(1)}, f16[320,128]{1,0:T(8,128)(2,1)S(1)}, u32[]{:S(2)}, u32[]{:S(2)}) collective-permute-start(f16[320,128]{1,0:T(8,128)(2,1)S(1)} %convert_element_type.46), channel_id=1, source_target_pairs={{0,6},{1,7},{2,4},{3,5},{4,2},{5,3},{6,0},{7,1},{8,14},{9,15},{10,... | collective-permute-start | bytes 245768 | tf_op jit(solution)/shard_map/ppermute | solution.py:318
  19.0 7.9 %collective-permute-start.12 = (bf16[320,128]{1,0:T(8,128)(2,1)S(1)}, bf16[320,128]{1,0:T(8,128)(2,1)S(1)}, u32[]{:S(2)}, u32[]{:S(2)}) collective-permute-start(bf16[320,128]{1,0:T(8,128)(2,1)S(1)} %add_convert_fusion.refs_0_), channel_id=1, source_target_pairs={{0,24},{8,16},{16,8},{24,0},{1,25},{9,17},{17,9},{25,1},{2,26},{10... | collective-permute-start | bytes 245768 | tf_op jit(solution)/shard_map/ppermute | solution.py:318
  21.6 6.0 %collective-permute-start.11 = (bf16[320,128]{1,0:T(8,128)(2,1)S(1)}, bf16[320,128]{1,0:T(8,128)(2,1)S(1)}, u32[]{:S(2)}, u32[]{:S(2)}) collective-permute-start(bf16[320,128]{1,0:T(8,128)(2,1)S(1)} %add_convert_fusion.refs_0_), channel_id=1, source_target_pairs={{0,16},{8,24},{16,0},{24,8},{1,17},{9,25},{17,1},{25,9},{2,18},{10... | collective-permute-start | bytes 245768 | tf_op jit(solution)/shard_map/ppermute | solution.py:318
  22.1 5.5 %collective-permute-start.10 = (bf16[320,128]{1,0:T(8,128)(2,1)S(1)}, bf16[320,128]{1,0:T(8,128)(2,1)S(1)}, u32[]{:S(2)}, u32[]{:S(2)}) collective-permute-start(bf16[320,128]{1,0:T(8,128)(2,1)S(1)} %add_convert_fusion.refs_0_), channel_id=1, source_target_pairs={{0,8},{8,0},{16,24},{24,16},{1,9},{9,1},{17,25},{25,17},{2,10},{10... | collective-permute-start | bytes 245768 | tf_op jit(solution)/shard_map/ppermute | solution.py:318
  24.0 7.0 %collective-permute-start.6 = (bf16[320,128]{1,0:T(8,128)(2,1)S(1)}, bf16[320,128]{1,0:T(8,128)(2,1)S(1)}, u32[]{:S(2)}, u32[]{:S(2)}) collective-permute-start(bf16[320,128]{1,0:T(8,128)(2,1)S(1)} %add_convert_fusion.1.refs_0_), channel_id=1, source_target_pairs={{0,24},{8,16},{16,8},{24,0},{1,25},{9,17},{17,9},{25,1},{2,26},{10... | collective-permute-start | bytes 245768 | tf_op jit(solution)/shard_map/ppermute | solution.py:318
  26.5 4.5 %collective-permute-start.5 = (bf16[320,128]{1,0:T(8,128)(2,1)S(1)}, bf16[320,128]{1,0:T(8,128)(2,1)S(1)}, u32[]{:S(2)}, u32[]{:S(2)}) collective-permute-start(bf16[320,128]{1,0:T(8,128)(2,1)S(1)} %add_convert_fusion.1.refs_0_), channel_id=1, source_target_pairs={{0,16},{8,24},{16,0},{24,8},{1,17},{9,25},{17,1},{25,9},{2,18},{10... | collective-permute-start | bytes 245768 | tf_op jit(solution)/shard_map/ppermute | solution.py:318
  27.0 4.4 %collective-permute-start.4 = (bf16[320,128]{1,0:T(8,128)(2,1)S(1)}, bf16[320,128]{1,0:T(8,128)(2,1)S(1)}, u32[]{:S(2)}, u32[]{:S(2)}) collective-permute-start(bf16[320,128]{1,0:T(8,128)(2,1)S(1)} %add_convert_fusion.1.refs_0_), channel_id=1, source_target_pairs={{0,8},{8,0},{16,24},{24,16},{1,9},{9,1},{17,25},{25,17},{2,10},{10... | collective-permute-start | bytes 245768 | tf_op jit(solution)/shard_map/ppermute | solution.py:318

commit v9 on v8

--- a/solution.py
+++ b/solution.py
@@ -98,11 +98,15 @@
     multiplier = jnp.where(sub < GROUP, sub, jnp.where(order < heads, head, (order - heads) * GROUP))
     for r in range(rows):
         length = lengths[r:r + 1, :1]
-        scale = jnp.where(slot < body + extra, lax.rsqrt(jnp.broadcast_to(length, (1, wide))), 1.0)
+        scale = jnp.where(slot < body + extra, lax.rsqrt(jnp.broadcast_to(length, (1, wide))) * headroom(points), 1.0)
         scale = jnp.where(sub < GROUP, scale, 1.0)
         real, imag = unit_circle(multiplier, point, length, 1.0 / length)
         factor[r, 0] = jnp.where(order == heads - 1, length, real * scale)
         factor[r, 1] = imag * scale
+
+
+def headroom(points):
+    return 2.0 ** math.floor(math.log2(60000 / (12 * math.sqrt(2 * points))))
 
 
 def table_rows(peers, pair_count):
@@ -351,7 +355,7 @@
         total = parts[0]
         for part in arrived:
             total = total + part.astype(F32)
-        rounded = total.astype(BF16)
+        rounded = (total * (1 / headroom(points))).astype(BF16)
         turns = list(range(1, band_size))
         gathered.append([rounded] + exchange([rounded] * len(turns), "band", turns))
     out = None

time: 35 us -> 35 us (level)
  no operation moved by 1% of the time
where the time goes in v9:
time: 35 us; the launch traced here: 34.9 us
  starting transfers between devices  18.8 us (54%)
  Pallas kernels  13.3 us (38%)
  waiting for transfers between devices  1.22 us (3%)
  other arithmetic  1.06 us (3%)
    ppermute x12, starting transfers between devices, exchange(): lax.ppermute(part, axis, swap(axis, lax.axis_size(axis), step))  18.4 us
    pallas_call x2, Pallas kernels, spectra_part(): pl.pallas_call(functools.partial(spectra_kernel, bands, first_group, pair...  6.84 us
    pallas_call x2, Pallas kernels, fourier_sums(): pl.pallas_call(functools.partial(fourier_kernel, groups, first_group, pee...  5.19 us
    pallas_call x1, Pallas kernels, spread_weights(): pl.pallas_call(functools.partial(weights_kernel, rows, bands), out_shape=...  0.97 us
    convert_element_type x1, other arithmetic, shards(): lengths = jnp.broadcast_to(row_points.astype(F32)[:, None], (rows, width))  0.88 us
    ppermute x12, waiting for transfers between devices, exchange(): lax.ppermute(part, axis, swap(axis, lax.axis_size(axis), step))  0.81 us
  transfers between devices with their start and end apart: 13, of which 3 were waited for; matrix products, arithmetic and copies ran while one was open for 4% of the time, Pallas kernels for 21%

profile of v9, /device:TPU:0, one launch (start us, length us, event | category | flops | bytes accessed | tf_op | source)
XLA Modules:
  0.0 34.9 jit_solution(1772038026204605678)
XLA Ops:
  0.0 0.5 %collective-permute-start = (f32[1288,128]{1,0:T(8,128)}, f32[1288,128]{1,0:T(8,128)S(1)}, u32[]{:S(2)}, u32[]{:S(2)}) collective-permute-start(f32[1288,128]{1,0:T(8,128)} %bitcast.3), channel_id=1, source_target_pairs={{0,1},{1,0},{2,3},{3,2},{4,5},{5,4},{6,7},{7,6},{8,9},{9,8},{10,11... | collective-permute-start | bytes 1978376 | tf_op jit(solution)/shard_map/ppermute | solution.py:333
  0.5 0.9 %convert_element_type.45 = f32[2]{0:T(128)S(1)} convert(s32[2]{0:T(128)} %param.4) | non-fusion elementwise | flops 2 | bytes 16 | tf_op jit(solution)/shard_map/convert_element_type | solution.py:334
  1.3 0.1 broadcast_in_dim.2.lengths
  1.4 0.3 prepare.1.factor
  1.7 0.2 constant_dynamic-slice_fusion.legend
  2.0 0.4 %collective-permute-done.theirs = f32[1288,128]{1,0:T(8,128)S(1)} collective-permute-done((f32[1288,128]{1,0:T(8,128)}, f32[1288,128]{1,0:T(8,128)S(1)}, u32[]{:S(2)}, u32[]{:S(2)}) %collective-permute-start) | collective-permute-done | bytes 659488 | tf_op jit(solution)/shard_map/ppermute | solution.py:333
  2.4 2.6 %fourier_sums.3 = (f32[320,128]{1,0:T(8,128)S(1)}, f32[320,128]{1,0:T(8,128)S(1)}, f32[320,128]{1,0:T(8,128)S(1)}, f32[320,128]{1,0:T(8,128)S(1)}) custom-call(f32[2,2,24,896]{3,2,1,0:T(8,128)S(1)} %prepare.1.factor, f32[1288,128]{1,0:T(8,128)S(1)} %bitcast.4, f32[1288,128]{1,0:T(8,128)S(1)} %collective-permute-done.theirs), custom_call_target="tpu_custom_call" | custom-call | bytes 9000000 | tf_op jit(solution)/shard_map/fourier_sums/pallas_call | solution.py:195
  5.0 4.0 %collective-permute-start.9 = (f16[320,128]{1,0:T(8,128)(2,1)S(1)}, f16[320,128]{1,0:T(8,128)(2,1)S(1)}, u32[]{:S(2)}, u32[]{:S(2)}) collective-permute-start(f16[320,128]{1,0:T(8,128)(2,1)S(1)} %convert_element_type.57), channel_id=1, source_target_pairs={{0,4},{1,5},{2,6},{3,7},{4,0},{5,1},{6,2},{7,3},{8,12},{9,13},{10,... | collective-permute-start | bytes 245768 | tf_op jit(solution)/shard_map/ppermute | solution.py:322
  9.1 1.4 %collective-permute-start.8 = (f16[320,128]{1,0:T(8,128)(2,1)S(1)}, f16[320,128]{1,0:T(8,128)(2,1)S(1)}, u32[]{:S(2)}, u32[]{:S(2)}) collective-permute-start(f16[320,128]{1,0:T(8,128)(2,1)S(1)} %convert_element_type.55), channel_id=1, source_target_pairs={{0,6},{1,7},{2,4},{3,5},{4,2},{5,3},{6,0},{7,1},{8,14},{9,15},{10,... | collective-permute-start | bytes 245768 | tf_op jit(solution)/shard_map/ppermute | solution.py:322
  10.5 0.3 collective-permute-start.7
  10.8 2.6 %fourier_sums.2 = (f32[320,128]{1,0:T(8,128)S(1)}, f32[320,128]{1,0:T(8,128)S(1)}, f32[320,128]{1,0:T(8,128)S(1)}, f32[320,128]{1,0:T(8,128)S(1)}) custom-call(f32[2,2,24,896]{3,2,1,0:T(8,128)S(1)} %prepare.1.factor, f32[1288,128]{1,0:T(8,128)S(1)} %bitcast.5, f32[1288,128]{1,0:T(8,128)S(1)} %collective-permute-done.theirs), custom_call_target="tpu_custom_call" | custom-call | bytes 9000000 | tf_op jit(solution)/shard_map/fourier_sums/pallas_call | solution.py:195
  13.5 1.8 %collective-permute-start.3 = (f16[320,128]{1,0:T(8,128)(2,1)S(1)}, f16[320,128]{1,0:T(8,128)(2,1)S(1)}, u32[]{:S(2)}, u32[]{:S(2)}) collective-permute-start(f16[320,128]{1,0:T(8,128)(2,1)S(1)} %convert_element_type.48), channel_id=1, source_target_pairs={{0,2},{1,3},{2,0},{3,1},{4,6},{5,7},{6,4},{7,5},{8,10},{9,11},{10,... | collective-permute-start | bytes 245768 | tf_op jit(solution)/shard_map/ppermute | solution.py:322
  15.3 1.7 %collective-permute-start.2 = (f16[320,128]{1,0:T(8,128)(2,1)S(1)}, f16[320,128]{1,0:T(8,128)(2,1)S(1)}, u32[]{:S(2)}, u32[]{:S(2)}) collective-permute-start(f16[320,128]{1,0:T(8,128)(2,1)S(1)} %convert_element_type.47), channel_id=1, source_target_pairs={{0,4},{1,5},{2,6},{3,7},{4,0},{5,1},{6,2},{7,3},{8,12},{9,13},{10,... | collective-permute-start | bytes 245768 | tf_op jit(solution)/shard_map/ppermute | solution.py:322
  17.0 0.0 collective-permute-done.9
  17.0 2.0 %collective-permute-start.1 = (f16[320,128]{1,0:T(8,128)(2,1)S(1)}, f16[320,128]{1,0:T(8,128)(2,1)S(1)}, u32[]{:S(2)}, u32[]{:S(2)}) collective-permute-start(f16[320,128]{1,0:T(8,128)(2,1)S(1)} %convert_element_type.46), channel_id=1, source_target_pairs={{0,6},{1,7},{2,4},{3,5},{4,2},{5,3},{6,0},{7,1},{8,14},{9,15},{10,... | collective-permute-start | bytes 245768 | tf_op jit(solution)/shard_map/ppermute | solution.py:322
  19.0 0.0 collective-permute-done.8
  19.0 0.1 multiply_convert_fusion.refs_0_
  19.0 2.5 %collective-permute-start.12 = (bf16[320,128]{1,0:T(8,128)(2,1)S(1)}, bf16[320,128]{1,0:T(8,128)(2,1)S(1)}, u32[]{:S(2)}, u32[]{:S(2)}) collective-permute-start(bf16[320,128]{1,0:T(8,128)(2,1)S(1)} %multiply_convert_fusion.refs_0_), channel_id=1, source_target_pairs={{0,24},{8,16},{16,8},{24,0},{1,25},{9,17},{17,9},{25,1},{2,26},{10... | collective-permute-start | bytes 245768 | tf_op jit(solution)/shard_map/ppermute | solution.py:322
  21.6 0.5 %collective-permute-start.11 = (bf16[320,128]{1,0:T(8,128)(2,1)S(1)}, bf16[320,128]{1,0:T(8,128)(2,1)S(1)}, u32[]{:S(2)}, u32[]{:S(2)}) collective-permute-start(bf16[320,128]{1,0:T(8,128)(2,1)S(1)} %multiply_convert_fusion.refs_0_), channel_id=1, source_target_pairs={{0,16},{8,24},{16,0},{24,8},{1,17},{9,25},{17,1},{25,9},{2,18},{10... | collective-permute-start | bytes 245768 | tf_op jit(solution)/shard_map/ppermute | solution.py:322
  22.1 0.0 collective-permute-done.3
  22.1 0.5 %collective-permute-start.10 = (bf16[320,128]{1,0:T(8,128)(2,1)S(1)}, bf16[320,128]{1,0:T(8,128)(2,1)S(1)}, u32[]{:S(2)}, u32[]{:S(2)}) collective-permute-start(bf16[320,128]{1,0:T(8,128)(2,1)S(1)} %multiply_convert_fusion.refs_0_), channel_id=1, source_target_pairs={{0,8},{8,0},{16,24},{24,16},{1,9},{9,1},{17,25},{25,17},{2,10},{10... | collective-permute-start | bytes 245768 | tf_op jit(solution)/shard_map/ppermute | solution.py:322
  22.6 1.0 %spread_weights.1.weights = bf16[10,352,256]{2,1,0:T(8,128)(2,1)S(1)} custom-call(bf16[80,8,352]{2,1,0:T(8,128)(2,1)S(1)} %constant_dynamic-slice_fusion.legend), custom_call_target="tpu_custom_call" | custom-call | bytes 3000000 | tf_op jit(solution)/shard_map/spread_weights/pallas_call | solution.py:245
  23.6 0.3 collective-permute-done.2
  24.0 2.5 %collective-permute-start.6 = (bf16[320,128]{1,0:T(8,128)(2,1)S(1)}, bf16[320,128]{1,0:T(8,128)(2,1)S(1)}, u32[]{:S(2)}, u32[]{:S(2)}) collective-permute-start(bf16[320,128]{1,0:T(8,128)(2,1)S(1)} %multiply_convert_fusion.1.refs_0_), channel_id=1, source_target_pairs={{0,24},{8,16},{16,8},{24,0},{1,25},{9,17},{17,9},{25,1},{2,26},{10... | collective-permute-start | bytes 245768 | tf_op jit(solution)/shard_map/ppermute | solution.py:322
  26.5 0.5 %collective-permute-start.5 = (bf16[320,128]{1,0:T(8,128)(2,1)S(1)}, bf16[320,128]{1,0:T(8,128)(2,1)S(1)}, u32[]{:S(2)}, u32[]{:S(2)}) collective-permute-start(bf16[320,128]{1,0:T(8,128)(2,1)S(1)} %multiply_convert_fusion.1.refs_0_), channel_id=1, source_target_pairs={{0,16},{8,24},{16,0},{24,8},{1,17},{9,25},{17,1},{25,9},{2,18},{10... | collective-permute-start | bytes 245768 | tf_op jit(solution)/shard_map/ppermute | solution.py:322
  27.0 0.0 collective-permute-done.12.refs_3_
  27.0 0.5 %collective-permute-start.4 = (bf16[320,128]{1,0:T(8,128)(2,1)S(1)}, bf16[320,128]{1,0:T(8,128)(2,1)S(1)}, u32[]{:S(2)}, u32[]{:S(2)}) collective-permute-start(bf16[320,128]{1,0:T(8,128)(2,1)S(1)} %multiply_convert_fusion.1.refs_0_), channel_id=1, source_target_pairs={{0,8},{8,0},{16,24},{24,16},{1,9},{9,1},{17,25},{25,17},{2,10},{10... | collective-permute-start | bytes 245768 | tf_op jit(solution)/shard_map/ppermute | solution.py:322
  27.5 3.4 %spectra_part.2.refs_4_ = f32[80,352,128]{2,1,0:T(8,128)} custom-call(bf16[10,352,256]{2,1,0:T(8,128)(2,1)S(1)} %spread_weights.1.weights, bf16[320,128]{1,0:T(8,128)(2,1)S(1)} %multiply_convert_fusion.refs_0_, bf16[320,128]{1,0:T(8,128)(2,1)S(1)} %collective-permute-done.10.refs_1_, bf16[320,128]{1,0:T(8,128)(2,1)S(1)} %collective-permute-done.11.refs_2_, ...), custom_call_target="tpu_custom_call" | custom-call | bytes 9000000 | tf_op jit(solution)/shard_map/spectra_part/pallas_call | solution.py:304
  31.0 0.0 collective-permute-done.6.refs_3_
  31.0 0.0 collective-permute-done.5.refs_2_
  31.0 0.4 %collective-permute-done.4.refs_1_ = bf16[320,128]{1,0:T(8,128)(2,1)S(1)} collective-permute-done((bf16[320,128]{1,0:T(8,128)(2,1)S(1)}, bf16[320,128]{1,0:T(8,128)(2,1)S(1)}, u32[]{:S(2)}, u32[]{:S(2)}) %collective-permute-start.4) | collective-permute-done | bytes 81952 | tf_op jit(solution)/shard_map/ppermute | solution.py:322
  31.4 3.4 %spectra_part.3 = f32[80,352,128]{2,1,0:T(8,128)} custom-call(bf16[10,352,256]{2,1,0:T(8,128)(2,1)S(1)} %spread_weights.1.weights, bf16[320,128]{1,0:T(8,128)(2,1)S(1)} %multiply_convert_fusion.1.refs_0_, bf16[320,128]{1,0:T(8,128)(2,1)S(1)} %collective-permute-done.4.refs_1_, ...), custom_call_target="tpu_custom_call", output_to_operand_aliasing={{}: (5, {})} | custom-call | bytes 9000000 | tf_op jit(solution)/shard_map/spectra_part/pallas_call | solution.py:304
  (15 shorter events, 0.2 us)
Async XLA Ops:
  0.0 1.7 %copy-start = (bf16[80,8,1408]{2,1,0:T(8,128)(2,1)S(1)}, bf16[80,8,1408]{2,1,0:T(8,128)(2,1)}, u32[]{:S(2)}) copy-start(bf16[80,8,1408]{2,1,0:T(8,128)(2,1)} %param.5) | copy-start | bytes 5406724
  0.0 2.4 %copy-start.1 = (f32[2,644,128]{2,0,1:T(2,128)S(1)}, f32[2,644,128]{2,0,1:T(2,128)}, u32[]{:S(2)}) copy-start(f32[2,644,128]{2,0,1:T(2,128)} %param.3) | copy-start | bytes 1978372
  0.0 2.4 %collective-permute-start = (f32[1288,128]{1,0:T(8,128)}, f32[1288,128]{1,0:T(8,128)S(1)}, u32[]{:S(2)}, u32[]{:S(2)}) collective-permute-start(f32[1288,128]{1,0:T(8,128)} %bitcast.3), channel_id=1, source_target_pairs={{0,1},{1,0},{2,3},{3,2},{4,5},{5,4},{6,7},{7,6},{8,9},{9,8},{10,11... | collective-permute-start | bytes 1978376 | tf_op jit(solution)/shard_map/ppermute | solution.py:333
  5.0 11.9 %collective-permute-start.9 = (f16[320,128]{1,0:T(8,128)(2,1)S(1)}, f16[320,128]{1,0:T(8,128)(2,1)S(1)}, u32[]{:S(2)}, u32[]{:S(2)}) collective-permute-start(f16[320,128]{1,0:T(8,128)(2,1)S(1)} %convert_element_type.57), channel_id=1, source_target_pairs={{0,4},{1,5},{2,6},{3,7},{4,0},{5,1},{6,2},{7,3},{8,12},{9,13},{10,... | collective-permute-start | bytes 245768 | tf_op jit(solution)/shard_map/ppermute | solution.py:322
  9.1 9.9 %collective-permute-start.8 = (f16[320,128]{1,0:T(8,128)(2,1)S(1)}, f16[320,128]{1,0:T(8,128)(2,1)S(1)}, u32[]{:S(2)}, u32[]{:S(2)}) collective-permute-start(f16[320,128]{1,0:T(8,128)(2,1)S(1)} %convert_element_type.55), channel_id=1, source_target_pairs={{0,6},{1,7},{2,4},{3,5},{4,2},{5,3},{6,0},{7,1},{8,14},{9,15},{10,... | collective-permute-start | bytes 245768 | tf_op jit(solution)/shard_map/ppermute | solution.py:322
  10.5 8.5 %collective-permute-start.7 = (f16[320,128]{1,0:T(8,128)(2,1)S(1)}, f16[320,128]{1,0:T(8,128)(2,1)S(1)}, u32[]{:S(2)}, u32[]{:S(2)}) collective-permute-start(f16[320,128]{1,0:T(8,128)(2,1)S(1)} %convert_element_type.53), channel_id=1, source_target_pairs={{0,2},{1,3},{2,0},{3,1},{4,6},{5,7},{6,4},{7,5},{8,10},{9,11},{10,... | collective-permute-start | bytes 245768 | tf_op jit(solution)/shard_map/ppermute | solution.py:322
  13.5 8.6 %collective-permute-start.3 = (f16[320,128]{1,0:T(8,128)(2,1)S(1)}, f16[320,128]{1,0:T(8,128)(2,1)S(1)}, u32[]{:S(2)}, u32[]{:S(2)}) collective-permute-start(f16[320,128]{1,0:T(8,128)(2,1)S(1)} %convert_element_type.48), channel_id=1, source_target_pairs={{0,2},{1,3},{2,0},{3,1},{4,6},{5,7},{6,4},{7,5},{8,10},{9,11},{10,... | collective-permute-start | bytes 245768 | tf_op jit(solution)/shard_map/ppermute | solution.py:322
  15.3 8.7 %collective-permute-start.2 = (f16[320,128]{1,0:T(8,128)(2,1)S(1)}, f16[320,128]{1,0:T(8,128)(2,1)S(1)}, u32[]{:S(2)}, u32[]{:S(2)}) collective-permute-start(f16[320,128]{1,0:T(8,128)(2,1)S(1)} %convert_element_type.47), channel_id=1, source_target_pairs={{0,4},{1,5},{2,6},{3,7},{4,0},{5,1},{6,2},{7,3},{8,12},{9,13},{10,... | collective-permute-start | bytes 245768 | tf_op jit(solution)/shard_map/ppermute | solution.py:322
  17.0 7.0 %collective-permute-start.1 = (f16[320,128]{1,0:T(8,128)(2,1)S(1)}, f16[320,128]{1,0:T(8,128)(2,1)S(1)}, u32[]{:S(2)}, u32[]{:S(2)}) collective-permute-start(f16[320,128]{1,0:T(8,128)(2,1)S(1)} %convert_element_type.46), channel_id=1, source_target_pairs={{0,6},{1,7},{2,4},{3,5},{4,2},{5,3},{6,0},{7,1},{8,14},{9,15},{10,... | collective-permute-start | bytes 245768 | tf_op jit(solution)/shard_map/ppermute | solution.py:322
  19.0 7.9 %collective-permute-start.12 = (bf16[320,128]{1,0:T(8,128)(2,1)S(1)}, bf16[320,128]{1,0:T(8,128)(2,1)S(1)}, u32[]{:S(2)}, u32[]{:S(2)}) collective-permute-start(bf16[320,128]{1,0:T(8,128)(2,1)S(1)} %multiply_convert_fusion.refs_0_), channel_id=1, source_target_pairs={{0,24},{8,16},{16,8},{24,0},{1,25},{9,17},{17,9},{25,1},{2,26},{10... | collective-permute-start | bytes 245768 | tf_op jit(solution)/shard_map/ppermute | solution.py:322
  21.6 6.0 %collective-permute-start.11 = (bf16[320,128]{1,0:T(8,128)(2,1)S(1)}, bf16[320,128]{1,0:T(8,128)(2,1)S(1)}, u32[]{:S(2)}, u32[]{:S(2)}) collective-permute-start(bf16[320,128]{1,0:T(8,128)(2,1)S(1)} %multiply_convert_fusion.refs_0_), channel_id=1, source_target_pairs={{0,16},{8,24},{16,0},{24,8},{1,17},{9,25},{17,1},{25,9},{2,18},{10... | collective-permute-start | bytes 245768 | tf_op jit(solution)/shard_map/ppermute | solution.py:322
  22.1 5.5 %collective-permute-start.10 = (bf16[320,128]{1,0:T(8,128)(2,1)S(1)}, bf16[320,128]{1,0:T(8,128)(2,1)S(1)}, u32[]{:S(2)}, u32[]{:S(2)}) collective-permute-start(bf16[320,128]{1,0:T(8,128)(2,1)S(1)} %multiply_convert_fusion.refs_0_), channel_id=1, source_target_pairs={{0,8},{8,0},{16,24},{24,16},{1,9},{9,1},{17,25},{25,17},{2,10},{10... | collective-permute-start | bytes 245768 | tf_op jit(solution)/shard_map/ppermute | solution.py:322
  24.0 7.0 %collective-permute-start.6 = (bf16[320,128]{1,0:T(8,128)(2,1)S(1)}, bf16[320,128]{1,0:T(8,128)(2,1)S(1)}, u32[]{:S(2)}, u32[]{:S(2)}) collective-permute-start(bf16[320,128]{1,0:T(8,128)(2,1)S(1)} %multiply_convert_fusion.1.refs_0_), channel_id=1, source_target_pairs={{0,24},{8,16},{16,8},{24,0},{1,25},{9,17},{17,9},{25,1},{2,26},{10... | collective-permute-start | bytes 245768 | tf_op jit(solution)/shard_map/ppermute | solution.py:322
  26.5 4.5 %collective-permute-start.5 = (bf16[320,128]{1,0:T(8,128)(2,1)S(1)}, bf16[320,128]{1,0:T(8,128)(2,1)S(1)}, u32[]{:S(2)}, u32[]{:S(2)}) collective-permute-start(bf16[320,128]{1,0:T(8,128)(2,1)S(1)} %multiply_convert_fusion.1.refs_0_), channel_id=1, source_target_pairs={{0,16},{8,24},{16,0},{24,8},{1,17},{9,25},{17,1},{25,9},{2,18},{10... | collective-permute-start | bytes 245768 | tf_op jit(solution)/shard_map/ppermute | solution.py:322
  27.0 4.4 %collective-permute-start.4 = (bf16[320,128]{1,0:T(8,128)(2,1)S(1)}, bf16[320,128]{1,0:T(8,128)(2,1)S(1)}, u32[]{:S(2)}, u32[]{:S(2)}) collective-permute-start(bf16[320,128]{1,0:T(8,128)(2,1)S(1)} %multiply_convert_fusion.1.refs_0_), channel_id=1, source_target_pairs={{0,8},{8,0},{16,24},{24,16},{1,9},{9,1},{17,25},{25,17},{2,10},{10... | collective-permute-start | bytes 245768 | tf_op jit(solution)/shard_map/ppermute | solution.py:322

commit v10 on v9

--- a/solution.py
+++ b/solution.py
@@ -287,7 +287,7 @@
             copy = pltpu.make_async_copy(
                 block.at[pl.ds(pair, 2)], out.at[pl.ds(first_group * GROUP + pair, 2)], sems.at[pair // 2]
             )
-            copy.start()
+            copy.start(priority=len(copies) % 2)
             copies.append(copy)
     for copy in copies:
         copy.wait()

time: 35 us -> 35 us (level)
  no operation moved by 1% of the time
where the time goes in v10:
time: 35 us; the launch traced here: 34.9 us
  starting transfers between devices  18.8 us (54%)
  Pallas kernels  13.3 us (38%)
  waiting for transfers between devices  1.22 us (3%)
  other arithmetic  1.06 us (3%)
    ppermute x12, starting transfers between devices, exchange(): lax.ppermute(part, axis, swap(axis, lax.axis_size(axis), step))  18.4 us
    pallas_call x2, Pallas kernels, spectra_part(): pl.pallas_call(functools.partial(spectra_kernel, bands, first_group, pair...  6.84 us
    pallas_call x2, Pallas kernels, fourier_sums(): pl.pallas_call(functools.partial(fourier_kernel, groups, first_group, pee...  5.19 us
    pallas_call x1, Pallas kernels, spread_weights(): pl.pallas_call(functools.partial(weights_kernel, rows, bands), out_shape=...  0.97 us
    convert_element_type x1, other arithmetic, shards(): lengths = jnp.broadcast_to(row_points.astype(F32)[:, None], (rows, width))  0.88 us
    ppermute x12, waiting for transfers between devices, exchange(): lax.ppermute(part, axis, swap(axis, lax.axis_size(axis), step))  0.81 us
  transfers between devices with their start and end apart: 13, of which 3 were waited for; matrix products, arithmetic and copies ran while one was open for 4% of the time, Pallas kernels for 21%

profile of v10, /device:TPU:0, one launch (start us, length us, event | category | flops | bytes accessed | tf_op | source)
XLA Modules:
  0.0 34.9 jit_solution(6795547205838705805)
XLA Ops:
  0.0 0.5 %collective-permute-start = (f32[1288,128]{1,0:T(8,128)}, f32[1288,128]{1,0:T(8,128)S(1)}, u32[]{:S(2)}, u32[]{:S(2)}) collective-permute-start(f32[1288,128]{1,0:T(8,128)} %bitcast.3), channel_id=1, source_target_pairs={{0,1},{1,0},{2,3},{3,2},{4,5},{5,4},{6,7},{7,6},{8,9},{9,8},{10,11... | collective-permute-start | bytes 1978376 | tf_op jit(solution)/shard_map/ppermute | solution.py:333
  0.5 0.9 %convert_element_type.45 = f32[2]{0:T(128)S(1)} convert(s32[2]{0:T(128)} %param.4) | non-fusion elementwise | flops 2 | bytes 16 | tf_op jit(solution)/shard_map/convert_element_type | solution.py:334
  1.3 0.1 broadcast_in_dim.2.lengths
  1.4 0.3 prepare.1.factor
  1.7 0.2 constant_dynamic-slice_fusion.legend
  2.0 0.4 %collective-permute-done.theirs = f32[1288,128]{1,0:T(8,128)S(1)} collective-permute-done((f32[1288,128]{1,0:T(8,128)}, f32[1288,128]{1,0:T(8,128)S(1)}, u32[]{:S(2)}, u32[]{:S(2)}) %collective-permute-start) | collective-permute-done | bytes 659488 | tf_op jit(solution)/shard_map/ppermute | solution.py:333
  2.4 2.6 %fourier_sums.3 = (f32[320,128]{1,0:T(8,128)S(1)}, f32[320,128]{1,0:T(8,128)S(1)}, f32[320,128]{1,0:T(8,128)S(1)}, f32[320,128]{1,0:T(8,128)S(1)}) custom-call(f32[2,2,24,896]{3,2,1,0:T(8,128)S(1)} %prepare.1.factor, f32[1288,128]{1,0:T(8,128)S(1)} %bitcast.4, f32[1288,128]{1,0:T(8,128)S(1)} %collective-permute-done.theirs), custom_call_target="tpu_custom_call" | custom-call | bytes 9000000 | tf_op jit(solution)/shard_map/fourier_sums/pallas_call | solution.py:195
  5.0 4.0 %collective-permute-start.9 = (f16[320,128]{1,0:T(8,128)(2,1)S(1)}, f16[320,128]{1,0:T(8,128)(2,1)S(1)}, u32[]{:S(2)}, u32[]{:S(2)}) collective-permute-start(f16[320,128]{1,0:T(8,128)(2,1)S(1)} %convert_element_type.57), channel_id=1, source_target_pairs={{0,4},{1,5},{2,6},{3,7},{4,0},{5,1},{6,2},{7,3},{8,12},{9,13},{10,... | collective-permute-start | bytes 245768 | tf_op jit(solution)/shard_map/ppermute | solution.py:322
  9.1 1.4 %collective-permute-start.8 = (f16[320,128]{1,0:T(8,128)(2,1)S(1)}, f16[320,128]{1,0:T(8,128)(2,1)S(1)}, u32[]{:S(2)}, u32[]{:S(2)}) collective-permute-start(f16[320,128]{1,0:T(8,128)(2,1)S(1)} %convert_element_type.55), channel_id=1, source_target_pairs={{0,6},{1,7},{2,4},{3,5},{4,2},{5,3},{6,0},{7,1},{8,14},{9,15},{10,... | collective-permute-start | bytes 245768 | tf_op jit(solution)/shard_map/ppermute | solution.py:322
  10.5 0.3 collective-permute-start.7
  10.8 2.6 %fourier_sums.2 = (f32[320,128]{1,0:T(8,128)S(1)}, f32[320,128]{1,0:T(8,128)S(1)}, f32[320,128]{1,0:T(8,128)S(1)}, f32[320,128]{1,0:T(8,128)S(1)}) custom-call(f32[2,2,24,896]{3,2,1,0:T(8,128)S(1)} %prepare.1.factor, f32[1288,128]{1,0:T(8,128)S(1)} %bitcast.5, f32[1288,128]{1,0:T(8,128)S(1)} %collective-permute-done.theirs), custom_call_target="tpu_custom_call" | custom-call | bytes 9000000 | tf_op jit(solution)/shard_map/fourier_sums/pallas_call | solution.py:195
  13.5 1.8 %collective-permute-start.3 = (f16[320,128]{1,0:T(8,128)(2,1)S(1)}, f16[320,128]{1,0:T(8,128)(2,1)S(1)}, u32[]{:S(2)}, u32[]{:S(2)}) collective-permute-start(f16[320,128]{1,0:T(8,128)(2,1)S(1)} %convert_element_type.48), channel_id=1, source_target_pairs={{0,2},{1,3},{2,0},{3,1},{4,6},{5,7},{6,4},{7,5},{8,10},{9,11},{10,... | collective-permute-start | bytes 245768 | tf_op jit(solution)/shard_map/ppermute | solution.py:322
  15.3 1.7 %collective-permute-start.2 = (f16[320,128]{1,0:T(8,128)(2,1)S(1)}, f16[320,128]{1,0:T(8,128)(2,1)S(1)}, u32[]{:S(2)}, u32[]{:S(2)}) collective-permute-start(f16[320,128]{1,0:T(8,128)(2,1)S(1)} %convert_element_type.47), channel_id=1, source_target_pairs={{0,4},{1,5},{2,6},{3,7},{4,0},{5,1},{6,2},{7,3},{8,12},{9,13},{10,... | collective-permute-start | bytes 245768 | tf_op jit(solution)/shard_map/ppermute | solution.py:322
  17.0 0.0 collective-permute-done.9
  17.0 2.0 %collective-permute-start.1 = (f16[320,128]{1,0:T(8,128)(2,1)S(1)}, f16[320,128]{1,0:T(8,128)(2,1)S(1)}, u32[]{:S(2)}, u32[]{:S(2)}) collective-permute-start(f16[320,128]{1,0:T(8,128)(2,1)S(1)} %convert_element_type.46), channel_id=1, source_target_pairs={{0,6},{1,7},{2,4},{3,5},{4,2},{5,3},{6,0},{7,1},{8,14},{9,15},{10,... | collective-permute-start | bytes 245768 | tf_op jit(solution)/shard_map/ppermute | solution.py:322
  19.0 0.0 collective-permute-done.8
  19.0 0.1 multiply_convert_fusion.refs_0_
  19.0 2.5 %collective-permute-start.12 = (bf16[320,128]{1,0:T(8,128)(2,1)S(1)}, bf16[320,128]{1,0:T(8,128)(2,1)S(1)}, u32[]{:S(2)}, u32[]{:S(2)}) collective-permute-start(bf16[320,128]{1,0:T(8,128)(2,1)S(1)} %multiply_convert_fusion.refs_0_), channel_id=1, source_target_pairs={{0,24},{8,16},{16,8},{24,0},{1,25},{9,17},{17,9},{25,1},{2,26},{10... | collective-permute-start | bytes 245768 | tf_op jit(solution)/shard_map/ppermute | solution.py:322
  21.6 0.5 %collective-permute-start.11 = (bf16[320,128]{1,0:T(8,128)(2,1)S(1)}, bf16[320,128]{1,0:T(8,128)(2,1)S(1)}, u32[]{:S(2)}, u32[]{:S(2)}) collective-permute-start(bf16[320,128]{1,0:T(8,128)(2,1)S(1)} %multiply_convert_fusion.refs_0_), channel_id=1, source_target_pairs={{0,16},{8,24},{16,0},{24,8},{1,17},{9,25},{17,1},{25,9},{2,18},{10... | collective-permute-start | bytes 245768 | tf_op jit(solution)/shard_map/ppermute | solution.py:322
  22.1 0.0 collective-permute-done.3
  22.1 0.5 %collective-permute-start.10 = (bf16[320,128]{1,0:T(8,128)(2,1)S(1)}, bf16[320,128]{1,0:T(8,128)(2,1)S(1)}, u32[]{:S(2)}, u32[]{:S(2)}) collective-permute-start(bf16[320,128]{1,0:T(8,128)(2,1)S(1)} %multiply_convert_fusion.refs_0_), channel_id=1, source_target_pairs={{0,8},{8,0},{16,24},{24,16},{1,9},{9,1},{17,25},{25,17},{2,10},{10... | collective-permute-start | bytes 245768 | tf_op jit(solution)/shard_map/ppermute | solution.py:322
  22.6 1.0 %spread_weights.1.weights = bf16[10,352,256]{2,1,0:T(8,128)(2,1)S(1)} custom-call(bf16[80,8,352]{2,1,0:T(8,128)(2,1)S(1)} %constant_dynamic-slice_fusion.legend), custom_call_target="tpu_custom_call" | custom-call | bytes 3000000 | tf_op jit(solution)/shard_map/spread_weights/pallas_call | solution.py:245
  23.6 0.3 collective-permute-done.2
  24.0 2.5 %collective-permute-start.6 = (bf16[320,128]{1,0:T(8,128)(2,1)S(1)}, bf16[320,128]{1,0:T(8,128)(2,1)S(1)}, u32[]{:S(2)}, u32[]{:S(2)}) collective-permute-start(bf16[320,128]{1,0:T(8,128)(2,1)S(1)} %multiply_convert_fusion.1.refs_0_), channel_id=1, source_target_pairs={{0,24},{8,16},{16,8},{24,0},{1,25},{9,17},{17,9},{25,1},{2,26},{10... | collective-permute-start | bytes 245768 | tf_op jit(solution)/shard_map/ppermute | solution.py:322
  26.5 0.5 %collective-permute-start.5 = (bf16[320,128]{1,0:T(8,128)(2,1)S(1)}, bf16[320,128]{1,0:T(8,128)(2,1)S(1)}, u32[]{:S(2)}, u32[]{:S(2)}) collective-permute-start(bf16[320,128]{1,0:T(8,128)(2,1)S(1)} %multiply_convert_fusion.1.refs_0_), channel_id=1, source_target_pairs={{0,16},{8,24},{16,0},{24,8},{1,17},{9,25},{17,1},{25,9},{2,18},{10... | collective-permute-start | bytes 245768 | tf_op jit(solution)/shard_map/ppermute | solution.py:322
  27.0 0.0 collective-permute-done.12.refs_3_
  27.0 0.5 %collective-permute-start.4 = (bf16[320,128]{1,0:T(8,128)(2,1)S(1)}, bf16[320,128]{1,0:T(8,128)(2,1)S(1)}, u32[]{:S(2)}, u32[]{:S(2)}) collective-permute-start(bf16[320,128]{1,0:T(8,128)(2,1)S(1)} %multiply_convert_fusion.1.refs_0_), channel_id=1, source_target_pairs={{0,8},{8,0},{16,24},{24,16},{1,9},{9,1},{17,25},{25,17},{2,10},{10... | collective-permute-start | bytes 245768 | tf_op jit(solution)/shard_map/ppermute | solution.py:322
  27.5 3.4 %spectra_part.2.refs_4_ = f32[80,352,128]{2,1,0:T(8,128)} custom-call(bf16[10,352,256]{2,1,0:T(8,128)(2,1)S(1)} %spread_weights.1.weights, bf16[320,128]{1,0:T(8,128)(2,1)S(1)} %multiply_convert_fusion.refs_0_, bf16[320,128]{1,0:T(8,128)(2,1)S(1)} %collective-permute-done.10.refs_1_, bf16[320,128]{1,0:T(8,128)(2,1)S(1)} %collective-permute-done.11.refs_2_, ...), custom_call_target="tpu_custom_call" | custom-call | bytes 9000000 | tf_op jit(solution)/shard_map/spectra_part/pallas_call | solution.py:304
  31.0 0.0 collective-permute-done.6.refs_3_
  31.0 0.0 collective-permute-done.5.refs_2_
  31.0 0.4 %collective-permute-done.4.refs_1_ = bf16[320,128]{1,0:T(8,128)(2,1)S(1)} collective-permute-done((bf16[320,128]{1,0:T(8,128)(2,1)S(1)}, bf16[320,128]{1,0:T(8,128)(2,1)S(1)}, u32[]{:S(2)}, u32[]{:S(2)}) %collective-permute-start.4) | collective-permute-done | bytes 81952 | tf_op jit(solution)/shard_map/ppermute | solution.py:322
  31.4 3.4 %spectra_part.3 = f32[80,352,128]{2,1,0:T(8,128)} custom-call(bf16[10,352,256]{2,1,0:T(8,128)(2,1)S(1)} %spread_weights.1.weights, bf16[320,128]{1,0:T(8,128)(2,1)S(1)} %multiply_convert_fusion.1.refs_0_, bf16[320,128]{1,0:T(8,128)(2,1)S(1)} %collective-permute-done.4.refs_1_, ...), custom_call_target="tpu_custom_call", output_to_operand_aliasing={{}: (5, {})} | custom-call | bytes 9000000 | tf_op jit(solution)/shard_map/spectra_part/pallas_call | solution.py:304
  (15 shorter events, 0.2 us)
Async XLA Ops:
  0.0 1.7 %copy-start = (bf16[80,8,1408]{2,1,0:T(8,128)(2,1)S(1)}, bf16[80,8,1408]{2,1,0:T(8,128)(2,1)}, u32[]{:S(2)}) copy-start(bf16[80,8,1408]{2,1,0:T(8,128)(2,1)} %param.5) | copy-start | bytes 5406724
  0.0 2.4 %copy-start.1 = (f32[2,644,128]{2,0,1:T(2,128)S(1)}, f32[2,644,128]{2,0,1:T(2,128)}, u32[]{:S(2)}) copy-start(f32[2,644,128]{2,0,1:T(2,128)} %param.3) | copy-start | bytes 1978372
  0.0 2.4 %collective-permute-start = (f32[1288,128]{1,0:T(8,128)}, f32[1288,128]{1,0:T(8,128)S(1)}, u32[]{:S(2)}, u32[]{:S(2)}) collective-permute-start(f32[1288,128]{1,0:T(8,128)} %bitcast.3), channel_id=1, source_target_pairs={{0,1},{1,0},{2,3},{3,2},{4,5},{5,4},{6,7},{7,6},{8,9},{9,8},{10,11... | collective-permute-start | bytes 1978376 | tf_op jit(solution)/shard_map/ppermute | solution.py:333
  5.0 11.9 %collective-permute-start.9 = (f16[320,128]{1,0:T(8,128)(2,1)S(1)}, f16[320,128]{1,0:T(8,128)(2,1)S(1)}, u32[]{:S(2)}, u32[]{:S(2)}) collective-permute-start(f16[320,128]{1,0:T(8,128)(2,1)S(1)} %convert_element_type.57), channel_id=1, source_target_pairs={{0,4},{1,5},{2,6},{3,7},{4,0},{5,1},{6,2},{7,3},{8,12},{9,13},{10,... | collective-permute-start | bytes 245768 | tf_op jit(solution)/shard_map/ppermute | solution.py:322
  9.1 9.9 %collective-permute-start.8 = (f16[320,128]{1,0:T(8,128)(2,1)S(1)}, f16[320,128]{1,0:T(8,128)(2,1)S(1)}, u32[]{:S(2)}, u32[]{:S(2)}) collective-permute-start(f16[320,128]{1,0:T(8,128)(2,1)S(1)} %convert_element_type.55), channel_id=1, source_target_pairs={{0,6},{1,7},{2,4},{3,5},{4,2},{5,3},{6,0},{7,1},{8,14},{9,15},{10,... | collective-permute-start | bytes 245768 | tf_op jit(solution)/shard_map/ppermute | solution.py:322
  10.5 8.5 %collective-permute-start.7 = (f16[320,128]{1,0:T(8,128)(2,1)S(1)}, f16[320,128]{1,0:T(8,128)(2,1)S(1)}, u32[]{:S(2)}, u32[]{:S(2)}) collective-permute-start(f16[320,128]{1,0:T(8,128)(2,1)S(1)} %convert_element_type.53), channel_id=1, source_target_pairs={{0,2},{1,3},{2,0},{3,1},{4,6},{5,7},{6,4},{7,5},{8,10},{9,11},{10,... | collective-permute-start | bytes 245768 | tf_op jit(solution)/shard_map/ppermute | solution.py:322
  13.5 8.6 %collective-permute-start.3 = (f16[320,128]{1,0:T(8,128)(2,1)S(1)}, f16[320,128]{1,0:T(8,128)(2,1)S(1)}, u32[]{:S(2)}, u32[]{:S(2)}) collective-permute-start(f16[320,128]{1,0:T(8,128)(2,1)S(1)} %convert_element_type.48), channel_id=1, source_target_pairs={{0,2},{1,3},{2,0},{3,1},{4,6},{5,7},{6,4},{7,5},{8,10},{9,11},{10,... | collective-permute-start | bytes 245768 | tf_op jit(solution)/shard_map/ppermute | solution.py:322
  15.3 8.7 %collective-permute-start.2 = (f16[320,128]{1,0:T(8,128)(2,1)S(1)}, f16[320,128]{1,0:T(8,128)(2,1)S(1)}, u32[]{:S(2)}, u32[]{:S(2)}) collective-permute-start(f16[320,128]{1,0:T(8,128)(2,1)S(1)} %convert_element_type.47), channel_id=1, source_target_pairs={{0,4},{1,5},{2,6},{3,7},{4,0},{5,1},{6,2},{7,3},{8,12},{9,13},{10,... | collective-permute-start | bytes 245768 | tf_op jit(solution)/shard_map/ppermute | solution.py:322
  17.0 7.0 %collective-permute-start.1 = (f16[320,128]{1,0:T(8,128)(2,1)S(1)}, f16[320,128]{1,0:T(8,128)(2,1)S(1)}, u32[]{:S(2)}, u32[]{:S(2)}) collective-permute-start(f16[320,128]{1,0:T(8,128)(2,1)S(1)} %convert_element_type.46), channel_id=1, source_target_pairs={{0,6},{1,7},{2,4},{3,5},{4,2},{5,3},{6,0},{7,1},{8,14},{9,15},{10,... | collective-permute-start | bytes 245768 | tf_op jit(solution)/shard_map/ppermute | solution.py:322
  19.0 7.9 %collective-permute-start.12 = (bf16[320,128]{1,0:T(8,128)(2,1)S(1)}, bf16[320,128]{1,0:T(8,128)(2,1)S(1)}, u32[]{:S(2)}, u32[]{:S(2)}) collective-permute-start(bf16[320,128]{1,0:T(8,128)(2,1)S(1)} %multiply_convert_fusion.refs_0_), channel_id=1, source_target_pairs={{0,24},{8,16},{16,8},{24,0},{1,25},{9,17},{17,9},{25,1},{2,26},{10... | collective-permute-start | bytes 245768 | tf_op jit(solution)/shard_map/ppermute | solution.py:322
  21.6 6.0 %collective-permute-start.11 = (bf16[320,128]{1,0:T(8,128)(2,1)S(1)}, bf16[320,128]{1,0:T(8,128)(2,1)S(1)}, u32[]{:S(2)}, u32[]{:S(2)}) collective-permute-start(bf16[320,128]{1,0:T(8,128)(2,1)S(1)} %multiply_convert_fusion.refs_0_), channel_id=1, source_target_pairs={{0,16},{8,24},{16,0},{24,8},{1,17},{9,25},{17,1},{25,9},{2,18},{10... | collective-permute-start | bytes 245768 | tf_op jit(solution)/shard_map/ppermute | solution.py:322
  22.1 5.5 %collective-permute-start.10 = (bf16[320,128]{1,0:T(8,128)(2,1)S(1)}, bf16[320,128]{1,0:T(8,128)(2,1)S(1)}, u32[]{:S(2)}, u32[]{:S(2)}) collective-permute-start(bf16[320,128]{1,0:T(8,128)(2,1)S(1)} %multiply_convert_fusion.refs_0_), channel_id=1, source_target_pairs={{0,8},{8,0},{16,24},{24,16},{1,9},{9,1},{17,25},{25,17},{2,10},{10... | collective-permute-start | bytes 245768 | tf_op jit(solution)/shard_map/ppermute | solution.py:322
  24.0 7.0 %collective-permute-start.6 = (bf16[320,128]{1,0:T(8,128)(2,1)S(1)}, bf16[320,128]{1,0:T(8,128)(2,1)S(1)}, u32[]{:S(2)}, u32[]{:S(2)}) collective-permute-start(bf16[320,128]{1,0:T(8,128)(2,1)S(1)} %multiply_convert_fusion.1.refs_0_), channel_id=1, source_target_pairs={{0,24},{8,16},{16,8},{24,0},{1,25},{9,17},{17,9},{25,1},{2,26},{10... | collective-permute-start | bytes 245768 | tf_op jit(solution)/shard_map/ppermute | solution.py:322
  26.5 4.5 %collective-permute-start.5 = (bf16[320,128]{1,0:T(8,128)(2,1)S(1)}, bf16[320,128]{1,0:T(8,128)(2,1)S(1)}, u32[]{:S(2)}, u32[]{:S(2)}) collective-permute-start(bf16[320,128]{1,0:T(8,128)(2,1)S(1)} %multiply_convert_fusion.1.refs_0_), channel_id=1, source_target_pairs={{0,16},{8,24},{16,0},{24,8},{1,17},{9,25},{17,1},{25,9},{2,18},{10... | collective-permute-start | bytes 245768 | tf_op jit(solution)/shard_map/ppermute | solution.py:322
  27.0 4.4 %collective-permute-start.4 = (bf16[320,128]{1,0:T(8,128)(2,1)S(1)}, bf16[320,128]{1,0:T(8,128)(2,1)S(1)}, u32[]{:S(2)}, u32[]{:S(2)}) collective-permute-start(bf16[320,128]{1,0:T(8,128)(2,1)S(1)} %multiply_convert_fusion.1.refs_0_), channel_id=1, source_target_pairs={{0,8},{8,0},{16,24},{24,16},{1,9},{9,1},{17,25},{25,17},{2,10},{10... | collective-permute-start | bytes 245768 | tf_op jit(solution)/shard_map/ppermute | solution.py:322
